TPU v7x, 32 devices: a whole 2x2x4 slice. The times are simulated.
32 devices in a mesh: leaf: 32 (over z, y, x, core).
Axes of the slice: x: 2, y: 2, z: 4, core: 2. Of those that a mesh axis runs over, the one named last changes fastest.
Arguments:
- rhs: float32 [32768, 128], P('leaf'), may hold values from -6 to 6
- proj_bases: float32 [5, 32768, 256], P(None, 'leaf'), may hold values from -6 to 6
- corr_bases: float32 [5, 32768, 256], P(None, 'leaf'), may hold values from -0.375 to 0.375
- cores: float32 [5, 8192, 512], P(None, 'leaf'), may hold values from -0.25 to 0.25
Outputs:
- solution: float32 [32768, 128], P('leaf')
All inputs are finite; a program needn't handle non-finite values.
Results may differ from a plain program's by a relative error of at most 0.00017.
Values sent between devices are 32-bit elements; how exact they have to be, the bound alone decides.
No kernel may reach another device: no remote copies, remote signals or barrier semaphores. Data moves between devices by JAX's collectives and lax.ppermute only.
A program may use at most 64 MiB of HBM per device.

v0:
```python
import jax
import jax.numpy as jnp
from jax import lax
from jax.experimental import pallas as pl
from jax.experimental.pallas import tpu as pltpu
from jax.sharding import PartitionSpec as P

LEVELS = 5
HIGH = lax.Precision.HIGH
MIB = 2**20
IN_HBM = pl.BlockSpec(memory_space=pltpu.HBM)
IN_VMEM = pl.BlockSpec(memory_space=pltpu.VMEM)


def exchange(value, mask):
    pairs = [(source, source ^ mask) for source in range(lax.axis_size("leaf"))]
    return lax.ppermute(value, "leaf", pairs)


def tie(value, after):
    return lax.optimization_barrier((value, after))[0]


def pair_up(low, mine, other, axis):
    return jnp.where(
        low,
        jnp.concatenate([mine, other], axis),
        jnp.concatenate([other, mine], axis),
    )


def project(basis, state):
    return jnp.einsum("kn,nr->kr", state, basis, precision=HIGH)


def times_transposed(left, right):
    return jnp.einsum("kb,ab->ka", left, right, precision=HIGH)


def parts(value):
    high = value.astype(jnp.bfloat16)
    return high, (value - high.astype(jnp.float32)).astype(jnp.bfloat16)


def three_passes(left, right, dim):
    rows = left.shape[0]
    left_high, left_low = parts(left)
    right_high, right_low = parts(right)

    def one(a, b):
        return lax.dot_general(a, b, (((1,), (dim,)), ((), ())), preferred_element_type=jnp.float32)

    both = one(jnp.concatenate([left_high, left_low], 0), right_high)
    return both[:rows] + (both[rows:] + one(left_high, right_low))


def begin(rhs, proj_bases, corr_bases, cores, first, leaf_core, groups):
    rows, width = rhs.shape
    rank = proj_bases.shape[2]
    shapes = [(width, rank), (width, rows)] + [(rows, rank)] * 4
    shapes += [(rank, 2 * rank)] if leaf_core else []
    shapes += [(sum(n for _, n in group), 2 * rank) for group in groups]

    def body(x_hbm, p_hbm, w_hbm, c_hbm, *refs):
        outs, (x_ref, p_ref, sems) = list(refs[: len(shapes)]), refs[len(shapes) :]
        q_out, state_out, w_out, p_out, w_next, p_next = outs[:6]
        rest = outs[6:]
        moves = [(x_hbm, x_ref), (p_hbm.at[first], p_ref)]
        if leaf_core:
            moves.append((c_hbm.at[first], rest.pop(0)))
        moves += [(w_hbm.at[first], w_out), (p_hbm.at[first - 1], p_out)]
        for group, out in zip(groups, rest):
            start = 0
            for level, n in group:
                moves.append((c_hbm.at[level, 0:n], out.at[start : start + n]))
                start += n
        moves += [(w_hbm.at[first - 1], w_next), (p_hbm.at[first - 2], p_next)]
        copies = [pltpu.make_async_copy(a, b, sems.at[at]) for at, (a, b) in enumerate(moves)]
        for copy in copies:
            copy.start()
        copies[0].wait()
        state = x_ref[...].T
        state_out[...] = state
        copies[1].wait()
        q_out[...] = three_passes(state, p_ref[...], 0)
        for copy in copies[2:]:
            copy.wait()

    count = 6 + (1 if leaf_core else 0) + sum(len(group) for group in groups)
    return pl.pallas_call(
        body,
        in_specs=[IN_HBM] * 4,
        out_specs=[IN_VMEM] * len(shapes),
        out_shape=[pltpu.VMEM(shape, jnp.float32) for shape in shapes],
        scratch_shapes=[
            pltpu.VMEM((rows, width), jnp.float32),
            pltpu.VMEM((rows, rank), jnp.float32),
            pltpu.SemaphoreType.DMA((count,)),
        ],
        compiler_params=pltpu.CompilerParams(vmem_limit_bytes=49 * MIB),
        cost_estimate=pl.CostEstimate(
            flops=6 * rows * width * rank, bytes_accessed=2**22, transcendentals=0
        ),
        name="begin",
    )(rhs, proj_bases, corr_bases, cores)


def fetch(proj_bases, corr_bases, projs, corrs, after):
    rows, rank = corr_bases.shape[1:]
    count = len(projs) + len(corrs)

    def body(p_hbm, w_hbm, _, *refs):
        sources = [p_hbm.at[level] for level in projs] + [w_hbm.at[level] for level in corrs]
        sems = refs[-1]
        copies = [
            pltpu.make_async_copy(source, out, sems.at[at])
            for at, (source, out) in enumerate(zip(sources, refs[:-1]))
        ]
        for copy in copies:
            copy.start()
        for copy in copies:
            copy.wait()

    return pl.pallas_call(
        body,
        in_specs=[IN_HBM, IN_HBM, pl.BlockSpec(memory_space=pl.ANY)],
        out_specs=[IN_VMEM] * count,
        out_shape=[pltpu.VMEM((rows, rank), jnp.float32)] * count,
        scratch_shapes=[pltpu.SemaphoreType.DMA((count,))],
        compiler_params=pltpu.CompilerParams(vmem_limit_bytes=45 * MIB),
        cost_estimate=pl.CostEstimate(
            flops=0, bytes_accessed=8 * count * rows * rank, transcendentals=0
        ),
        name="fetch",
    )(proj_bases, corr_bases, after)


def finish(state, corr, held):
    width, rows = state.shape

    def body(x_ref, w_ref, t_ref, out_ref):
        out_ref[...] = (x_ref[...] - three_passes(t_ref[...], w_ref[...], 1)).T

    return pl.pallas_call(
        body,
        in_specs=[IN_VMEM] * 3,
        out_specs=IN_VMEM,
        out_shape=jax.ShapeDtypeStruct((rows, width), jnp.float32),
        compiler_params=pltpu.CompilerParams(vmem_limit_bytes=16 * MIB),
        cost_estimate=pl.CostEstimate(
            flops=6 * rows * width * corr.shape[1], bytes_accessed=2**21, transcendentals=0
        ),
        name="finish",
    )(state, corr, held)


def on_device(rhs, proj_bases, corr_bases, cores):
    count = lax.axis_size("leaf")
    me = lax.axis_index("leaf")
    rows_here, width = rhs.shape
    rank = proj_bases.shape[2]
    bits = [(count >> level).bit_length() - 2 for level in range(LEVELS)]
    first = LEVELS - 1
    chain = [level for level in reversed(range(LEVELS)) if bits[level] > 0]

    parity = me & 1
    for bit in range(1, count.bit_length() - 1):
        parity = parity ^ ((me >> bit) & 1)
    lows = [(me >> bit) & 1 == 0 for bit in range(count.bit_length() - 1)]
    rhs, upper, *lows = lax.optimization_barrier((rhs, parity == 0, *lows))

    def low(bit):
        return lows[bit]

    def across(value, bit):
        return exchange(value, (1 << bit) | (1 if bit > 0 else 0))

    def chip_sum(value):
        half = width // 2
        keep = jnp.where(upper, value[:half], value[half:])
        send = jnp.where(upper, value[half:], value[:half])
        return keep + exchange(send, 1)

    def chip_gather(value):
        return pair_up(upper, value, exchange(value, 1), 0)

    heads = [(level, rank >> bits[level]) for level in chain if bits[level] == 1]
    tails = [(level, rank >> bits[level]) for level in chain if bits[level] > 1]
    groups = [group for group in (heads, tails) if group]
    leaf_core = bits[first] == 0
    value, state, top_corr, next_proj, corr, proj, *fetched = begin(
        rhs, proj_bases, corr_bases, cores, first, leaf_core, groups
    )

    table = {}
    if leaf_core:
        table[first] = fetched.pop(0)

    def finish_table(level, mine):
        part = exchange(mine, 1)
        both = jnp.where(low(0), jnp.stack([mine, part], 1), jnp.stack([part, mine], 1))
        table[level] = both.reshape(rank, 2 * rank)

    def gather_steps():
        block = fetched[-1][None]
        waiting = [level for level, _ in tails]
        bit = 1
        coming = exchange(block, 2)
        while True:
            after = yield
            block = pair_up(low(bit), block, tie(coming, after), 0)
            bit += 1
            after = yield
            rows = rank >> bit
            for level in [level for level in waiting if bits[level] == bit]:
                finish_table(level, tie(block[:, :rows], after))
                block = block[:, rows:]
            waiting = [level for level in waiting if bits[level] > bit]
            if waiting:
                coming = exchange(tie(block, after), 1 << bit)
            else:
                return

    steps = gather_steps()
    next(steps)

    def step(after):
        try:
            steps.send(after)
        except StopIteration:
            pass

    def solve(level, value, ahead_of):
        top = bits[level]
        for bit in range(1, top):
            value = ahead_of.get(bit, lambda v: v)(value)
            value = value + across(value, bit)
        while level not in table:
            step(value)
        if level == 1:
            step(value)
            step(value)
        value = ahead_of.get(top, lambda v: v)(value)
        stacked = pair_up(low(top), value, across(value, top), 1)
        stacked = stacked / jnp.sqrt(jnp.float32(rows_here << top))
        return times_transposed(stacked, table[level])

    def update(corr, state, held):
        return state - jnp.einsum("ka,na->kn", held, corr, precision=HIGH)

    if leaf_core:
        top = pair_up(low(0), value, exchange(value, 1), 1)
        top = top / jnp.sqrt(jnp.float32(rows_here))
        held = times_transposed(top, table[first])
    else:
        held = chip_gather(solve(first, chip_sum(value), {}))
    state = update(top_corr, state, held)
    value = chip_sum(project(next_proj, state))
    if heads:
        finish_table(heads[0][0], tie(fetched[0], value)[None])
    for level in reversed(range(1, first)):
        start = value
        if heads and level < first - 1:
            step(start)
            step(start)
        held = solve(level, value, {})
        if level == first - 2:
            later = fetch(
                proj_bases,
                corr_bases,
                list(reversed(range(level))),
                list(reversed(range(level + 1))),
                start,
            )
            projs, corrs = list(later[:level]), list(later[level:])
        if level < first - 1:
            proj, corr = projs.pop(0), corrs.pop(0)
        proj, corr = tie(proj, start), tie(corr, start)
        ahead = chip_sum(project(proj, state))
        own = jnp.einsum("na,nb->ab", proj, corr, precision=HIGH)
        value = ahead - times_transposed(held, own + exchange(own, 1))
        if level > 1:
            state = update(corr, state, chip_gather(held))
    state = update(corr, state, chip_gather(held))
    ahead_of = {bits[0]: lambda v: tie(v, state)}
    held = solve(0, value, ahead_of)
    return finish(state, corrs[0], chip_gather(held))


def solution(mesh):
    return jax.shard_map(
        on_device,
        mesh=mesh,
        in_specs=(
            P("leaf", None),
            P(None, "leaf", None),
            P(None, "leaf", None),
            P(None, "leaf", None),
        ),
        out_specs=P("leaf", None),
        check_vma=False,
    )
```

profile of v0, /device:TPU:0, one launch (start us, length us, event | category | flops | bytes accessed | tf_op | source)
XLA Modules:
  0.0 64.8 jit_solution(3149648576451105927)
XLA Ops:
  0.0 3.0 %begin.1 = (f32[128,256]{1,0:T(8,128)S(1)}, f32[128,1024]{1,0:T(8,128)S(1)}, f32[1024,256]{1,0:T(8,128)S(1)}, f32[1024,256]{1,0:T(8,128)S(1)}, f32[1024,256]{1,0...) custom-call(f32[1024,128]{1,0:T(8,128)} %x_hbm, ...), custom_call_target="tpu_custom_call" | custom-call | flops 201326592 | bytes 4194304 | tf_op jit(solution)/shard_map/begin/pallas_call | solution.py:90
  3.1 0.5 collective-permute-start
  3.6 1.0 %collective-permute-done = f32[128,256]{1,0:T(8,128)S(1)} collective-permute-done((f32[128,256]{1,0:T(8,128)S(1)}, f32[128,256]{1,0:T(8,128)S(1)}, u32[]{:S(2)}, u32[]{:S(2)}) %collective-permute-start) | collective-permute-done | bytes 131104 | tf_op jit(solution)/shard_map/ppermute | solution.py:17
  4.6 0.4 fusion.1
  5.0 0.7 %convolution_subtract_fusion.3 = f32[128,1024]{1,0:T(8,128)S(1)} fusion(f32[128,1024]{1,0:T(8,128)S(1)} %get-tuple-element.43, f32[128,256]{1,0:T(8,128)S(1)} %fusion.1, f32[1024,256]{1,0:T(8,128)S(1)} %get-tuple-element.47), kind=kOutput, calls=%fused_computation.3 | convolution fusion | flops 201457664 | bytes 2228224 | tf_op jit(solution)/shard_map/ka,na->kn/dot_general | solution.py:249
  5.6 0.4 fusion.87
  6.1 0.4 collective-permute-start.1
  6.5 2.6 %collective-permute-start.9 = (f32[1,112,512]{2,1,0:T(8,128)S(1)}, f32[1,112,512]{2,1,0:T(8,128)S(1)}, u32[]{:S(2)}, u32[]{:S(2)}) collective-permute-start(f32[1,112,512]{2,1,0:T(8,128)S(1)} %bitcast.43), channel_id=1, source_target_pairs={{0,2},{1,3},{2,0},{3,1},{4,6},{5,7},{6,4},{7,5},{8,10},{9,11},{10,... | collective-permute-start | bytes 688136 | tf_op jit(solution)/shard_map/ppermute | solution.py:17
  9.1 0.0 collective-permute-done.1
  9.2 0.9 %collective-permute-start.2 = (f32[64,256]{1,0:T(8,128)S(1)}, f32[64,256]{1,0:T(8,128)S(1)}, u32[]{:S(2)}, u32[]{:S(2)}) collective-permute-start(f32[64,256]{1,0:T(8,128)S(1)} %select_add_fusion), channel_id=1, source_target_pairs={{0,3},{1,2},{2,1},{3,0},{4,7},{5,6},{6,5},{7,4},{8,11},{9,10},{10,... | collective-permute-start | bytes 196616 | tf_op jit(solution)/shard_map/ppermute | solution.py:17
  10.1 0.4 fusion.88
  10.5 0.4 collective-permute-start.5
  10.9 0.2 collective-permute-start.3
  11.1 1.0 %fusion.89 = f32[256,256]{1,0:T(8,128)S(1)} fusion(f32[1024,256]{1,0:T(8,128)S(1)} %get-tuple-element.57, f32[1024,256]{1,0:T(8,128)S(1)} %get-tuple-element.54), kind=kOutput, calls=%fused_computation.112 | convolution fusion | flops 402653184 | bytes 2359296 | tf_op jit(solution)/shard_map/na,nb->ab/dot_general | solution.py:280
  12.1 0.4 collective-permute-start.6
  12.5 0.0 collective-permute-done.3
  12.5 3.8 %collective-permute-done.2 = f32[64,256]{1,0:T(8,128)S(1)} collective-permute-done((f32[64,256]{1,0:T(8,128)S(1)}, f32[64,256]{1,0:T(8,128)S(1)}, u32[]{:S(2)}, u32[]{:S(2)}) %collective-permute-start.2) | collective-permute-done | bytes 65568 | tf_op jit(solution)/shard_map/ppermute | solution.py:17
  16.3 0.4 fusion.15
  16.7 0.2 collective-permute-start.4
  16.9 0.3 add_subtract_fusion.2._
  17.2 1.5 %collective-permute-start.7 = (f32[64,256]{1,0:T(8,128)S(1)}, f32[64,256]{1,0:T(8,128)S(1)}, u32[]{:S(2)}, u32[]{:S(2)}) collective-permute-start(f32[64,256]{1,0:T(8,128)S(1)} %add_subtract_fusion.2._), channel_id=1, source_target_pairs={{0,3},{1,2},{2,1},{3,0},{4,7},{5,6},{6,5},{7,4},{8,11},{9,10},{10,... | collective-permute-start | bytes 196616 | tf_op jit(solution)/shard_map/ppermute | solution.py:17
  18.8 2.5 %fetch.1 = (f32[1024,256]{1,0:T(8,128)S(1)}, f32[1024,256]{1,0:T(8,128)S(1)}, f32[1024,256]{1,0:T(8,128)S(1)}, f32[1024,256]{1,0:T(8,128)S(1)}, f32[1024,256]{1,0:T(8,128)S(1)}) custom-call(f32[5,1024,256]{2,1,0:T(8,128)} %p_hbm.3, f32[5,1024,256]{2,1,0:T(8,128)} %w_hbm.3, f32[64,256]{1,0:T(8,128)S(1)} %add_subtract_fusion.2._), custom_call_target="tpu_custom_call" | custom-call | bytes 10485760 | tf_op jit(solution)/shard_map/fetch/pallas_call | solution.py:124
  21.4 1.6 %collective-permute-start.17 = (f32[2,48,512]{2,1,0:T(8,128)S(1)}, f32[2,48,512]{2,1,0:T(8,128)S(1)}, u32[]{:S(2)}, u32[]{:S(2)}) collective-permute-start(f32[2,48,512]{2,1,0:T(8,128)S(1)} %slice.63), channel_id=1, source_target_pairs={{0,4},{1,5},{2,6},{3,7},{4,0},{5,1},{6,2},{7,3},{8,12},{9,13},{10,... | collective-permute-start | bytes 589832 | tf_op jit(solution)/shard_map/ppermute | solution.py:17
  23.0 0.1 collective-permute-start.10
  23.1 1.0 %fusion.91 = f32[256,256]{1,0:T(8,128)S(1)} fusion(f32[1024,256]{1,0:T(8,128)S(1)} %get-tuple-element.65, f32[1024,256]{1,0:T(8,128)S(1)} %get-tuple-element.62), kind=kOutput, calls=%fused_computation.114 | convolution fusion | flops 402653184 | bytes 2359296 | tf_op jit(solution)/shard_map/na,nb->ab/dot_general | solution.py:280
  24.1 0.5 collective-permute-start.13
  24.6 0.3 collective-permute-start.8
  24.8 0.7 %convolution_subtract_fusion.2 = f32[128,1024]{1,0:T(8,128)S(1)} fusion(f32[128,1024]{1,0:T(8,128)S(1)} %convolution_subtract_fusion.3, f32[1024,256]{1,0:T(8,128)S(1)} %get-tuple-element.54, f32[64,256]{1,0:T(8,128)S(1)} %collective-permute-done.4, f32[64,256]{1,0:T(8,128)S(1)} %fusion.15, pred[]{:T(512)S(6)} %eq.18), kind=kOutput, calls=%fused_computation.2 | convolution fusion | flops 201555968 | bytes 2228225 | tf_op jit(solution)/shard_map/ka,na->kn/dot_general | solution.py:249
  25.5 0.4 fusion.90
  25.9 0.5 collective-permute-start.12
  26.5 3.0 %collective-permute-done.8 = f32[64,256]{1,0:T(8,128)S(1)} collective-permute-done((f32[64,256]{1,0:T(8,128)S(1)}, f32[64,256]{1,0:T(8,128)S(1)}, u32[]{:S(2)}, u32[]{:S(2)}) %collective-permute-start.8) | collective-permute-done | bytes 65568 | tf_op jit(solution)/shard_map/ppermute | solution.py:17
  29.5 0.4 fusion.28
  29.9 0.4 collective-permute-start.11
  30.3 0.3 add_subtract_fusion.1
  30.6 0.1 collective-permute-start.14
  30.8 1.9 %collective-permute-start.26 = (f32[4,16,512]{2,1,0:T(8,128)S(1)}, f32[4,16,512]{2,1,0:T(8,128)S(1)}, u32[]{:S(2)}, u32[]{:S(2)}) collective-permute-start(f32[4,16,512]{2,1,0:T(8,128)S(1)} %slice.67), channel_id=1, source_target_pairs={{0,8},{1,9},{2,10},{3,11},{4,12},{5,13},{6,14},{7,15},{8,0},{9,1},... | collective-permute-start | bytes 393224 | tf_op jit(solution)/shard_map/ppermute | solution.py:17
  32.7 1.0 %fusion.93 = f32[256,256]{1,0:T(8,128)S(1)} fusion(f32[1024,256]{1,0:T(8,128)S(1)} %get-tuple-element.74, f32[1024,256]{1,0:T(8,128)S(1)} %get-tuple-element.70), kind=kOutput, calls=%fused_computation.116 | convolution fusion | flops 402653184 | bytes 2359296 | tf_op jit(solution)/shard_map/na,nb->ab/dot_general | solution.py:280
  33.7 0.1 collective-permute-start.21
  33.8 0.4 collective-permute-start.18
  34.3 0.5 collective-permute-done.14
  34.7 1.6 %collective-permute-start.15 = (f32[64,256]{1,0:T(8,128)S(1)}, f32[64,256]{1,0:T(8,128)S(1)}, u32[]{:S(2)}, u32[]{:S(2)}) collective-permute-start(f32[64,256]{1,0:T(8,128)S(1)} %add.45), channel_id=1, source_target_pairs={{0,5},{1,4},{2,7},{3,6},{4,1},{5,0},{6,3},{7,2},{8,13},{9,12},{10,... | collective-permute-start | bytes 196616 | tf_op jit(solution)/shard_map/ppermute | solution.py:17
  36.4 0.7 %convolution_subtract_fusion.1 = f32[128,1024]{1,0:T(8,128)S(1)} fusion(f32[128,1024]{1,0:T(8,128)S(1)} %convolution_subtract_fusion.2, f32[1024,256]{1,0:T(8,128)S(1)} %get-tuple-element.62, f32[64,256]{1,0:T(8,128)S(1)} %collective-permute-done.11, f32[64,256]{1,0:T(8,128)S(1)} %fusion.28, pred[]{:T(512)S(6)} %eq.18), kind=kOutput, calls=%fused_computation.1 | convolution fusion | flops 201555968 | bytes 2228225 | tf_op jit(solution)/shard_map/ka,na->kn/dot_general | solution.py:249
  37.1 0.4 fusion.92
  37.5 0.1 collective-permute-start.20
  37.6 1.0 %collective-permute-done.15 = f32[64,256]{1,0:T(8,128)S(1)} collective-permute-done((f32[64,256]{1,0:T(8,128)S(1)}, f32[64,256]{1,0:T(8,128)S(1)}, u32[]{:S(2)}, u32[]{:S(2)}) %collective-permute-start.15) | collective-permute-done | bytes 65568 | tf_op jit(solution)/shard_map/ppermute | solution.py:17
  38.6 1.7 %collective-permute-start.16 = (f32[64,256]{1,0:T(8,128)S(1)}, f32[64,256]{1,0:T(8,128)S(1)}, u32[]{:S(2)}, u32[]{:S(2)}) collective-permute-start(f32[64,256]{1,0:T(8,128)S(1)} %add.46), channel_id=1, source_target_pairs={{0,9},{1,8},{2,11},{3,10},{4,13},{5,12},{6,15},{7,14},{8,1},{9,0},... | collective-permute-start | bytes 196616 | tf_op jit(solution)/shard_map/ppermute | solution.py:17
  40.4 2.1 %collective-permute-done.16 = f32[64,256]{1,0:T(8,128)S(1)} collective-permute-done((f32[64,256]{1,0:T(8,128)S(1)}, f32[64,256]{1,0:T(8,128)S(1)}, u32[]{:S(2)}, u32[]{:S(2)}) %collective-permute-start.16) | collective-permute-done | bytes 65568 | tf_op jit(solution)/shard_map/ppermute | solution.py:17
  42.5 0.4 fusion.41
  42.9 0.3 add_subtract_fusion
  43.2 1.4 %collective-permute-start.22 = (f32[64,256]{1,0:T(8,128)S(1)}, f32[64,256]{1,0:T(8,128)S(1)}, u32[]{:S(2)}, u32[]{:S(2)}) collective-permute-start(f32[64,256]{1,0:T(8,128)S(1)} %add_subtract_fusion), channel_id=1, source_target_pairs={{0,3},{1,2},{2,1},{3,0},{4,7},{5,6},{6,5},{7,4},{8,11},{9,10},{10,... | collective-permute-start | bytes 196616 | tf_op jit(solution)/shard_map/ppermute | solution.py:17
  44.6 0.4 collective-permute-start.19
  45.0 2.2 %collective-permute-done.22 = f32[64,256]{1,0:T(8,128)S(1)} collective-permute-done((f32[64,256]{1,0:T(8,128)S(1)}, f32[64,256]{1,0:T(8,128)S(1)}, u32[]{:S(2)}, u32[]{:S(2)}) %collective-permute-start.22) | collective-permute-done | bytes 65568 | tf_op jit(solution)/shard_map/ppermute | solution.py:17
  47.2 1.5 %collective-permute-start.23 = (f32[64,256]{1,0:T(8,128)S(1)}, f32[64,256]{1,0:T(8,128)S(1)}, u32[]{:S(2)}, u32[]{:S(2)}) collective-permute-start(f32[64,256]{1,0:T(8,128)S(1)} %add.49), channel_id=1, source_target_pairs={{0,5},{1,4},{2,7},{3,6},{4,1},{5,0},{6,3},{7,2},{8,13},{9,12},{10,... | collective-permute-start | bytes 196616 | tf_op jit(solution)/shard_map/ppermute | solution.py:17
  48.8 0.3 collective-permute-start.27
  49.0 2.3 %collective-permute-done.23 = f32[64,256]{1,0:T(8,128)S(1)} collective-permute-done((f32[64,256]{1,0:T(8,128)S(1)}, f32[64,256]{1,0:T(8,128)S(1)}, u32[]{:S(2)}, u32[]{:S(2)}) %collective-permute-start.23) | collective-permute-done | bytes 65568 | tf_op jit(solution)/shard_map/ppermute | solution.py:17
  51.3 1.5 %collective-permute-start.24 = (f32[64,256]{1,0:T(8,128)S(1)}, f32[64,256]{1,0:T(8,128)S(1)}, u32[]{:S(2)}, u32[]{:S(2)}) collective-permute-start(f32[64,256]{1,0:T(8,128)S(1)} %add.50), channel_id=1, source_target_pairs={{0,9},{1,8},{2,11},{3,10},{4,13},{5,12},{6,15},{7,14},{8,1},{9,0},... | collective-permute-start | bytes 196616 | tf_op jit(solution)/shard_map/ppermute | solution.py:17
  52.8 0.7 %convolution_subtract_fusion.x_ref = f32[128,1024]{1,0:T(8,128)S(1)} fusion(f32[128,1024]{1,0:T(8,128)S(1)} %convolution_subtract_fusion.1, f32[1024,256]{1,0:T(8,128)S(1)} %get-tuple-element.70, f32[64,256]{1,0:T(8,128)S(1)} %collective-permute-done.19, f32[64,256]{1,0:T(8,128)S(1)} %fusion.41, pred[]{:T(512)S(6)} %eq.18), kind=kOutput, calls=%fused_computation | convolution fusion | flops 201555968 | bytes 2228225 | tf_op jit(solution)/shard_map/ka,na->kn/dot_general | solution.py:249
  53.4 2.0 %collective-permute-done.24 = f32[64,256]{1,0:T(8,128)S(1)} collective-permute-done((f32[64,256]{1,0:T(8,128)S(1)}, f32[64,256]{1,0:T(8,128)S(1)}, u32[]{:S(2)}, u32[]{:S(2)}) %collective-permute-start.24) | collective-permute-done | bytes 65568 | tf_op jit(solution)/shard_map/ppermute | solution.py:17
  55.5 2.4 %collective-permute-start.25 = (f32[64,256]{1,0:T(8,128)S(1)}, f32[64,256]{1,0:T(8,128)S(1)}, u32[]{:S(2)}, u32[]{:S(2)}) collective-permute-start(f32[64,256]{1,0:T(8,128)S(1)} %add.51), channel_id=1, source_target_pairs={{0,17},{1,16},{2,19},{3,18},{4,21},{5,20},{6,23},{7,22},{8,25},{9,... | collective-permute-start | bytes 196616 | tf_op jit(solution)/shard_map/ppermute | solution.py:17
  58.0 2.5 %collective-permute-done.25 = f32[64,256]{1,0:T(8,128)S(1)} collective-permute-done((f32[64,256]{1,0:T(8,128)S(1)}, f32[64,256]{1,0:T(8,128)S(1)}, u32[]{:S(2)}, u32[]{:S(2)}) %collective-permute-start.25) | collective-permute-done | bytes 65568 | tf_op jit(solution)/shard_map/ppermute | solution.py:17
  60.5 0.4 fusion.54
  60.9 1.6 %collective-permute-start.28 = (f32[64,256]{1,0:T(8,128)S(1)}, f32[64,256]{1,0:T(8,128)S(1)}, u32[]{:S(2)}, u32[]{:S(2)}) collective-permute-start(f32[64,256]{1,0:T(8,128)S(1)} %fusion.54), channel_id=1, source_target_pairs={{0,1},{1,0},{2,3},{3,2},{4,5},{5,4},{6,7},{7,6},{8,9},{9,8},{10,11... | collective-permute-start | bytes 196616 | tf_op jit(solution)/shard_map/ppermute | solution.py:17
  62.5 0.9 %collective-permute-done.28 = f32[64,256]{1,0:T(8,128)S(1)} collective-permute-done((f32[64,256]{1,0:T(8,128)S(1)}, f32[64,256]{1,0:T(8,128)S(1)}, u32[]{:S(2)}, u32[]{:S(2)}) %collective-permute-start.28) | collective-permute-done | bytes 65568 | tf_op jit(solution)/shard_map/ppermute | solution.py:17
  63.4 1.4 %finish.1 = f32[1024,128]{1,0:T(8,128)} custom-call(f32[128,1024]{1,0:T(8,128)S(1)} %convolution_subtract_fusion.x_ref, f32[1024,256]{1,0:T(8,128)S(1)} %get-tuple-element.71.w_ref, f32[128,256]{1,0:T(8,128)S(1)} %maximum_select_fusion.18.t_ref), custom_call_target="tpu_custom_call" | custom-call | flops 201326592 | bytes 2097152 | tf_op jit(solution)/shard_map/finish/pallas_call | solution.py:144
  (42 shorter events, 0.6 us)
Async XLA Ops:
  3.1 1.5 %collective-permute-start = (f32[128,256]{1,0:T(8,128)S(1)}, f32[128,256]{1,0:T(8,128)S(1)}, u32[]{:S(2)}, u32[]{:S(2)}) collective-permute-start(f32[128,256]{1,0:T(8,128)S(1)} %get-tuple-element.45), channel_id=1, source_target_pairs={{0,1},{1,0},{2,3},{3,2},{4,5},{5,4},{6,7},{7,6},{8,9},{9,8},{10,11... | collective-permute-start | bytes 393224 | tf_op jit(solution)/shard_map/ppermute | solution.py:17
  6.1 3.1 %collective-permute-start.1 = (f32[64,256]{1,0:T(8,128)S(1)}, f32[64,256]{1,0:T(8,128)S(1)}, u32[]{:S(2)}, u32[]{:S(2)}) collective-permute-start(f32[64,256]{1,0:T(8,128)S(1)} %slice_select_fusion.3), channel_id=1, source_target_pairs={{0,1},{1,0},{2,3},{3,2},{4,5},{5,4},{6,7},{7,6},{8,9},{9,8},{10,11... | collective-permute-start | bytes 196616 | tf_op jit(solution)/shard_map/ppermute | solution.py:17
  6.5 12.3 %collective-permute-start.9 = (f32[1,112,512]{2,1,0:T(8,128)S(1)}, f32[1,112,512]{2,1,0:T(8,128)S(1)}, u32[]{:S(2)}, u32[]{:S(2)}) collective-permute-start(f32[1,112,512]{2,1,0:T(8,128)S(1)} %bitcast.43), channel_id=1, source_target_pairs={{0,2},{1,3},{2,0},{3,1},{4,6},{5,7},{6,4},{7,5},{8,10},{9,11},{10,... | collective-permute-start | bytes 688136 | tf_op jit(solution)/shard_map/ppermute | solution.py:17
  9.2 7.2 %collective-permute-start.2 = (f32[64,256]{1,0:T(8,128)S(1)}, f32[64,256]{1,0:T(8,128)S(1)}, u32[]{:S(2)}, u32[]{:S(2)}) collective-permute-start(f32[64,256]{1,0:T(8,128)S(1)} %select_add_fusion), channel_id=1, source_target_pairs={{0,3},{1,2},{2,1},{3,0},{4,7},{5,6},{6,5},{7,4},{8,11},{9,10},{10,... | collective-permute-start | bytes 196616 | tf_op jit(solution)/shard_map/ppermute | solution.py:17
  10.5 6.4 %collective-permute-start.5 = (f32[64,256]{1,0:T(8,128)S(1)}, f32[64,256]{1,0:T(8,128)S(1)}, u32[]{:S(2)}, u32[]{:S(2)}) collective-permute-start(f32[64,256]{1,0:T(8,128)S(1)} %slice_select_fusion.2), channel_id=1, source_target_pairs={{0,1},{1,0},{2,3},{3,2},{4,5},{5,4},{6,7},{7,6},{8,9},{9,8},{10,11... | collective-permute-start | bytes 196616 | tf_op jit(solution)/shard_map/ppermute | solution.py:17
  10.9 1.6 %collective-permute-start.3 = (f32[1,128,512]{2,1,0:T(8,128)S(1)}, f32[1,128,512]{2,1,0:T(8,128)S(1)}, u32[]{:S(2)}, u32[]{:S(2)}) collective-permute-start(f32[1,128,512]{2,1,0:T(8,128)S(1)} %bitcast.41), channel_id=1, source_target_pairs={{0,1},{1,0},{2,3},{3,2},{4,5},{5,4},{6,7},{7,6},{8,9},{9,8},{10,11... | collective-permute-start | bytes 786440 | tf_op jit(solution)/shard_map/ppermute | solution.py:17
  12.1 4.8 %collective-permute-start.6 = (f32[256,256]{1,0:T(8,128)S(1)}, f32[256,256]{1,0:T(8,128)S(1)}, u32[]{:S(2)}, u32[]{:S(2)}) collective-permute-start(f32[256,256]{1,0:T(8,128)S(1)} %fusion.89), channel_id=1, source_target_pairs={{0,1},{1,0},{2,3},{3,2},{4,5},{5,4},{6,7},{7,6},{8,9},{9,8},{10,11... | collective-permute-start | bytes 786440 | tf_op jit(solution)/shard_map/ppermute | solution.py:17
  16.7 8.1 %collective-permute-start.4 = (f32[64,256]{1,0:T(8,128)S(1)}, f32[64,256]{1,0:T(8,128)S(1)}, u32[]{:S(2)}, u32[]{:S(2)}) collective-permute-start(f32[64,256]{1,0:T(8,128)S(1)} %fusion.15), channel_id=1, source_target_pairs={{0,1},{1,0},{2,3},{3,2},{4,5},{5,4},{6,7},{7,6},{8,9},{9,8},{10,11... | collective-permute-start | bytes 196616 | tf_op jit(solution)/shard_map/ppermute | solution.py:17
  17.2 7.4 %collective-permute-start.7 = (f32[64,256]{1,0:T(8,128)S(1)}, f32[64,256]{1,0:T(8,128)S(1)}, u32[]{:S(2)}, u32[]{:S(2)}) collective-permute-start(f32[64,256]{1,0:T(8,128)S(1)} %add_subtract_fusion.2._), channel_id=1, source_target_pairs={{0,3},{1,2},{2,1},{3,0},{4,7},{5,6},{6,5},{7,4},{8,11},{9,10},{10,... | collective-permute-start | bytes 196616 | tf_op jit(solution)/shard_map/ppermute | solution.py:17
  21.4 9.3 %collective-permute-start.17 = (f32[2,48,512]{2,1,0:T(8,128)S(1)}, f32[2,48,512]{2,1,0:T(8,128)S(1)}, u32[]{:S(2)}, u32[]{:S(2)}) collective-permute-start(f32[2,48,512]{2,1,0:T(8,128)S(1)} %slice.63), channel_id=1, source_target_pairs={{0,4},{1,5},{2,6},{3,7},{4,0},{5,1},{6,2},{7,3},{8,12},{9,13},{10,... | collective-permute-start | bytes 589832 | tf_op jit(solution)/shard_map/ppermute | solution.py:17
  23.0 3.4 %collective-permute-start.10 = (f32[2,64,512]{2,1,0:T(8,128)S(1)}, f32[2,64,512]{2,1,0:T(8,128)S(1)}, u32[]{:S(2)}, u32[]{:S(2)}) collective-permute-start(f32[2,64,512]{2,1,0:T(8,128)S(1)} %slice.60), channel_id=1, source_target_pairs={{0,1},{1,0},{2,3},{3,2},{4,5},{5,4},{6,7},{7,6},{8,9},{9,8},{10,11... | collective-permute-start | bytes 786440 | tf_op jit(solution)/shard_map/ppermute | solution.py:17
  24.1 6.2 %collective-permute-start.13 = (f32[256,256]{1,0:T(8,128)S(1)}, f32[256,256]{1,0:T(8,128)S(1)}, u32[]{:S(2)}, u32[]{:S(2)}) collective-permute-start(f32[256,256]{1,0:T(8,128)S(1)} %fusion.91), channel_id=1, source_target_pairs={{0,1},{1,0},{2,3},{3,2},{4,5},{5,4},{6,7},{7,6},{8,9},{9,8},{10,11... | collective-permute-start | bytes 786440 | tf_op jit(solution)/shard_map/ppermute | solution.py:17
  24.6 4.9 %collective-permute-start.8 = (f32[64,256]{1,0:T(8,128)S(1)}, f32[64,256]{1,0:T(8,128)S(1)}, u32[]{:S(2)}, u32[]{:S(2)}) collective-permute-start(f32[64,256]{1,0:T(8,128)S(1)} %add.42), channel_id=1, source_target_pairs={{0,5},{1,4},{2,7},{3,6},{4,1},{5,0},{6,3},{7,2},{8,13},{9,12},{10,... | collective-permute-start | bytes 196616 | tf_op jit(solution)/shard_map/ppermute | solution.py:17
  25.9 4.4 %collective-permute-start.12 = (f32[64,256]{1,0:T(8,128)S(1)}, f32[64,256]{1,0:T(8,128)S(1)}, u32[]{:S(2)}, u32[]{:S(2)}) collective-permute-start(f32[64,256]{1,0:T(8,128)S(1)} %slice_select_fusion.1), channel_id=1, source_target_pairs={{0,1},{1,0},{2,3},{3,2},{4,5},{5,4},{6,7},{7,6},{8,9},{9,8},{10,11... | collective-permute-start | bytes 196616 | tf_op jit(solution)/shard_map/ppermute | solution.py:17
  29.9 6.5 %collective-permute-start.11 = (f32[64,256]{1,0:T(8,128)S(1)}, f32[64,256]{1,0:T(8,128)S(1)}, u32[]{:S(2)}, u32[]{:S(2)}) collective-permute-start(f32[64,256]{1,0:T(8,128)S(1)} %fusion.28), channel_id=1, source_target_pairs={{0,1},{1,0},{2,3},{3,2},{4,5},{5,4},{6,7},{7,6},{8,9},{9,8},{10,11... | collective-permute-start | bytes 196616 | tf_op jit(solution)/shard_map/ppermute | solution.py:17
  30.6 4.1 %collective-permute-start.14 = (f32[64,256]{1,0:T(8,128)S(1)}, f32[64,256]{1,0:T(8,128)S(1)}, u32[]{:S(2)}, u32[]{:S(2)}) collective-permute-start(f32[64,256]{1,0:T(8,128)S(1)} %add_subtract_fusion.1), channel_id=1, source_target_pairs={{0,3},{1,2},{2,1},{3,0},{4,7},{5,6},{6,5},{7,4},{8,11},{9,10},{10,... | collective-permute-start | bytes 196616 | tf_op jit(solution)/shard_map/ppermute | solution.py:17
  30.8 13.8 %collective-permute-start.26 = (f32[4,16,512]{2,1,0:T(8,128)S(1)}, f32[4,16,512]{2,1,0:T(8,128)S(1)}, u32[]{:S(2)}, u32[]{:S(2)}) collective-permute-start(f32[4,16,512]{2,1,0:T(8,128)S(1)} %slice.67), channel_id=1, source_target_pairs={{0,8},{1,9},{2,10},{3,11},{4,12},{5,13},{6,14},{7,15},{8,0},{9,1},... | collective-permute-start | bytes 393224 | tf_op jit(solution)/shard_map/ppermute | solution.py:17
  33.7 9.3 %collective-permute-start.21 = (f32[256,256]{1,0:T(8,128)S(1)}, f32[256,256]{1,0:T(8,128)S(1)}, u32[]{:S(2)}, u32[]{:S(2)}) collective-permute-start(f32[256,256]{1,0:T(8,128)S(1)} %fusion.93), channel_id=1, source_target_pairs={{0,1},{1,0},{2,3},{3,2},{4,5},{5,4},{6,7},{7,6},{8,9},{9,8},{10,11... | collective-permute-start | bytes 786440 | tf_op jit(solution)/shard_map/ppermute | solution.py:17
  33.8 6.5 %collective-permute-start.18 = (f32[4,32,512]{2,1,0:T(8,128)S(1)}, f32[4,32,512]{2,1,0:T(8,128)S(1)}, u32[]{:S(2)}, u32[]{:S(2)}) collective-permute-start(f32[4,32,512]{2,1,0:T(8,128)S(1)} %slice.64), channel_id=1, source_target_pairs={{0,1},{1,0},{2,3},{3,2},{4,5},{5,4},{6,7},{7,6},{8,9},{9,8},{10,11... | collective-permute-start | bytes 786440 | tf_op jit(solution)/shard_map/ppermute | solution.py:17
  34.7 3.9 %collective-permute-start.15 = (f32[64,256]{1,0:T(8,128)S(1)}, f32[64,256]{1,0:T(8,128)S(1)}, u32[]{:S(2)}, u32[]{:S(2)}) collective-permute-start(f32[64,256]{1,0:T(8,128)S(1)} %add.45), channel_id=1, source_target_pairs={{0,5},{1,4},{2,7},{3,6},{4,1},{5,0},{6,3},{7,2},{8,13},{9,12},{10,... | collective-permute-start | bytes 196616 | tf_op jit(solution)/shard_map/ppermute | solution.py:17
  37.5 5.4 %collective-permute-start.20 = (f32[64,256]{1,0:T(8,128)S(1)}, f32[64,256]{1,0:T(8,128)S(1)}, u32[]{:S(2)}, u32[]{:S(2)}) collective-permute-start(f32[64,256]{1,0:T(8,128)S(1)} %slice_select_fusion), channel_id=1, source_target_pairs={{0,1},{1,0},{2,3},{3,2},{4,5},{5,4},{6,7},{7,6},{8,9},{9,8},{10,11... | collective-permute-start | bytes 196616 | tf_op jit(solution)/shard_map/ppermute | solution.py:17
  38.6 3.9 %collective-permute-start.16 = (f32[64,256]{1,0:T(8,128)S(1)}, f32[64,256]{1,0:T(8,128)S(1)}, u32[]{:S(2)}, u32[]{:S(2)}) collective-permute-start(f32[64,256]{1,0:T(8,128)S(1)} %add.46), channel_id=1, source_target_pairs={{0,9},{1,8},{2,11},{3,10},{4,13},{5,12},{6,15},{7,14},{8,1},{9,0},... | collective-permute-start | bytes 196616 | tf_op jit(solution)/shard_map/ppermute | solution.py:17
  43.2 4.0 %collective-permute-start.22 = (f32[64,256]{1,0:T(8,128)S(1)}, f32[64,256]{1,0:T(8,128)S(1)}, u32[]{:S(2)}, u32[]{:S(2)}) collective-permute-start(f32[64,256]{1,0:T(8,128)S(1)} %add_subtract_fusion), channel_id=1, source_target_pairs={{0,3},{1,2},{2,1},{3,0},{4,7},{5,6},{6,5},{7,4},{8,11},{9,10},{10,... | collective-permute-start | bytes 196616 | tf_op jit(solution)/shard_map/ppermute | solution.py:17
  44.6 8.2 %collective-permute-start.19 = (f32[64,256]{1,0:T(8,128)S(1)}, f32[64,256]{1,0:T(8,128)S(1)}, u32[]{:S(2)}, u32[]{:S(2)}) collective-permute-start(f32[64,256]{1,0:T(8,128)S(1)} %fusion.41), channel_id=1, source_target_pairs={{0,1},{1,0},{2,3},{3,2},{4,5},{5,4},{6,7},{7,6},{8,9},{9,8},{10,11... | collective-permute-start | bytes 196616 | tf_op jit(solution)/shard_map/ppermute | solution.py:17
  47.2 4.1 %collective-permute-start.23 = (f32[64,256]{1,0:T(8,128)S(1)}, f32[64,256]{1,0:T(8,128)S(1)}, u32[]{:S(2)}, u32[]{:S(2)}) collective-permute-start(f32[64,256]{1,0:T(8,128)S(1)} %add.49), channel_id=1, source_target_pairs={{0,5},{1,4},{2,7},{3,6},{4,1},{5,0},{6,3},{7,2},{8,13},{9,12},{10,... | collective-permute-start | bytes 196616 | tf_op jit(solution)/shard_map/ppermute | solution.py:17
  48.8 9.1 %collective-permute-start.27 = (f32[8,16,512]{2,1,0:T(8,128)S(1)}, f32[8,16,512]{2,1,0:T(8,128)S(1)}, u32[]{:S(2)}, u32[]{:S(2)}) collective-permute-start(f32[8,16,512]{2,1,0:T(8,128)S(1)} %maximum_select_fusion.7), channel_id=1, source_target_pairs={{0,1},{1,0},{2,3},{3,2},{4,5},{5,4},{6,7},{7,6},{8,9},{9,8},{10,11... | collective-permute-start | bytes 786440 | tf_op jit(solution)/shard_map/ppermute | solution.py:17
  51.3 4.1 %collective-permute-start.24 = (f32[64,256]{1,0:T(8,128)S(1)}, f32[64,256]{1,0:T(8,128)S(1)}, u32[]{:S(2)}, u32[]{:S(2)}) collective-permute-start(f32[64,256]{1,0:T(8,128)S(1)} %add.50), channel_id=1, source_target_pairs={{0,9},{1,8},{2,11},{3,10},{4,13},{5,12},{6,15},{7,14},{8,1},{9,0},... | collective-permute-start | bytes 196616 | tf_op jit(solution)/shard_map/ppermute | solution.py:17
  55.5 5.0 %collective-permute-start.25 = (f32[64,256]{1,0:T(8,128)S(1)}, f32[64,256]{1,0:T(8,128)S(1)}, u32[]{:S(2)}, u32[]{:S(2)}) collective-permute-start(f32[64,256]{1,0:T(8,128)S(1)} %add.51), channel_id=1, source_target_pairs={{0,17},{1,16},{2,19},{3,18},{4,21},{5,20},{6,23},{7,22},{8,25},{9,... | collective-permute-start | bytes 196616 | tf_op jit(solution)/shard_map/ppermute | solution.py:17
  60.9 2.5 %collective-permute-start.28 = (f32[64,256]{1,0:T(8,128)S(1)}, f32[64,256]{1,0:T(8,128)S(1)}, u32[]{:S(2)}, u32[]{:S(2)}) collective-permute-start(f32[64,256]{1,0:T(8,128)S(1)} %fusion.54), channel_id=1, source_target_pairs={{0,1},{1,0},{2,3},{3,2},{4,5},{5,4},{6,7},{7,6},{8,9},{9,8},{10,11... | collective-permute-start | bytes 196616 | tf_op jit(solution)/shard_map/ppermute | solution.py:17
where the time goes:
time: 64.9 us; the launch traced here: 64.8 us
  starting transfers between devices  25.6 us (39%)
  waiting for transfers between devices  21.3 us (33%)
  matrix products  9.97 us (15%)
  Pallas kernels  6.94 us (11%)
    ppermute x29, starting transfers between devices, exchange(): return lax.ppermute(value, 'leaf', pairs)  25.6 us
    ppermute x29, waiting for transfers between devices, exchange(): return lax.ppermute(value, 'leaf', pairs)  21.3 us
    pallas_call x1, Pallas kernels, begin(): pl.pallas_call(body, in_specs=[IN_HBM] * 4, out_specs=[IN_VMEM] * len(sha...  3.05 us
    dot_general x3, matrix products, on_device(): own = jnp.einsum('na,nb->ab', proj, corr, precision=HIGH)  2.98 us
    dot_general x8, matrix products, times_transposed(): return jnp.einsum('kb,ab->ka', left, right, precision=HIGH)  2.74 us
    dot_general x4, matrix products, update(): return state - jnp.einsum('ka,na->kn', held, corr, precision=HIGH)  2.63 us
    pallas_call x1, Pallas kernels, fetch(): pl.pallas_call(body, in_specs=[IN_HBM, IN_HBM, pl.BlockSpec(memory_space=...  2.54 us
    dot_general x4, matrix products, project(): return jnp.einsum('kn,nr->kr', state, basis, precision=HIGH)  1.62 us
  transfers between devices with their start and end apart: 29, of which 11 were waited for; matrix products, arithmetic and copies ran while one was open for 13% of the time, Pallas kernels for 4%

commit v1 on v0

--- a/solution.py
+++ b/solution.py
@@ -127,9 +127,9 @@
         out_specs=[IN_VMEM] * count,
         out_shape=[pltpu.VMEM((rows, rank), jnp.float32)] * count,
         scratch_shapes=[pltpu.SemaphoreType.DMA((count,))],
-        compiler_params=pltpu.CompilerParams(vmem_limit_bytes=45 * MIB),
+        compiler_params=pltpu.CompilerParams(vmem_limit_bytes=50 * MIB),
         cost_estimate=pl.CostEstimate(
-            flops=0, bytes_accessed=8 * count * rows * rank, transcendentals=0
+            flops=0, bytes_accessed=2**16, transcendentals=0
         ),
         name="fetch",
     )(proj_bases, corr_bases, after)
@@ -186,7 +186,9 @@
 
     heads = [(level, rank >> bits[level]) for level in chain if bits[level] == 1]
     tails = [(level, rank >> bits[level]) for level in chain if bits[level] > 1]
-    groups = [group for group in (heads, tails) if group]
+    near = [item for item in tails if heads and bits[item[0]] == 2]
+    far = [item for item in tails if item not in near]
+    groups = [group for group in (heads, near, far) if group]
     leaf_core = bits[first] == 0
     value, state, top_corr, next_proj, corr, proj, *fetched = begin(
         rhs, proj_bases, corr_bases, cores, first, leaf_core, groups
@@ -201,11 +203,10 @@
         both = jnp.where(low(0), jnp.stack([mine, part], 1), jnp.stack([part, mine], 1))
         table[level] = both.reshape(rank, 2 * rank)
 
-    def gather_steps():
-        block = fetched[-1][None]
-        waiting = [level for level, _ in tails]
+    def gather_steps(items, block, after):
+        waiting = [level for level, _ in items]
         bit = 1
-        coming = exchange(block, 2)
+        coming = exchange(block if after is None else tie(block, after), 2)
         while True:
             after = yield
             block = pair_up(low(bit), block, tie(coming, after), 0)
@@ -216,30 +217,40 @@
                 finish_table(level, tie(block[:, :rows], after))
                 block = block[:, rows:]
             waiting = [level for level in waiting if bits[level] > bit]
-            if waiting:
-                coming = exchange(tie(block, after), 1 << bit)
-            else:
+            if not waiting:
                 return
-
-    steps = gather_steps()
-    next(steps)
+            after = yield
+            coming = exchange(tie(block, after), 1 << bit)
+
+    gathers = []
+
+    def open_gather(items, block, after):
+        steps = gather_steps(items, block[None], after)
+        next(steps)
+        gathers.append(steps)
 
     def step(after):
         try:
-            steps.send(after)
+            gathers[0].send(after)
         except StopIteration:
-            pass
-
-    def solve(level, value, ahead_of):
+            gathers.pop(0)
+
+    if near:
+        open_gather(near, fetched[1], None)
+    else:
+        open_gather(far, fetched[-1], None)
+
+    def solve(level, value, ahead_of, later=None, fetch_rest=None):
         top = bits[level]
         for bit in range(1, top):
             value = ahead_of.get(bit, lambda v: v)(value)
             value = value + across(value, bit)
+        if near and level == near[0][0]:
+            open_gather(far, fetched[2], value)
         while level not in table:
             step(value)
-        if level == 1:
-            step(value)
-            step(value)
+        if fetch_rest is not None:
+            later.append(fetch_rest(value))
         value = ahead_of.get(top, lambda v: v)(value)
         stacked = pair_up(low(top), value, across(value, top), 1)
         stacked = stacked / jnp.sqrt(jnp.float32(rows_here << top))
@@ -258,33 +269,37 @@
     value = chip_sum(project(next_proj, state))
     if heads:
         finish_table(heads[0][0], tie(fetched[0], value)[None])
+    later = []
     for level in reversed(range(1, first)):
         start = value
-        if heads and level < first - 1:
+        if near and level == near[0][0]:
             step(start)
             step(start)
-        held = solve(level, value, {})
+        elif near and level < near[0][0]:
+            for _ in range(3):
+                step(start)
+        if level == first - 1:
+            later.append(fetch(proj_bases, corr_bases, [level - 2], [level - 1], start))
         if level == first - 2:
-            later = fetch(
-                proj_bases,
-                corr_bases,
-                list(reversed(range(level))),
-                list(reversed(range(level + 1))),
-                start,
+            fetch_rest = lambda v: fetch(
+                proj_bases, corr_bases, list(reversed(range(level - 1))), list(reversed(range(level))), v
             )
-            projs, corrs = list(later[:level]), list(later[level:])
+        held = solve(level, value, {}, later, fetch_rest if level == first - 2 else None)
         if level < first - 1:
-            proj, corr = projs.pop(0), corrs.pop(0)
+            proj, corr = (later[0][0], later[0][1]) if level == first - 2 else (later[1][0], later[1][1])
         proj, corr = tie(proj, start), tie(corr, start)
         ahead = chip_sum(project(proj, state))
         own = jnp.einsum("na,nb->ab", proj, corr, precision=HIGH)
         value = ahead - times_transposed(held, own + exchange(own, 1))
         if level > 1:
             state = update(corr, state, chip_gather(held))
-    state = update(corr, state, chip_gather(held))
-    ahead_of = {bits[0]: lambda v: tie(v, state)}
+    gathered = chip_gather(held)
+    state = update(corr, state, gathered)
+    ahead_of = {bits[0] - 1: lambda v: tie(v, gathered)}
+    if near:
+        step(value)
     held = solve(0, value, ahead_of)
-    return finish(state, corrs[0], chip_gather(held))
+    return finish(state, later[1][2], chip_gather(held))
 
 
 def solution(mesh):

time: 64.9 us -> 63.2 us (0.974)
  starting transfers between devices: 25.6 us -> 24.3 us
  waiting for transfers between devices: 21.3 us -> 20.1 us
  Pallas kernels: 6.94 us -> 7.84 us
    ppermute x29 -> x30, starting transfers between devices: 25.6 us -> 24.3 us  [exchange(): return lax.ppermute(value, 'leaf', pairs)]
    ppermute x29 -> x30, waiting for transfers between devices: 21.3 us -> 20.1 us  [exchange(): return lax.ppermute(value, 'leaf', pairs)]
    pallas_call x1 -> x2, Pallas kernels: 2.54 us -> 3.44 us  [fetch(): pl.pallas_call(body, in_specs=[IN_HBM, IN_HBM, pl.BlockSpec(memory_space=...]
  transfers between devices with their start and end apart: 29 -> 30, of which waited for: 11 -> 13; matrix products, arithmetic and copies ran while one was open for 13% -> 13% of each run, Pallas kernels for 4% -> 5%
where the time goes in v1:
time: 63.2 us; the launch traced here: 63.1 us
  starting transfers between devices  24.3 us (38%)
  waiting for transfers between devices  20.1 us (32%)
  matrix products  9.97 us (16%)
  Pallas kernels  7.84 us (12%)
    ppermute x30, starting transfers between devices, exchange(): return lax.ppermute(value, 'leaf', pairs)  24.3 us
    ppermute x30, waiting for transfers between devices, exchange(): return lax.ppermute(value, 'leaf', pairs)  20.1 us
    pallas_call x2, Pallas kernels, fetch(): pl.pallas_call(body, in_specs=[IN_HBM, IN_HBM, pl.BlockSpec(memory_space=...  3.44 us
    pallas_call x1, Pallas kernels, begin(): pl.pallas_call(body, in_specs=[IN_HBM] * 4, out_specs=[IN_VMEM] * len(sha...  3.05 us
    dot_general x3, matrix products, on_device(): own = jnp.einsum('na,nb->ab', proj, corr, precision=HIGH)  2.98 us
    dot_general x8, matrix products, times_transposed(): return jnp.einsum('kb,ab->ka', left, right, precision=HIGH)  2.75 us
    dot_general x4, matrix products, update(): return state - jnp.einsum('ka,na->kn', held, corr, precision=HIGH)  2.63 us
    dot_general x4, matrix products, project(): return jnp.einsum('kn,nr->kr', state, basis, precision=HIGH)  1.62 us
  transfers between devices with their start and end apart: 30, of which 13 were waited for; matrix products, arithmetic and copies ran while one was open for 13% of the time, Pallas kernels for 5%

profile of v1, /device:TPU:0, one launch (start us, length us, event | category | flops | bytes accessed | tf_op | source)
XLA Modules:
  0.0 63.1 jit_solution(13733074271302385269)
XLA Ops:
  0.0 3.0 %begin.1 = (f32[128,256]{1,0:T(8,128)S(1)}, f32[128,1024]{1,0:T(8,128)S(1)}, f32[1024,256]{1,0:T(8,128)S(1)}, f32[1024,256]{1,0:T(8,128)S(1)}, f32[1024,256]{1,0...) custom-call(f32[1024,128]{1,0:T(8,128)} %x_hbm, ...), custom_call_target="tpu_custom_call" | custom-call | flops 201326592 | bytes 4194304 | tf_op jit(solution)/shard_map/begin/pallas_call | solution.py:90
  3.1 0.5 collective-permute-start
  3.6 1.0 %collective-permute-done = f32[128,256]{1,0:T(8,128)S(1)} collective-permute-done((f32[128,256]{1,0:T(8,128)S(1)}, f32[128,256]{1,0:T(8,128)S(1)}, u32[]{:S(2)}, u32[]{:S(2)}) %collective-permute-start) | collective-permute-done | bytes 131104 | tf_op jit(solution)/shard_map/ppermute | solution.py:17
  4.6 0.4 fusion.1
  5.0 0.7 %convolution_subtract_fusion.3 = f32[128,1024]{1,0:T(8,128)S(1)} fusion(f32[128,1024]{1,0:T(8,128)S(1)} %get-tuple-element.46, f32[128,256]{1,0:T(8,128)S(1)} %fusion.1, f32[1024,256]{1,0:T(8,128)S(1)} %get-tuple-element.50), kind=kOutput, calls=%fused_computation.3 | convolution fusion | flops 201457664 | bytes 2228224 | tf_op jit(solution)/shard_map/ka,na->kn/dot_general | solution.py:260
  5.6 0.4 fusion.80
  6.1 0.4 collective-permute-start.1
  6.5 2.6 %collective-permute-start.9 = (f32[1,64,512]{2,1,0:T(8,128)S(1)}, f32[1,64,512]{2,1,0:T(8,128)S(1)}, u32[]{:S(2)}, u32[]{:S(2)}) collective-permute-start(f32[1,64,512]{2,1,0:T(8,128)S(1)} %bitcast.45), channel_id=1, source_target_pairs={{0,2},{1,3},{2,0},{3,1},{4,6},{5,7},{6,4},{7,5},{8,10},{9,11},{10,... | collective-permute-start | bytes 393224 | tf_op jit(solution)/shard_map/ppermute | solution.py:17
  9.2 0.9 %collective-permute-start.2 = (f32[64,256]{1,0:T(8,128)S(1)}, f32[64,256]{1,0:T(8,128)S(1)}, u32[]{:S(2)}, u32[]{:S(2)}) collective-permute-start(f32[64,256]{1,0:T(8,128)S(1)} %select_add_fusion._), channel_id=1, source_target_pairs={{0,3},{1,2},{2,1},{3,0},{4,7},{5,6},{6,5},{7,4},{8,11},{9,10},{10,... | collective-permute-start | bytes 196616 | tf_op jit(solution)/shard_map/ppermute | solution.py:17
  10.1 1.6 %fetch.2 = (f32[1024,256]{1,0:T(8,128)S(1)}, f32[1024,256]{1,0:T(8,128)S(1)}) custom-call(f32[5,1024,256]{2,1,0:T(8,128)} %p_hbm.5, f32[5,1024,256]{2,1,0:T(8,128)} %w_hbm.5, f32[64,256]{1,0:T(8,128)S(1)} %select_add_fusion._), custom_call_target="tpu_custom_call" | custom-call | bytes 65536 | tf_op jit(solution)/shard_map/fetch/pallas_call | solution.py:124
  11.6 0.4 collective-permute-start.3
  12.1 0.4 fusion.81
  12.5 0.2 collective-permute-start.5
  12.7 1.0 %fusion.82 = f32[256,256]{1,0:T(8,128)S(1)} fusion(f32[1024,256]{1,0:T(8,128)S(1)} %get-tuple-element.60, f32[1024,256]{1,0:T(8,128)S(1)} %get-tuple-element.57), kind=kOutput, calls=%fused_computation.106 | convolution fusion | flops 402653184 | bytes 2359296 | tf_op jit(solution)/shard_map/na,nb->ab/dot_general | solution.py:292
  13.7 0.4 collective-permute-start.6
  14.2 0.4 fusion.15
  14.6 0.2 collective-permute-start.4
  14.8 0.5 collective-permute-done.6
  15.3 0.3 add_subtract_fusion.2
  15.6 1.0 %collective-permute-start.7 = (f32[64,256]{1,0:T(8,128)S(1)}, f32[64,256]{1,0:T(8,128)S(1)}, u32[]{:S(2)}, u32[]{:S(2)}) collective-permute-start(f32[64,256]{1,0:T(8,128)S(1)} %add_subtract_fusion.2), channel_id=1, source_target_pairs={{0,3},{1,2},{2,1},{3,0},{4,7},{5,6},{6,5},{7,4},{8,11},{9,10},{10,... | collective-permute-start | bytes 196616 | tf_op jit(solution)/shard_map/ppermute | solution.py:17
  16.7 0.5 collective-permute-start.10
  17.1 1.0 %fusion.84 = f32[256,256]{1,0:T(8,128)S(1)} fusion(f32[1024,256]{1,0:T(8,128)S(1)} %get-tuple-element.68, f32[1024,256]{1,0:T(8,128)S(1)} %get-tuple-element.65), kind=kOutput, calls=%fused_computation.108 | convolution fusion | flops 402653184 | bytes 2359296 | tf_op jit(solution)/shard_map/na,nb->ab/dot_general | solution.py:292
  18.1 0.2 collective-permute-start.13
  18.3 1.3 %collective-permute-done.7 = f32[64,256]{1,0:T(8,128)S(1)} collective-permute-done((f32[64,256]{1,0:T(8,128)S(1)}, f32[64,256]{1,0:T(8,128)S(1)}, u32[]{:S(2)}, u32[]{:S(2)}) %collective-permute-start.7) | collective-permute-done | bytes 65568 | tf_op jit(solution)/shard_map/ppermute | solution.py:17
  19.6 1.5 %collective-permute-start.8 = (f32[64,256]{1,0:T(8,128)S(1)}, f32[64,256]{1,0:T(8,128)S(1)}, u32[]{:S(2)}, u32[]{:S(2)}) collective-permute-start(f32[64,256]{1,0:T(8,128)S(1)} %add.42._), channel_id=1, source_target_pairs={{0,5},{1,4},{2,7},{3,6},{4,1},{5,0},{6,3},{7,2},{8,13},{9,12},{10,... | collective-permute-start | bytes 196616 | tf_op jit(solution)/shard_map/ppermute | solution.py:17
  21.1 1.9 %fetch.3 = (f32[1024,256]{1,0:T(8,128)S(1)}, f32[1024,256]{1,0:T(8,128)S(1)}, f32[1024,256]{1,0:T(8,128)S(1)}) custom-call(f32[5,1024,256]{2,1,0:T(8,128)} %p_hbm.5, f32[5,1024,256]{2,1,0:T(8,128)} %w_hbm.5, f32[64,256]{1,0:T(8,128)S(1)} %add.42._), custom_call_target="tpu_custom_call" | custom-call | bytes 65536 | tf_op jit(solution)/shard_map/fetch/pallas_call | solution.py:124
  23.0 1.3 %collective-permute-start.17 = (f32[1,48,512]{2,1,0:T(8,128)S(1)}, f32[1,48,512]{2,1,0:T(8,128)S(1)}, u32[]{:S(2)}, u32[]{:S(2)}) collective-permute-start(f32[1,48,512]{2,1,0:T(8,128)S(1)} %bitcast.47), channel_id=1, source_target_pairs={{0,2},{1,3},{2,0},{3,1},{4,6},{5,7},{6,4},{7,5},{8,10},{9,11},{10,... | collective-permute-start | bytes 294920 | tf_op jit(solution)/shard_map/ppermute | solution.py:17
  24.3 0.7 %convolution_subtract_fusion.2 = f32[128,1024]{1,0:T(8,128)S(1)} fusion(f32[128,1024]{1,0:T(8,128)S(1)} %convolution_subtract_fusion.3, f32[1024,256]{1,0:T(8,128)S(1)} %get-tuple-element.57, f32[64,256]{1,0:T(8,128)S(1)} %collective-permute-done.4, f32[64,256]{1,0:T(8,128)S(1)} %fusion.15, pred[]{:T(512)S(6)} %eq.18), kind=kOutput, calls=%fused_computation.2 | convolution fusion | flops 201555968 | bytes 2228225 | tf_op jit(solution)/shard_map/ka,na->kn/dot_general | solution.py:260
  25.0 0.4 fusion.83
  25.7 0.4 fusion.28
  26.0 0.5 collective-permute-start.11
  26.5 0.2 collective-permute-done.12
  26.7 0.3 add_subtract_fusion.1
  27.0 0.6 collective-permute-start.14
  27.6 0.4 collective-permute-done.17
  28.0 0.6 collective-permute-start.18
  28.6 1.0 %fusion.86 = f32[256,256]{1,0:T(8,128)S(1)} fusion(f32[1024,256]{1,0:T(8,128)S(1)} %get-tuple-element.80, f32[1024,256]{1,0:T(8,128)S(1)} %get-tuple-element.76), kind=kOutput, calls=%fused_computation.110 | convolution fusion | flops 402653184 | bytes 2359296 | tf_op jit(solution)/shard_map/na,nb->ab/dot_general | solution.py:292
  29.6 1.5 %collective-permute-done.14 = f32[64,256]{1,0:T(8,128)S(1)} collective-permute-done((f32[64,256]{1,0:T(8,128)S(1)}, f32[64,256]{1,0:T(8,128)S(1)}, u32[]{:S(2)}, u32[]{:S(2)}) %collective-permute-start.14) | collective-permute-done | bytes 65568 | tf_op jit(solution)/shard_map/ppermute | solution.py:17
  31.2 0.3 collective-permute-start.15
  31.5 0.7 %convolution_subtract_fusion.1 = f32[128,1024]{1,0:T(8,128)S(1)} fusion(f32[128,1024]{1,0:T(8,128)S(1)} %convolution_subtract_fusion.2, f32[1024,256]{1,0:T(8,128)S(1)} %get-tuple-element.65, f32[64,256]{1,0:T(8,128)S(1)} %collective-permute-done.11, f32[64,256]{1,0:T(8,128)S(1)} %fusion.28, pred[]{:T(512)S(6)} %eq.18), kind=kOutput, calls=%fused_computation.1 | convolution fusion | flops 201555968 | bytes 2228225 | tf_op jit(solution)/shard_map/ka,na->kn/dot_general | solution.py:260
  32.2 3.5 %collective-permute-done.15 = f32[64,256]{1,0:T(8,128)S(1)} collective-permute-done((f32[64,256]{1,0:T(8,128)S(1)}, f32[64,256]{1,0:T(8,128)S(1)}, u32[]{:S(2)}, u32[]{:S(2)}) %collective-permute-start.15) | collective-permute-done | bytes 65568 | tf_op jit(solution)/shard_map/ppermute | solution.py:17
  35.8 0.5 collective-permute-start.19
  36.2 0.4 fusion.85
  36.7 0.2 collective-permute-start.21
  36.8 1.6 %collective-permute-start.16 = (f32[64,256]{1,0:T(8,128)S(1)}, f32[64,256]{1,0:T(8,128)S(1)}, u32[]{:S(2)}, u32[]{:S(2)}) collective-permute-start(f32[64,256]{1,0:T(8,128)S(1)} %add.46), channel_id=1, source_target_pairs={{0,9},{1,8},{2,11},{3,10},{4,13},{5,12},{6,15},{7,14},{8,1},{9,0},... | collective-permute-start | bytes 196616 | tf_op jit(solution)/shard_map/ppermute | solution.py:17
  38.6 2.1 %collective-permute-done.16 = f32[64,256]{1,0:T(8,128)S(1)} collective-permute-done((f32[64,256]{1,0:T(8,128)S(1)}, f32[64,256]{1,0:T(8,128)S(1)}, u32[]{:S(2)}, u32[]{:S(2)}) %collective-permute-start.16) | collective-permute-done | bytes 65568 | tf_op jit(solution)/shard_map/ppermute | solution.py:17
  40.7 0.4 fusion.41
  41.1 0.3 add_subtract_fusion
  41.4 1.3 %collective-permute-start.23 = (f32[64,256]{1,0:T(8,128)S(1)}, f32[64,256]{1,0:T(8,128)S(1)}, u32[]{:S(2)}, u32[]{:S(2)}) collective-permute-start(f32[64,256]{1,0:T(8,128)S(1)} %add_subtract_fusion), channel_id=1, source_target_pairs={{0,3},{1,2},{2,1},{3,0},{4,7},{5,6},{6,5},{7,4},{8,11},{9,10},{10,... | collective-permute-start | bytes 196616 | tf_op jit(solution)/shard_map/ppermute | solution.py:17
  42.7 0.1 collective-permute-start.20
  42.8 1.7 %collective-permute-start.27 = (f32[4,16,512]{2,1,0:T(8,128)S(1)}, f32[4,16,512]{2,1,0:T(8,128)S(1)}, u32[]{:S(2)}, u32[]{:S(2)}) collective-permute-start(f32[4,16,512]{2,1,0:T(8,128)S(1)} %slice.57), channel_id=1, source_target_pairs={{0,8},{1,9},{2,10},{3,11},{4,12},{5,13},{6,14},{7,15},{8,0},{9,1},... | collective-permute-start | bytes 393224 | tf_op jit(solution)/shard_map/ppermute | solution.py:17
  44.5 0.9 %collective-permute-done.23 = f32[64,256]{1,0:T(8,128)S(1)} collective-permute-done((f32[64,256]{1,0:T(8,128)S(1)}, f32[64,256]{1,0:T(8,128)S(1)}, u32[]{:S(2)}, u32[]{:S(2)}) %collective-permute-start.23) | collective-permute-done | bytes 65568 | tf_op jit(solution)/shard_map/ppermute | solution.py:17
  45.4 0.5 collective-permute-start.24
  45.9 3.6 %collective-permute-done.24 = f32[64,256]{1,0:T(8,128)S(1)} collective-permute-done((f32[64,256]{1,0:T(8,128)S(1)}, f32[64,256]{1,0:T(8,128)S(1)}, u32[]{:S(2)}, u32[]{:S(2)}) %collective-permute-start.24) | collective-permute-done | bytes 65568 | tf_op jit(solution)/shard_map/ppermute | solution.py:17
  49.4 1.5 %collective-permute-start.25 = (f32[64,256]{1,0:T(8,128)S(1)}, f32[64,256]{1,0:T(8,128)S(1)}, u32[]{:S(2)}, u32[]{:S(2)}) collective-permute-start(f32[64,256]{1,0:T(8,128)S(1)} %add.50), channel_id=1, source_target_pairs={{0,9},{1,8},{2,11},{3,10},{4,13},{5,12},{6,15},{7,14},{8,1},{9,0},... | collective-permute-start | bytes 196616 | tf_op jit(solution)/shard_map/ppermute | solution.py:17
  50.9 2.7 %collective-permute-done.25 = f32[64,256]{1,0:T(8,128)S(1)} collective-permute-done((f32[64,256]{1,0:T(8,128)S(1)}, f32[64,256]{1,0:T(8,128)S(1)}, u32[]{:S(2)}, u32[]{:S(2)}) %collective-permute-start.25) | collective-permute-done | bytes 65568 | tf_op jit(solution)/shard_map/ppermute | solution.py:17
  53.6 0.2 collective-permute-start.28
  53.8 2.6 %collective-permute-start.26 = (f32[64,256]{1,0:T(8,128)S(1)}, f32[64,256]{1,0:T(8,128)S(1)}, u32[]{:S(2)}, u32[]{:S(2)}) collective-permute-start(f32[64,256]{1,0:T(8,128)S(1)} %add.51), channel_id=1, source_target_pairs={{0,17},{1,16},{2,19},{3,18},{4,21},{5,20},{6,23},{7,22},{8,25},{9,... | collective-permute-start | bytes 196616 | tf_op jit(solution)/shard_map/ppermute | solution.py:17
  56.5 2.2 %collective-permute-done.26 = f32[64,256]{1,0:T(8,128)S(1)} collective-permute-done((f32[64,256]{1,0:T(8,128)S(1)}, f32[64,256]{1,0:T(8,128)S(1)}, u32[]{:S(2)}, u32[]{:S(2)}) %collective-permute-start.26) | collective-permute-done | bytes 65568 | tf_op jit(solution)/shard_map/ppermute | solution.py:17
  58.7 0.4 fusion.49
  59.0 1.8 %collective-permute-start.29 = (f32[64,256]{1,0:T(8,128)S(1)}, f32[64,256]{1,0:T(8,128)S(1)}, u32[]{:S(2)}, u32[]{:S(2)}) collective-permute-start(f32[64,256]{1,0:T(8,128)S(1)} %fusion.49), channel_id=1, source_target_pairs={{0,1},{1,0},{2,3},{3,2},{4,5},{5,4},{6,7},{7,6},{8,9},{9,8},{10,11... | collective-permute-start | bytes 196616 | tf_op jit(solution)/shard_map/ppermute | solution.py:17
  60.8 0.7 %convolution_subtract_fusion.x_ref = f32[128,1024]{1,0:T(8,128)S(1)} fusion(f32[128,1024]{1,0:T(8,128)S(1)} %convolution_subtract_fusion.1, f32[128,256]{1,0:T(8,128)S(1)} %maximum_select_fusion.16, f32[1024,256]{1,0:T(8,128)S(1)} %get-tuple-element.76), kind=kOutput, calls=%fused_computation | convolution fusion | flops 201457664 | bytes 2228224 | tf_op jit(solution)/shard_map/ka,na->kn/dot_general | solution.py:260
  61.5 0.2 collective-permute-done.29
  61.7 1.4 %finish.1 = f32[1024,128]{1,0:T(8,128)} custom-call(f32[128,1024]{1,0:T(8,128)S(1)} %convolution_subtract_fusion.x_ref, f32[1024,256]{1,0:T(8,128)S(1)} %get-tuple-element.77.w_ref, f32[128,256]{1,0:T(8,128)S(1)} %maximum_select_fusion.18.t_ref), custom_call_target="tpu_custom_call" | custom-call | flops 201326592 | bytes 2097152 | tf_op jit(solution)/shard_map/finish/pallas_call | solution.py:144
  (45 shorter events, 0.8 us)
Async XLA Ops:
  3.1 1.5 %collective-permute-start = (f32[128,256]{1,0:T(8,128)S(1)}, f32[128,256]{1,0:T(8,128)S(1)}, u32[]{:S(2)}, u32[]{:S(2)}) collective-permute-start(f32[128,256]{1,0:T(8,128)S(1)} %get-tuple-element.48), channel_id=1, source_target_pairs={{0,1},{1,0},{2,3},{3,2},{4,5},{5,4},{6,7},{7,6},{8,9},{9,8},{10,11... | collective-permute-start | bytes 393224 | tf_op jit(solution)/shard_map/ppermute | solution.py:17
  6.1 3.1 %collective-permute-start.1 = (f32[64,256]{1,0:T(8,128)S(1)}, f32[64,256]{1,0:T(8,128)S(1)}, u32[]{:S(2)}, u32[]{:S(2)}) collective-permute-start(f32[64,256]{1,0:T(8,128)S(1)} %slice_select_fusion.3), channel_id=1, source_target_pairs={{0,1},{1,0},{2,3},{3,2},{4,5},{5,4},{6,7},{7,6},{8,9},{9,8},{10,11... | collective-permute-start | bytes 196616 | tf_op jit(solution)/shard_map/ppermute | solution.py:17
  6.5 10.2 %collective-permute-start.9 = (f32[1,64,512]{2,1,0:T(8,128)S(1)}, f32[1,64,512]{2,1,0:T(8,128)S(1)}, u32[]{:S(2)}, u32[]{:S(2)}) collective-permute-start(f32[1,64,512]{2,1,0:T(8,128)S(1)} %bitcast.45), channel_id=1, source_target_pairs={{0,2},{1,3},{2,0},{3,1},{4,6},{5,7},{6,4},{7,5},{8,10},{9,11},{10,... | collective-permute-start | bytes 393224 | tf_op jit(solution)/shard_map/ppermute | solution.py:17
  9.2 5.1 %collective-permute-start.2 = (f32[64,256]{1,0:T(8,128)S(1)}, f32[64,256]{1,0:T(8,128)S(1)}, u32[]{:S(2)}, u32[]{:S(2)}) collective-permute-start(f32[64,256]{1,0:T(8,128)S(1)} %select_add_fusion._), channel_id=1, source_target_pairs={{0,3},{1,2},{2,1},{3,0},{4,7},{5,6},{6,5},{7,4},{8,11},{9,10},{10,... | collective-permute-start | bytes 196616 | tf_op jit(solution)/shard_map/ppermute | solution.py:17
  11.6 2.5 %collective-permute-start.3 = (f32[1,128,512]{2,1,0:T(8,128)S(1)}, f32[1,128,512]{2,1,0:T(8,128)S(1)}, u32[]{:S(2)}, u32[]{:S(2)}) collective-permute-start(f32[1,128,512]{2,1,0:T(8,128)S(1)} %bitcast.43), channel_id=1, source_target_pairs={{0,1},{1,0},{2,3},{3,2},{4,5},{5,4},{6,7},{7,6},{8,9},{9,8},{10,11... | collective-permute-start | bytes 786440 | tf_op jit(solution)/shard_map/ppermute | solution.py:17
  12.5 2.3 %collective-permute-start.5 = (f32[64,256]{1,0:T(8,128)S(1)}, f32[64,256]{1,0:T(8,128)S(1)}, u32[]{:S(2)}, u32[]{:S(2)}) collective-permute-start(f32[64,256]{1,0:T(8,128)S(1)} %slice_select_fusion.2), channel_id=1, source_target_pairs={{0,1},{1,0},{2,3},{3,2},{4,5},{5,4},{6,7},{7,6},{8,9},{9,8},{10,11... | collective-permute-start | bytes 196616 | tf_op jit(solution)/shard_map/ppermute | solution.py:17
  13.7 1.6 %collective-permute-start.6 = (f32[256,256]{1,0:T(8,128)S(1)}, f32[256,256]{1,0:T(8,128)S(1)}, u32[]{:S(2)}, u32[]{:S(2)}) collective-permute-start(f32[256,256]{1,0:T(8,128)S(1)} %fusion.82), channel_id=1, source_target_pairs={{0,1},{1,0},{2,3},{3,2},{4,5},{5,4},{6,7},{7,6},{8,9},{9,8},{10,11... | collective-permute-start | bytes 786440 | tf_op jit(solution)/shard_map/ppermute | solution.py:17
  14.6 9.7 %collective-permute-start.4 = (f32[64,256]{1,0:T(8,128)S(1)}, f32[64,256]{1,0:T(8,128)S(1)}, u32[]{:S(2)}, u32[]{:S(2)}) collective-permute-start(f32[64,256]{1,0:T(8,128)S(1)} %fusion.15), channel_id=1, source_target_pairs={{0,1},{1,0},{2,3},{3,2},{4,5},{5,4},{6,7},{7,6},{8,9},{9,8},{10,11... | collective-permute-start | bytes 196616 | tf_op jit(solution)/shard_map/ppermute | solution.py:17
  15.6 4.0 %collective-permute-start.7 = (f32[64,256]{1,0:T(8,128)S(1)}, f32[64,256]{1,0:T(8,128)S(1)}, u32[]{:S(2)}, u32[]{:S(2)}) collective-permute-start(f32[64,256]{1,0:T(8,128)S(1)} %add_subtract_fusion.2), channel_id=1, source_target_pairs={{0,3},{1,2},{2,1},{3,0},{4,7},{5,6},{6,5},{7,4},{8,11},{9,10},{10,... | collective-permute-start | bytes 196616 | tf_op jit(solution)/shard_map/ppermute | solution.py:17
  16.7 8.9 %collective-permute-start.10 = (f32[2,64,512]{2,1,0:T(8,128)S(1)}, f32[2,64,512]{2,1,0:T(8,128)S(1)}, u32[]{:S(2)}, u32[]{:S(2)}) collective-permute-start(f32[2,64,512]{2,1,0:T(8,128)S(1)} %maximum_select_fusion.6), channel_id=1, source_target_pairs={{0,1},{1,0},{2,3},{3,2},{4,5},{5,4},{6,7},{7,6},{8,9},{9,8},{10,11... | collective-permute-start | bytes 786440 | tf_op jit(solution)/shard_map/ppermute | solution.py:17
  18.1 8.6 %collective-permute-start.13 = (f32[256,256]{1,0:T(8,128)S(1)}, f32[256,256]{1,0:T(8,128)S(1)}, u32[]{:S(2)}, u32[]{:S(2)}) collective-permute-start(f32[256,256]{1,0:T(8,128)S(1)} %fusion.84), channel_id=1, source_target_pairs={{0,1},{1,0},{2,3},{3,2},{4,5},{5,4},{6,7},{7,6},{8,9},{9,8},{10,11... | collective-permute-start | bytes 786440 | tf_op jit(solution)/shard_map/ppermute | solution.py:17
  19.6 6.1 %collective-permute-start.8 = (f32[64,256]{1,0:T(8,128)S(1)}, f32[64,256]{1,0:T(8,128)S(1)}, u32[]{:S(2)}, u32[]{:S(2)}) collective-permute-start(f32[64,256]{1,0:T(8,128)S(1)} %add.42._), channel_id=1, source_target_pairs={{0,5},{1,4},{2,7},{3,6},{4,1},{5,0},{6,3},{7,2},{8,13},{9,12},{10,... | collective-permute-start | bytes 196616 | tf_op jit(solution)/shard_map/ppermute | solution.py:17
  23.0 5.0 %collective-permute-start.17 = (f32[1,48,512]{2,1,0:T(8,128)S(1)}, f32[1,48,512]{2,1,0:T(8,128)S(1)}, u32[]{:S(2)}, u32[]{:S(2)}) collective-permute-start(f32[1,48,512]{2,1,0:T(8,128)S(1)} %bitcast.47), channel_id=1, source_target_pairs={{0,2},{1,3},{2,0},{3,1},{4,6},{5,7},{6,4},{7,5},{8,10},{9,11},{10,... | collective-permute-start | bytes 294920 | tf_op jit(solution)/shard_map/ppermute | solution.py:17
  25.4 1.3 %collective-permute-start.12 = (f32[64,256]{1,0:T(8,128)S(1)}, f32[64,256]{1,0:T(8,128)S(1)}, u32[]{:S(2)}, u32[]{:S(2)}) collective-permute-start(f32[64,256]{1,0:T(8,128)S(1)} %slice_select_fusion.1), channel_id=1, source_target_pairs={{0,1},{1,0},{2,3},{3,2},{4,5},{5,4},{6,7},{7,6},{8,9},{9,8},{10,11... | collective-permute-start | bytes 196616 | tf_op jit(solution)/shard_map/ppermute | solution.py:17
  26.0 5.5 %collective-permute-start.11 = (f32[64,256]{1,0:T(8,128)S(1)}, f32[64,256]{1,0:T(8,128)S(1)}, u32[]{:S(2)}, u32[]{:S(2)}) collective-permute-start(f32[64,256]{1,0:T(8,128)S(1)} %fusion.28), channel_id=1, source_target_pairs={{0,1},{1,0},{2,3},{3,2},{4,5},{5,4},{6,7},{7,6},{8,9},{9,8},{10,11... | collective-permute-start | bytes 196616 | tf_op jit(solution)/shard_map/ppermute | solution.py:17
  27.0 4.1 %collective-permute-start.14 = (f32[64,256]{1,0:T(8,128)S(1)}, f32[64,256]{1,0:T(8,128)S(1)}, u32[]{:S(2)}, u32[]{:S(2)}) collective-permute-start(f32[64,256]{1,0:T(8,128)S(1)} %add_subtract_fusion.1), channel_id=1, source_target_pairs={{0,3},{1,2},{2,1},{3,0},{4,7},{5,6},{6,5},{7,4},{8,11},{9,10},{10,... | collective-permute-start | bytes 196616 | tf_op jit(solution)/shard_map/ppermute | solution.py:17
  28.0 7.7 %collective-permute-start.18 = (f32[2,48,512]{2,1,0:T(8,128)S(1)}, f32[2,48,512]{2,1,0:T(8,128)S(1)}, u32[]{:S(2)}, u32[]{:S(2)}) collective-permute-start(f32[2,48,512]{2,1,0:T(8,128)S(1)} %maximum_select_fusion.8), channel_id=1, source_target_pairs={{0,4},{1,5},{2,6},{3,7},{4,0},{5,1},{6,2},{7,3},{8,12},{9,13},{10,... | collective-permute-start | bytes 589832 | tf_op jit(solution)/shard_map/ppermute | solution.py:17
  29.6 11.5 %collective-permute-start.22 = (f32[256,256]{1,0:T(8,128)S(1)}, f32[256,256]{1,0:T(8,128)S(1)}, u32[]{:S(2)}, u32[]{:S(2)}) collective-permute-start(f32[256,256]{1,0:T(8,128)S(1)} %fusion.86), channel_id=1, source_target_pairs={{0,1},{1,0},{2,3},{3,2},{4,5},{5,4},{6,7},{7,6},{8,9},{9,8},{10,11... | collective-permute-start | bytes 786440 | tf_op jit(solution)/shard_map/ppermute | solution.py:17
  31.2 4.5 %collective-permute-start.15 = (f32[64,256]{1,0:T(8,128)S(1)}, f32[64,256]{1,0:T(8,128)S(1)}, u32[]{:S(2)}, u32[]{:S(2)}) collective-permute-start(f32[64,256]{1,0:T(8,128)S(1)} %add.45), channel_id=1, source_target_pairs={{0,5},{1,4},{2,7},{3,6},{4,1},{5,0},{6,3},{7,2},{8,13},{9,12},{10,... | collective-permute-start | bytes 196616 | tf_op jit(solution)/shard_map/ppermute | solution.py:17
  35.8 2.7 %collective-permute-start.19 = (f32[4,32,512]{2,1,0:T(8,128)S(1)}, f32[4,32,512]{2,1,0:T(8,128)S(1)}, u32[]{:S(2)}, u32[]{:S(2)}) collective-permute-start(f32[4,32,512]{2,1,0:T(8,128)S(1)} %slice.54), channel_id=1, source_target_pairs={{0,1},{1,0},{2,3},{3,2},{4,5},{5,4},{6,7},{7,6},{8,9},{9,8},{10,11... | collective-permute-start | bytes 786440 | tf_op jit(solution)/shard_map/ppermute | solution.py:17
  36.7 4.4 %collective-permute-start.21 = (f32[64,256]{1,0:T(8,128)S(1)}, f32[64,256]{1,0:T(8,128)S(1)}, u32[]{:S(2)}, u32[]{:S(2)}) collective-permute-start(f32[64,256]{1,0:T(8,128)S(1)} %slice_select_fusion), channel_id=1, source_target_pairs={{0,1},{1,0},{2,3},{3,2},{4,5},{5,4},{6,7},{7,6},{8,9},{9,8},{10,11... | collective-permute-start | bytes 196616 | tf_op jit(solution)/shard_map/ppermute | solution.py:17
  36.8 3.8 %collective-permute-start.16 = (f32[64,256]{1,0:T(8,128)S(1)}, f32[64,256]{1,0:T(8,128)S(1)}, u32[]{:S(2)}, u32[]{:S(2)}) collective-permute-start(f32[64,256]{1,0:T(8,128)S(1)} %add.46), channel_id=1, source_target_pairs={{0,9},{1,8},{2,11},{3,10},{4,13},{5,12},{6,15},{7,14},{8,1},{9,0},... | collective-permute-start | bytes 196616 | tf_op jit(solution)/shard_map/ppermute | solution.py:17
  41.4 4.0 %collective-permute-start.23 = (f32[64,256]{1,0:T(8,128)S(1)}, f32[64,256]{1,0:T(8,128)S(1)}, u32[]{:S(2)}, u32[]{:S(2)}) collective-permute-start(f32[64,256]{1,0:T(8,128)S(1)} %add_subtract_fusion), channel_id=1, source_target_pairs={{0,3},{1,2},{2,1},{3,0},{4,7},{5,6},{6,5},{7,4},{8,11},{9,10},{10,... | collective-permute-start | bytes 196616 | tf_op jit(solution)/shard_map/ppermute | solution.py:17
  42.7 3.2 %collective-permute-start.20 = (f32[64,256]{1,0:T(8,128)S(1)}, f32[64,256]{1,0:T(8,128)S(1)}, u32[]{:S(2)}, u32[]{:S(2)}) collective-permute-start(f32[64,256]{1,0:T(8,128)S(1)} %fusion.41), channel_id=1, source_target_pairs={{0,1},{1,0},{2,3},{3,2},{4,5},{5,4},{6,7},{7,6},{8,9},{9,8},{10,11... | collective-permute-start | bytes 196616 | tf_op jit(solution)/shard_map/ppermute | solution.py:17
  42.8 10.8 %collective-permute-start.27 = (f32[4,16,512]{2,1,0:T(8,128)S(1)}, f32[4,16,512]{2,1,0:T(8,128)S(1)}, u32[]{:S(2)}, u32[]{:S(2)}) collective-permute-start(f32[4,16,512]{2,1,0:T(8,128)S(1)} %slice.57), channel_id=1, source_target_pairs={{0,8},{1,9},{2,10},{3,11},{4,12},{5,13},{6,14},{7,15},{8,0},{9,1},... | collective-permute-start | bytes 393224 | tf_op jit(solution)/shard_map/ppermute | solution.py:17
  45.4 4.1 %collective-permute-start.24 = (f32[64,256]{1,0:T(8,128)S(1)}, f32[64,256]{1,0:T(8,128)S(1)}, u32[]{:S(2)}, u32[]{:S(2)}) collective-permute-start(f32[64,256]{1,0:T(8,128)S(1)} %add.49), channel_id=1, source_target_pairs={{0,5},{1,4},{2,7},{3,6},{4,1},{5,0},{6,3},{7,2},{8,13},{9,12},{10,... | collective-permute-start | bytes 196616 | tf_op jit(solution)/shard_map/ppermute | solution.py:17
  49.4 4.1 %collective-permute-start.25 = (f32[64,256]{1,0:T(8,128)S(1)}, f32[64,256]{1,0:T(8,128)S(1)}, u32[]{:S(2)}, u32[]{:S(2)}) collective-permute-start(f32[64,256]{1,0:T(8,128)S(1)} %add.50), channel_id=1, source_target_pairs={{0,9},{1,8},{2,11},{3,10},{4,13},{5,12},{6,15},{7,14},{8,1},{9,0},... | collective-permute-start | bytes 196616 | tf_op jit(solution)/shard_map/ppermute | solution.py:17
  53.6 2.8 %collective-permute-start.28 = (f32[8,16,512]{2,1,0:T(8,128)S(1)}, f32[8,16,512]{2,1,0:T(8,128)S(1)}, u32[]{:S(2)}, u32[]{:S(2)}) collective-permute-start(f32[8,16,512]{2,1,0:T(8,128)S(1)} %maximum_select_fusion.7), channel_id=1, source_target_pairs={{0,1},{1,0},{2,3},{3,2},{4,5},{5,4},{6,7},{7,6},{8,9},{9,8},{10,11... | collective-permute-start | bytes 786440 | tf_op jit(solution)/shard_map/ppermute | solution.py:17
  53.8 4.8 %collective-permute-start.26 = (f32[64,256]{1,0:T(8,128)S(1)}, f32[64,256]{1,0:T(8,128)S(1)}, u32[]{:S(2)}, u32[]{:S(2)}) collective-permute-start(f32[64,256]{1,0:T(8,128)S(1)} %add.51), channel_id=1, source_target_pairs={{0,17},{1,16},{2,19},{3,18},{4,21},{5,20},{6,23},{7,22},{8,25},{9,... | collective-permute-start | bytes 196616 | tf_op jit(solution)/shard_map/ppermute | solution.py:17
  59.0 2.7 %collective-permute-start.29 = (f32[64,256]{1,0:T(8,128)S(1)}, f32[64,256]{1,0:T(8,128)S(1)}, u32[]{:S(2)}, u32[]{:S(2)}) collective-permute-start(f32[64,256]{1,0:T(8,128)S(1)} %fusion.49), channel_id=1, source_target_pairs={{0,1},{1,0},{2,3},{3,2},{4,5},{5,4},{6,7},{7,6},{8,9},{9,8},{10,11... | collective-permute-start | bytes 196616 | tf_op jit(solution)/shard_map/ppermute | solution.py:17

commit v2 on v1

--- a/solution.py
+++ b/solution.py
@@ -245,6 +245,9 @@
         for bit in range(1, top):
             value = ahead_of.get(bit, lambda v: v)(value)
             value = value + across(value, bit)
+            if near and level < near[0][0] and bit == top - 2:
+                step(value)
+                step(value)
         if near and level == near[0][0]:
             open_gather(far, fetched[2], value)
         while level not in table:
@@ -295,7 +298,7 @@
             state = update(corr, state, chip_gather(held))
     gathered = chip_gather(held)
     state = update(corr, state, gathered)
-    ahead_of = {bits[0] - 1: lambda v: tie(v, gathered)}
+    ahead_of = {bits[0]: lambda v: tie(v, state)}
     if near:
         step(value)
     held = solve(0, value, ahead_of)

time: 63.2 us -> 63.8 us (level)
  transfers between devices with their start and end apart: 30 -> 30, of which waited for: 13 -> 12; matrix products, arithmetic and copies ran while one was open for 13% -> 13% of each run, Pallas kernels for 5% -> 5%
where the time goes in v2:
time: 63.8 us; the launch traced here: 63.7 us
  starting transfers between devices  24.7 us (39%)
  waiting for transfers between devices  20.3 us (32%)
  matrix products  9.97 us (16%)
  Pallas kernels  7.84 us (12%)
    ppermute x30, starting transfers between devices, exchange(): return lax.ppermute(value, 'leaf', pairs)  24.7 us
    ppermute x30, waiting for transfers between devices, exchange(): return lax.ppermute(value, 'leaf', pairs)  20.3 us
    pallas_call x2, Pallas kernels, fetch(): pl.pallas_call(body, in_specs=[IN_HBM, IN_HBM, pl.BlockSpec(memory_space=...  3.44 us
    pallas_call x1, Pallas kernels, begin(): pl.pallas_call(body, in_specs=[IN_HBM] * 4, out_specs=[IN_VMEM] * len(sha...  3.05 us
    dot_general x3, matrix products, on_device(): own = jnp.einsum('na,nb->ab', proj, corr, precision=HIGH)  2.98 us
    dot_general x8, matrix products, times_transposed(): return jnp.einsum('kb,ab->ka', left, right, precision=HIGH)  2.74 us
    dot_general x4, matrix products, update(): return state - jnp.einsum('ka,na->kn', held, corr, precision=HIGH)  2.63 us
    dot_general x4, matrix products, project(): return jnp.einsum('kn,nr->kr', state, basis, precision=HIGH)  1.62 us
  transfers between devices with their start and end apart: 30, of which 12 were waited for; matrix products, arithmetic and copies ran while one was open for 13% of the time, Pallas kernels for 5%

profile of v2, /device:TPU:0, one launch (start us, length us, event | category | flops | bytes accessed | tf_op | source)
XLA Modules:
  0.0 63.7 jit_solution(3400770198094792935)
XLA Ops:
  0.0 3.0 %begin.1 = (f32[128,256]{1,0:T(8,128)S(1)}, f32[128,1024]{1,0:T(8,128)S(1)}, f32[1024,256]{1,0:T(8,128)S(1)}, f32[1024,256]{1,0:T(8,128)S(1)}, f32[1024,256]{1,0...) custom-call(f32[1024,128]{1,0:T(8,128)} %x_hbm, ...), custom_call_target="tpu_custom_call" | custom-call | flops 201326592 | bytes 4194304 | tf_op jit(solution)/shard_map/begin/pallas_call | solution.py:90
  3.1 0.5 collective-permute-start
  3.6 1.0 %collective-permute-done = f32[128,256]{1,0:T(8,128)S(1)} collective-permute-done((f32[128,256]{1,0:T(8,128)S(1)}, f32[128,256]{1,0:T(8,128)S(1)}, u32[]{:S(2)}, u32[]{:S(2)}) %collective-permute-start) | collective-permute-done | bytes 131104 | tf_op jit(solution)/shard_map/ppermute | solution.py:17
  4.6 0.4 fusion.1
  5.0 0.7 %convolution_subtract_fusion.3 = f32[128,1024]{1,0:T(8,128)S(1)} fusion(f32[128,1024]{1,0:T(8,128)S(1)} %get-tuple-element.46, f32[128,256]{1,0:T(8,128)S(1)} %fusion.1, f32[1024,256]{1,0:T(8,128)S(1)} %get-tuple-element.50), kind=kOutput, calls=%fused_computation.3 | convolution fusion | flops 201457664 | bytes 2228224 | tf_op jit(solution)/shard_map/ka,na->kn/dot_general | solution.py:263
  5.6 0.4 fusion.87
  6.1 0.4 collective-permute-start.1
  6.5 2.6 %collective-permute-start.9 = (f32[1,64,512]{2,1,0:T(8,128)S(1)}, f32[1,64,512]{2,1,0:T(8,128)S(1)}, u32[]{:S(2)}, u32[]{:S(2)}) collective-permute-start(f32[1,64,512]{2,1,0:T(8,128)S(1)} %bitcast.44), channel_id=1, source_target_pairs={{0,2},{1,3},{2,0},{3,1},{4,6},{5,7},{6,4},{7,5},{8,10},{9,11},{10,... | collective-permute-start | bytes 393224 | tf_op jit(solution)/shard_map/ppermute | solution.py:17
  9.2 0.1 collective-permute-start.3
  9.3 1.0 %fusion.89 = f32[256,256]{1,0:T(8,128)S(1)} fusion(f32[1024,256]{1,0:T(8,128)S(1)} %get-tuple-element.60, f32[1024,256]{1,0:T(8,128)S(1)} %get-tuple-element.57), kind=kOutput, calls=%fused_computation.113 | convolution fusion | flops 402653184 | bytes 2359296 | tf_op jit(solution)/shard_map/na,nb->ab/dot_general | solution.py:295
  10.3 0.4 fusion.88
  10.7 1.2 %collective-permute-start.2 = (f32[64,256]{1,0:T(8,128)S(1)}, f32[64,256]{1,0:T(8,128)S(1)}, u32[]{:S(2)}, u32[]{:S(2)}) collective-permute-start(f32[64,256]{1,0:T(8,128)S(1)} %select_add_fusion._), channel_id=1, source_target_pairs={{0,3},{1,2},{2,1},{3,0},{4,7},{5,6},{6,5},{7,4},{8,11},{9,10},{10,... | collective-permute-start | bytes 196616 | tf_op jit(solution)/shard_map/ppermute | solution.py:17
  11.9 1.6 %fetch.2 = (f32[1024,256]{1,0:T(8,128)S(1)}, f32[1024,256]{1,0:T(8,128)S(1)}) custom-call(f32[5,1024,256]{2,1,0:T(8,128)} %p_hbm.5, f32[5,1024,256]{2,1,0:T(8,128)} %w_hbm.5, f32[64,256]{1,0:T(8,128)S(1)} %select_add_fusion._), custom_call_target="tpu_custom_call" | custom-call | bytes 65536 | tf_op jit(solution)/shard_map/fetch/pallas_call | solution.py:124
  13.5 0.2 collective-permute-start.6
  13.7 0.4 collective-permute-start.5
  14.2 0.4 collective-permute-done.2
  14.6 0.4 fusion.15
  15.0 0.5 collective-permute-start.4
  15.4 0.3 add_subtract_fusion.2
  15.7 1.1 %collective-permute-start.7 = (f32[64,256]{1,0:T(8,128)S(1)}, f32[64,256]{1,0:T(8,128)S(1)}, u32[]{:S(2)}, u32[]{:S(2)}) collective-permute-start(f32[64,256]{1,0:T(8,128)S(1)} %add_subtract_fusion.2), channel_id=1, source_target_pairs={{0,3},{1,2},{2,1},{3,0},{4,7},{5,6},{6,5},{7,4},{8,11},{9,10},{10,... | collective-permute-start | bytes 196616 | tf_op jit(solution)/shard_map/ppermute | solution.py:17
  16.8 1.0 %fusion.91 = f32[256,256]{1,0:T(8,128)S(1)} fusion(f32[1024,256]{1,0:T(8,128)S(1)} %get-tuple-element.68, f32[1024,256]{1,0:T(8,128)S(1)} %get-tuple-element.65), kind=kOutput, calls=%fused_computation.115 | convolution fusion | flops 402653184 | bytes 2359296 | tf_op jit(solution)/shard_map/na,nb->ab/dot_general | solution.py:295
  17.8 0.4 collective-permute-start.13
  18.2 0.3 collective-permute-start.10
  18.5 0.7 %convolution_subtract_fusion.2 = f32[128,1024]{1,0:T(8,128)S(1)} fusion(f32[128,1024]{1,0:T(8,128)S(1)} %convolution_subtract_fusion.3, f32[1024,256]{1,0:T(8,128)S(1)} %get-tuple-element.57, f32[64,256]{1,0:T(8,128)S(1)} %collective-permute-done.4, f32[64,256]{1,0:T(8,128)S(1)} %fusion.15, pred[]{:T(512)S(6)} %eq.18), kind=kOutput, calls=%fused_computation.2 | convolution fusion | flops 201555968 | bytes 2228225 | tf_op jit(solution)/shard_map/ka,na->kn/dot_general | solution.py:263
  19.1 0.4 fusion.90
  19.5 0.3 collective-permute-done.7
  19.9 1.3 %collective-permute-start.8 = (f32[64,256]{1,0:T(8,128)S(1)}, f32[64,256]{1,0:T(8,128)S(1)}, u32[]{:S(2)}, u32[]{:S(2)}) collective-permute-start(f32[64,256]{1,0:T(8,128)S(1)} %add.42._), channel_id=1, source_target_pairs={{0,5},{1,4},{2,7},{3,6},{4,1},{5,0},{6,3},{7,2},{8,13},{9,12},{10,... | collective-permute-start | bytes 196616 | tf_op jit(solution)/shard_map/ppermute | solution.py:17
  21.2 1.9 %fetch.3 = (f32[1024,256]{1,0:T(8,128)S(1)}, f32[1024,256]{1,0:T(8,128)S(1)}, f32[1024,256]{1,0:T(8,128)S(1)}) custom-call(f32[5,1024,256]{2,1,0:T(8,128)} %p_hbm.5, f32[5,1024,256]{2,1,0:T(8,128)} %w_hbm.5, f32[64,256]{1,0:T(8,128)S(1)} %add.42._), custom_call_target="tpu_custom_call" | custom-call | bytes 65536 | tf_op jit(solution)/shard_map/fetch/pallas_call | solution.py:124
  23.1 0.5 collective-permute-start.12
  23.6 1.2 %collective-permute-start.17 = (f32[1,48,512]{2,1,0:T(8,128)S(1)}, f32[1,48,512]{2,1,0:T(8,128)S(1)}, u32[]{:S(2)}, u32[]{:S(2)}) collective-permute-start(f32[1,48,512]{2,1,0:T(8,128)S(1)} %bitcast.46), channel_id=1, source_target_pairs={{0,2},{1,3},{2,0},{3,1},{4,6},{5,7},{6,4},{7,5},{8,10},{9,11},{10,... | collective-permute-start | bytes 294920 | tf_op jit(solution)/shard_map/ppermute | solution.py:17
  24.8 0.4 fusion.28
  25.3 0.3 add_subtract_fusion.1
  25.6 1.0 %collective-permute-start.14 = (f32[64,256]{1,0:T(8,128)S(1)}, f32[64,256]{1,0:T(8,128)S(1)}, u32[]{:S(2)}, u32[]{:S(2)}) collective-permute-start(f32[64,256]{1,0:T(8,128)S(1)} %add_subtract_fusion.1), channel_id=1, source_target_pairs={{0,3},{1,2},{2,1},{3,0},{4,7},{5,6},{6,5},{7,4},{8,11},{9,10},{10,... | collective-permute-start | bytes 196616 | tf_op jit(solution)/shard_map/ppermute | solution.py:17
  26.6 1.0 %fusion.93 = f32[256,256]{1,0:T(8,128)S(1)} fusion(f32[1024,256]{1,0:T(8,128)S(1)} %get-tuple-element.80, f32[1024,256]{1,0:T(8,128)S(1)} %get-tuple-element.76), kind=kOutput, calls=%fused_computation.117 | convolution fusion | flops 402653184 | bytes 2359296 | tf_op jit(solution)/shard_map/na,nb->ab/dot_general | solution.py:295
  27.6 0.1 collective-permute-start.22
  27.7 0.7 %collective-permute-done.17 = f32[1,48,512]{2,1,0:T(8,128)S(1)} collective-permute-done((f32[1,48,512]{2,1,0:T(8,128)S(1)}, f32[1,48,512]{2,1,0:T(8,128)S(1)}, u32[]{:S(2)}, u32[]{:S(2)}) %collective-permute-start.17) | collective-permute-done | bytes 98336 | tf_op jit(solution)/shard_map/ppermute | solution.py:17
  28.4 0.6 collective-permute-start.18
  29.0 0.5 collective-permute-done.14
  29.4 1.0 %collective-permute-start.15 = (f32[64,256]{1,0:T(8,128)S(1)}, f32[64,256]{1,0:T(8,128)S(1)}, u32[]{:S(2)}, u32[]{:S(2)}) collective-permute-start(f32[64,256]{1,0:T(8,128)S(1)} %add.45), channel_id=1, source_target_pairs={{0,5},{1,4},{2,7},{3,6},{4,1},{5,0},{6,3},{7,2},{8,13},{9,12},{10,... | collective-permute-start | bytes 196616 | tf_op jit(solution)/shard_map/ppermute | solution.py:17
  30.4 0.7 %convolution_subtract_fusion.1 = f32[128,1024]{1,0:T(8,128)S(1)} fusion(f32[128,1024]{1,0:T(8,128)S(1)} %convolution_subtract_fusion.2, f32[1024,256]{1,0:T(8,128)S(1)} %get-tuple-element.65, f32[64,256]{1,0:T(8,128)S(1)} %collective-permute-done.11, f32[64,256]{1,0:T(8,128)S(1)} %fusion.28, pred[]{:T(512)S(6)} %eq.18), kind=kOutput, calls=%fused_computation.1 | convolution fusion | flops 201555968 | bytes 2228225 | tf_op jit(solution)/shard_map/ka,na->kn/dot_general | solution.py:263
  31.1 4.7 %collective-permute-done.18 = f32[2,48,512]{2,1,0:T(8,128)S(1)} collective-permute-done((f32[2,48,512]{2,1,0:T(8,128)S(1)}, f32[2,48,512]{2,1,0:T(8,128)S(1)}, u32[]{:S(2)}, u32[]{:S(2)}) %collective-permute-start.18) | collective-permute-done | bytes 196640 | tf_op jit(solution)/shard_map/ppermute | solution.py:17
  35.8 0.1 collective-permute-start.19
  35.9 0.4 fusion.92
  36.4 0.6 collective-permute-start.21
  36.9 1.3 %collective-permute-start.16 = (f32[64,256]{1,0:T(8,128)S(1)}, f32[64,256]{1,0:T(8,128)S(1)}, u32[]{:S(2)}, u32[]{:S(2)}) collective-permute-start(f32[64,256]{1,0:T(8,128)S(1)} %add.46), channel_id=1, source_target_pairs={{0,9},{1,8},{2,11},{3,10},{4,13},{5,12},{6,15},{7,14},{8,1},{9,0},... | collective-permute-start | bytes 196616 | tf_op jit(solution)/shard_map/ppermute | solution.py:17
  38.3 2.9 %collective-permute-done.16 = f32[64,256]{1,0:T(8,128)S(1)} collective-permute-done((f32[64,256]{1,0:T(8,128)S(1)}, f32[64,256]{1,0:T(8,128)S(1)}, u32[]{:S(2)}, u32[]{:S(2)}) %collective-permute-start.16) | collective-permute-done | bytes 65568 | tf_op jit(solution)/shard_map/ppermute | solution.py:17
  41.2 0.4 fusion.41
  41.6 0.3 add_subtract_fusion
  41.9 0.9 %collective-permute-start.23 = (f32[64,256]{1,0:T(8,128)S(1)}, f32[64,256]{1,0:T(8,128)S(1)}, u32[]{:S(2)}, u32[]{:S(2)}) collective-permute-start(f32[64,256]{1,0:T(8,128)S(1)} %add_subtract_fusion), channel_id=1, source_target_pairs={{0,3},{1,2},{2,1},{3,0},{4,7},{5,6},{6,5},{7,4},{8,11},{9,10},{10,... | collective-permute-start | bytes 196616 | tf_op jit(solution)/shard_map/ppermute | solution.py:17
  42.8 1.6 %collective-permute-start.27 = (f32[4,16,512]{2,1,0:T(8,128)S(1)}, f32[4,16,512]{2,1,0:T(8,128)S(1)}, u32[]{:S(2)}, u32[]{:S(2)}) collective-permute-start(f32[4,16,512]{2,1,0:T(8,128)S(1)} %slice.57), channel_id=1, source_target_pairs={{0,8},{1,9},{2,10},{3,11},{4,12},{5,13},{6,14},{7,15},{8,0},{9,1},... | collective-permute-start | bytes 393224 | tf_op jit(solution)/shard_map/ppermute | solution.py:17
  44.5 1.6 %collective-permute-done.23 = f32[64,256]{1,0:T(8,128)S(1)} collective-permute-done((f32[64,256]{1,0:T(8,128)S(1)}, f32[64,256]{1,0:T(8,128)S(1)}, u32[]{:S(2)}, u32[]{:S(2)}) %collective-permute-start.23) | collective-permute-done | bytes 65568 | tf_op jit(solution)/shard_map/ppermute | solution.py:17
  46.0 1.0 %collective-permute-start.24 = (f32[64,256]{1,0:T(8,128)S(1)}, f32[64,256]{1,0:T(8,128)S(1)}, u32[]{:S(2)}, u32[]{:S(2)}) collective-permute-start(f32[64,256]{1,0:T(8,128)S(1)} %add.49), channel_id=1, source_target_pairs={{0,5},{1,4},{2,7},{3,6},{4,1},{5,0},{6,3},{7,2},{8,13},{9,12},{10,... | collective-permute-start | bytes 196616 | tf_op jit(solution)/shard_map/ppermute | solution.py:17
  47.0 0.1 collective-permute-start.20
  47.1 3.1 %collective-permute-done.24 = f32[64,256]{1,0:T(8,128)S(1)} collective-permute-done((f32[64,256]{1,0:T(8,128)S(1)}, f32[64,256]{1,0:T(8,128)S(1)}, u32[]{:S(2)}, u32[]{:S(2)}) %collective-permute-start.24) | collective-permute-done | bytes 65568 | tf_op jit(solution)/shard_map/ppermute | solution.py:17
  50.2 1.4 %collective-permute-start.25 = (f32[64,256]{1,0:T(8,128)S(1)}, f32[64,256]{1,0:T(8,128)S(1)}, u32[]{:S(2)}, u32[]{:S(2)}) collective-permute-start(f32[64,256]{1,0:T(8,128)S(1)} %add.50), channel_id=1, source_target_pairs={{0,9},{1,8},{2,11},{3,10},{4,13},{5,12},{6,15},{7,14},{8,1},{9,0},... | collective-permute-start | bytes 196616 | tf_op jit(solution)/shard_map/ppermute | solution.py:17
  51.6 0.5 collective-permute-start.28
  52.1 0.7 %convolution_subtract_fusion.x_ref = f32[128,1024]{1,0:T(8,128)S(1)} fusion(f32[128,1024]{1,0:T(8,128)S(1)} %convolution_subtract_fusion.1, f32[1024,256]{1,0:T(8,128)S(1)} %get-tuple-element.76, f32[64,256]{1,0:T(8,128)S(1)} %collective-permute-done.20, f32[64,256]{1,0:T(8,128)S(1)} %fusion.41, pred[]{:T(512)S(6)} %eq.18), kind=kOutput, calls=%fused_computation | convolution fusion | flops 201555968 | bytes 2228225 | tf_op jit(solution)/shard_map/ka,na->kn/dot_general | solution.py:263
  52.7 1.6 %collective-permute-done.25 = f32[64,256]{1,0:T(8,128)S(1)} collective-permute-done((f32[64,256]{1,0:T(8,128)S(1)}, f32[64,256]{1,0:T(8,128)S(1)}, u32[]{:S(2)}, u32[]{:S(2)}) %collective-permute-start.25) | collective-permute-done | bytes 65568 | tf_op jit(solution)/shard_map/ppermute | solution.py:17
  54.4 2.4 %collective-permute-start.26 = (f32[64,256]{1,0:T(8,128)S(1)}, f32[64,256]{1,0:T(8,128)S(1)}, u32[]{:S(2)}, u32[]{:S(2)}) collective-permute-start(f32[64,256]{1,0:T(8,128)S(1)} %add.51), channel_id=1, source_target_pairs={{0,17},{1,16},{2,19},{3,18},{4,21},{5,20},{6,23},{7,22},{8,25},{9,... | collective-permute-start | bytes 196616 | tf_op jit(solution)/shard_map/ppermute | solution.py:17
  56.9 2.6 %collective-permute-done.26 = f32[64,256]{1,0:T(8,128)S(1)} collective-permute-done((f32[64,256]{1,0:T(8,128)S(1)}, f32[64,256]{1,0:T(8,128)S(1)}, u32[]{:S(2)}, u32[]{:S(2)}) %collective-permute-start.26) | collective-permute-done | bytes 65568 | tf_op jit(solution)/shard_map/ppermute | solution.py:17
  59.4 0.4 fusion.54
  59.8 1.6 %collective-permute-start.29 = (f32[64,256]{1,0:T(8,128)S(1)}, f32[64,256]{1,0:T(8,128)S(1)}, u32[]{:S(2)}, u32[]{:S(2)}) collective-permute-start(f32[64,256]{1,0:T(8,128)S(1)} %fusion.54), channel_id=1, source_target_pairs={{0,1},{1,0},{2,3},{3,2},{4,5},{5,4},{6,7},{7,6},{8,9},{9,8},{10,11... | collective-permute-start | bytes 196616 | tf_op jit(solution)/shard_map/ppermute | solution.py:17
  61.4 0.9 %collective-permute-done.29 = f32[64,256]{1,0:T(8,128)S(1)} collective-permute-done((f32[64,256]{1,0:T(8,128)S(1)}, f32[64,256]{1,0:T(8,128)S(1)}, u32[]{:S(2)}, u32[]{:S(2)}) %collective-permute-start.29) | collective-permute-done | bytes 65568 | tf_op jit(solution)/shard_map/ppermute | solution.py:17
  62.3 1.4 %finish.1 = f32[1024,128]{1,0:T(8,128)} custom-call(f32[128,1024]{1,0:T(8,128)S(1)} %convolution_subtract_fusion.x_ref, f32[1024,256]{1,0:T(8,128)S(1)} %get-tuple-element.77.w_ref, f32[128,256]{1,0:T(8,128)S(1)} %maximum_select_fusion.19.t_ref), custom_call_target="tpu_custom_call" | custom-call | flops 201326592 | bytes 2097152 | tf_op jit(solution)/shard_map/finish/pallas_call | solution.py:144
  (44 shorter events, 0.6 us)
Async XLA Ops:
  3.1 1.5 %collective-permute-start = (f32[128,256]{1,0:T(8,128)S(1)}, f32[128,256]{1,0:T(8,128)S(1)}, u32[]{:S(2)}, u32[]{:S(2)}) collective-permute-start(f32[128,256]{1,0:T(8,128)S(1)} %get-tuple-element.48), channel_id=1, source_target_pairs={{0,1},{1,0},{2,3},{3,2},{4,5},{5,4},{6,7},{7,6},{8,9},{9,8},{10,11... | collective-permute-start | bytes 393224 | tf_op jit(solution)/shard_map/ppermute | solution.py:17
  6.1 3.1 %collective-permute-start.1 = (f32[64,256]{1,0:T(8,128)S(1)}, f32[64,256]{1,0:T(8,128)S(1)}, u32[]{:S(2)}, u32[]{:S(2)}) collective-permute-start(f32[64,256]{1,0:T(8,128)S(1)} %slice_select_fusion.3), channel_id=1, source_target_pairs={{0,1},{1,0},{2,3},{3,2},{4,5},{5,4},{6,7},{7,6},{8,9},{9,8},{10,11... | collective-permute-start | bytes 196616 | tf_op jit(solution)/shard_map/ppermute | solution.py:17
  6.5 11.7 %collective-permute-start.9 = (f32[1,64,512]{2,1,0:T(8,128)S(1)}, f32[1,64,512]{2,1,0:T(8,128)S(1)}, u32[]{:S(2)}, u32[]{:S(2)}) collective-permute-start(f32[1,64,512]{2,1,0:T(8,128)S(1)} %bitcast.44), channel_id=1, source_target_pairs={{0,2},{1,3},{2,0},{3,1},{4,6},{5,7},{6,4},{7,5},{8,10},{9,11},{10,... | collective-permute-start | bytes 393224 | tf_op jit(solution)/shard_map/ppermute | solution.py:17
  9.2 5.0 %collective-permute-start.3 = (f32[1,128,512]{2,1,0:T(8,128)S(1)}, f32[1,128,512]{2,1,0:T(8,128)S(1)}, u32[]{:S(2)}, u32[]{:S(2)}) collective-permute-start(f32[1,128,512]{2,1,0:T(8,128)S(1)} %bitcast.42), channel_id=1, source_target_pairs={{0,1},{1,0},{2,3},{3,2},{4,5},{5,4},{6,7},{7,6},{8,9},{9,8},{10,11... | collective-permute-start | bytes 786440 | tf_op jit(solution)/shard_map/ppermute | solution.py:17
  10.7 3.9 %collective-permute-start.2 = (f32[64,256]{1,0:T(8,128)S(1)}, f32[64,256]{1,0:T(8,128)S(1)}, u32[]{:S(2)}, u32[]{:S(2)}) collective-permute-start(f32[64,256]{1,0:T(8,128)S(1)} %select_add_fusion._), channel_id=1, source_target_pairs={{0,3},{1,2},{2,1},{3,0},{4,7},{5,6},{6,5},{7,4},{8,11},{9,10},{10,... | collective-permute-start | bytes 196616 | tf_op jit(solution)/shard_map/ppermute | solution.py:17
  13.5 2.0 %collective-permute-start.6 = (f32[256,256]{1,0:T(8,128)S(1)}, f32[256,256]{1,0:T(8,128)S(1)}, u32[]{:S(2)}, u32[]{:S(2)}) collective-permute-start(f32[256,256]{1,0:T(8,128)S(1)} %fusion.89), channel_id=1, source_target_pairs={{0,1},{1,0},{2,3},{3,2},{4,5},{5,4},{6,7},{7,6},{8,9},{9,8},{10,11... | collective-permute-start | bytes 786440 | tf_op jit(solution)/shard_map/ppermute | solution.py:17
  13.7 1.7 %collective-permute-start.5 = (f32[64,256]{1,0:T(8,128)S(1)}, f32[64,256]{1,0:T(8,128)S(1)}, u32[]{:S(2)}, u32[]{:S(2)}) collective-permute-start(f32[64,256]{1,0:T(8,128)S(1)} %slice_select_fusion.2), channel_id=1, source_target_pairs={{0,1},{1,0},{2,3},{3,2},{4,5},{5,4},{6,7},{7,6},{8,9},{9,8},{10,11... | collective-permute-start | bytes 196616 | tf_op jit(solution)/shard_map/ppermute | solution.py:17
  15.0 3.5 %collective-permute-start.4 = (f32[64,256]{1,0:T(8,128)S(1)}, f32[64,256]{1,0:T(8,128)S(1)}, u32[]{:S(2)}, u32[]{:S(2)}) collective-permute-start(f32[64,256]{1,0:T(8,128)S(1)} %fusion.15), channel_id=1, source_target_pairs={{0,1},{1,0},{2,3},{3,2},{4,5},{5,4},{6,7},{7,6},{8,9},{9,8},{10,11... | collective-permute-start | bytes 196616 | tf_op jit(solution)/shard_map/ppermute | solution.py:17
  15.7 4.2 %collective-permute-start.7 = (f32[64,256]{1,0:T(8,128)S(1)}, f32[64,256]{1,0:T(8,128)S(1)}, u32[]{:S(2)}, u32[]{:S(2)}) collective-permute-start(f32[64,256]{1,0:T(8,128)S(1)} %add_subtract_fusion.2), channel_id=1, source_target_pairs={{0,3},{1,2},{2,1},{3,0},{4,7},{5,6},{6,5},{7,4},{8,11},{9,10},{10,... | collective-permute-start | bytes 196616 | tf_op jit(solution)/shard_map/ppermute | solution.py:17
  17.8 7.5 %collective-permute-start.13 = (f32[256,256]{1,0:T(8,128)S(1)}, f32[256,256]{1,0:T(8,128)S(1)}, u32[]{:S(2)}, u32[]{:S(2)}) collective-permute-start(f32[256,256]{1,0:T(8,128)S(1)} %fusion.91), channel_id=1, source_target_pairs={{0,1},{1,0},{2,3},{3,2},{4,5},{5,4},{6,7},{7,6},{8,9},{9,8},{10,11... | collective-permute-start | bytes 786440 | tf_op jit(solution)/shard_map/ppermute | solution.py:17
  18.2 6.6 %collective-permute-start.10 = (f32[2,64,512]{2,1,0:T(8,128)S(1)}, f32[2,64,512]{2,1,0:T(8,128)S(1)}, u32[]{:S(2)}, u32[]{:S(2)}) collective-permute-start(f32[2,64,512]{2,1,0:T(8,128)S(1)} %maximum_select_fusion.6), channel_id=1, source_target_pairs={{0,1},{1,0},{2,3},{3,2},{4,5},{5,4},{6,7},{7,6},{8,9},{9,8},{10,11... | collective-permute-start | bytes 786440 | tf_op jit(solution)/shard_map/ppermute | solution.py:17
  19.9 4.9 %collective-permute-start.8 = (f32[64,256]{1,0:T(8,128)S(1)}, f32[64,256]{1,0:T(8,128)S(1)}, u32[]{:S(2)}, u32[]{:S(2)}) collective-permute-start(f32[64,256]{1,0:T(8,128)S(1)} %add.42._), channel_id=1, source_target_pairs={{0,5},{1,4},{2,7},{3,6},{4,1},{5,0},{6,3},{7,2},{8,13},{9,12},{10,... | collective-permute-start | bytes 196616 | tf_op jit(solution)/shard_map/ppermute | solution.py:17
  23.1 2.2 %collective-permute-start.12 = (f32[64,256]{1,0:T(8,128)S(1)}, f32[64,256]{1,0:T(8,128)S(1)}, u32[]{:S(2)}, u32[]{:S(2)}) collective-permute-start(f32[64,256]{1,0:T(8,128)S(1)} %slice_select_fusion.1), channel_id=1, source_target_pairs={{0,1},{1,0},{2,3},{3,2},{4,5},{5,4},{6,7},{7,6},{8,9},{9,8},{10,11... | collective-permute-start | bytes 196616 | tf_op jit(solution)/shard_map/ppermute | solution.py:17
  23.6 4.8 %collective-permute-start.17 = (f32[1,48,512]{2,1,0:T(8,128)S(1)}, f32[1,48,512]{2,1,0:T(8,128)S(1)}, u32[]{:S(2)}, u32[]{:S(2)}) collective-permute-start(f32[1,48,512]{2,1,0:T(8,128)S(1)} %bitcast.46), channel_id=1, source_target_pairs={{0,2},{1,3},{2,0},{3,1},{4,6},{5,7},{6,4},{7,5},{8,10},{9,11},{10,... | collective-permute-start | bytes 294920 | tf_op jit(solution)/shard_map/ppermute | solution.py:17
  25.2 5.2 %collective-permute-start.11 = (f32[64,256]{1,0:T(8,128)S(1)}, f32[64,256]{1,0:T(8,128)S(1)}, u32[]{:S(2)}, u32[]{:S(2)}) collective-permute-start(f32[64,256]{1,0:T(8,128)S(1)} %fusion.28), channel_id=1, source_target_pairs={{0,1},{1,0},{2,3},{3,2},{4,5},{5,4},{6,7},{7,6},{8,9},{9,8},{10,11... | collective-permute-start | bytes 196616 | tf_op jit(solution)/shard_map/ppermute | solution.py:17
  25.6 3.8 %collective-permute-start.14 = (f32[64,256]{1,0:T(8,128)S(1)}, f32[64,256]{1,0:T(8,128)S(1)}, u32[]{:S(2)}, u32[]{:S(2)}) collective-permute-start(f32[64,256]{1,0:T(8,128)S(1)} %add_subtract_fusion.1), channel_id=1, source_target_pairs={{0,3},{1,2},{2,1},{3,0},{4,7},{5,6},{6,5},{7,4},{8,11},{9,10},{10,... | collective-permute-start | bytes 196616 | tf_op jit(solution)/shard_map/ppermute | solution.py:17
  27.6 14.0 %collective-permute-start.22 = (f32[256,256]{1,0:T(8,128)S(1)}, f32[256,256]{1,0:T(8,128)S(1)}, u32[]{:S(2)}, u32[]{:S(2)}) collective-permute-start(f32[256,256]{1,0:T(8,128)S(1)} %fusion.93), channel_id=1, source_target_pairs={{0,1},{1,0},{2,3},{3,2},{4,5},{5,4},{6,7},{7,6},{8,9},{9,8},{10,11... | collective-permute-start | bytes 786440 | tf_op jit(solution)/shard_map/ppermute | solution.py:17
  28.4 7.4 %collective-permute-start.18 = (f32[2,48,512]{2,1,0:T(8,128)S(1)}, f32[2,48,512]{2,1,0:T(8,128)S(1)}, u32[]{:S(2)}, u32[]{:S(2)}) collective-permute-start(f32[2,48,512]{2,1,0:T(8,128)S(1)} %maximum_select_fusion.8), channel_id=1, source_target_pairs={{0,4},{1,5},{2,6},{3,7},{4,0},{5,1},{6,2},{7,3},{8,12},{9,13},{10,... | collective-permute-start | bytes 589832 | tf_op jit(solution)/shard_map/ppermute | solution.py:17
  29.4 7.5 %collective-permute-start.15 = (f32[64,256]{1,0:T(8,128)S(1)}, f32[64,256]{1,0:T(8,128)S(1)}, u32[]{:S(2)}, u32[]{:S(2)}) collective-permute-start(f32[64,256]{1,0:T(8,128)S(1)} %add.45), channel_id=1, source_target_pairs={{0,5},{1,4},{2,7},{3,6},{4,1},{5,0},{6,3},{7,2},{8,13},{9,12},{10,... | collective-permute-start | bytes 196616 | tf_op jit(solution)/shard_map/ppermute | solution.py:17
  35.8 2.4 %collective-permute-start.19 = (f32[4,32,512]{2,1,0:T(8,128)S(1)}, f32[4,32,512]{2,1,0:T(8,128)S(1)}, u32[]{:S(2)}, u32[]{:S(2)}) collective-permute-start(f32[4,32,512]{2,1,0:T(8,128)S(1)} %slice.54), channel_id=1, source_target_pairs={{0,1},{1,0},{2,3},{3,2},{4,5},{5,4},{6,7},{7,6},{8,9},{9,8},{10,11... | collective-permute-start | bytes 786440 | tf_op jit(solution)/shard_map/ppermute | solution.py:17
  36.4 5.2 %collective-permute-start.21 = (f32[64,256]{1,0:T(8,128)S(1)}, f32[64,256]{1,0:T(8,128)S(1)}, u32[]{:S(2)}, u32[]{:S(2)}) collective-permute-start(f32[64,256]{1,0:T(8,128)S(1)} %slice_select_fusion), channel_id=1, source_target_pairs={{0,1},{1,0},{2,3},{3,2},{4,5},{5,4},{6,7},{7,6},{8,9},{9,8},{10,11... | collective-permute-start | bytes 196616 | tf_op jit(solution)/shard_map/ppermute | solution.py:17
  36.9 4.2 %collective-permute-start.16 = (f32[64,256]{1,0:T(8,128)S(1)}, f32[64,256]{1,0:T(8,128)S(1)}, u32[]{:S(2)}, u32[]{:S(2)}) collective-permute-start(f32[64,256]{1,0:T(8,128)S(1)} %add.46), channel_id=1, source_target_pairs={{0,9},{1,8},{2,11},{3,10},{4,13},{5,12},{6,15},{7,14},{8,1},{9,0},... | collective-permute-start | bytes 196616 | tf_op jit(solution)/shard_map/ppermute | solution.py:17
  41.9 4.2 %collective-permute-start.23 = (f32[64,256]{1,0:T(8,128)S(1)}, f32[64,256]{1,0:T(8,128)S(1)}, u32[]{:S(2)}, u32[]{:S(2)}) collective-permute-start(f32[64,256]{1,0:T(8,128)S(1)} %add_subtract_fusion), channel_id=1, source_target_pairs={{0,3},{1,2},{2,1},{3,0},{4,7},{5,6},{6,5},{7,4},{8,11},{9,10},{10,... | collective-permute-start | bytes 196616 | tf_op jit(solution)/shard_map/ppermute | solution.py:17
  42.8 8.8 %collective-permute-start.27 = (f32[4,16,512]{2,1,0:T(8,128)S(1)}, f32[4,16,512]{2,1,0:T(8,128)S(1)}, u32[]{:S(2)}, u32[]{:S(2)}) collective-permute-start(f32[4,16,512]{2,1,0:T(8,128)S(1)} %slice.57), channel_id=1, source_target_pairs={{0,8},{1,9},{2,10},{3,11},{4,12},{5,13},{6,14},{7,15},{8,0},{9,1},... | collective-permute-start | bytes 393224 | tf_op jit(solution)/shard_map/ppermute | solution.py:17
  46.0 4.2 %collective-permute-start.24 = (f32[64,256]{1,0:T(8,128)S(1)}, f32[64,256]{1,0:T(8,128)S(1)}, u32[]{:S(2)}, u32[]{:S(2)}) collective-permute-start(f32[64,256]{1,0:T(8,128)S(1)} %add.49), channel_id=1, source_target_pairs={{0,5},{1,4},{2,7},{3,6},{4,1},{5,0},{6,3},{7,2},{8,13},{9,12},{10,... | collective-permute-start | bytes 196616 | tf_op jit(solution)/shard_map/ppermute | solution.py:17
  47.0 5.0 %collective-permute-start.20 = (f32[64,256]{1,0:T(8,128)S(1)}, f32[64,256]{1,0:T(8,128)S(1)}, u32[]{:S(2)}, u32[]{:S(2)}) collective-permute-start(f32[64,256]{1,0:T(8,128)S(1)} %fusion.41), channel_id=1, source_target_pairs={{0,1},{1,0},{2,3},{3,2},{4,5},{5,4},{6,7},{7,6},{8,9},{9,8},{10,11... | collective-permute-start | bytes 196616 | tf_op jit(solution)/shard_map/ppermute | solution.py:17
  50.2 4.2 %collective-permute-start.25 = (f32[64,256]{1,0:T(8,128)S(1)}, f32[64,256]{1,0:T(8,128)S(1)}, u32[]{:S(2)}, u32[]{:S(2)}) collective-permute-start(f32[64,256]{1,0:T(8,128)S(1)} %add.50), channel_id=1, source_target_pairs={{0,9},{1,8},{2,11},{3,10},{4,13},{5,12},{6,15},{7,14},{8,1},{9,0},... | collective-permute-start | bytes 196616 | tf_op jit(solution)/shard_map/ppermute | solution.py:17
  51.6 5.2 %collective-permute-start.28 = (f32[8,16,512]{2,1,0:T(8,128)S(1)}, f32[8,16,512]{2,1,0:T(8,128)S(1)}, u32[]{:S(2)}, u32[]{:S(2)}) collective-permute-start(f32[8,16,512]{2,1,0:T(8,128)S(1)} %maximum_select_fusion.7), channel_id=1, source_target_pairs={{0,1},{1,0},{2,3},{3,2},{4,5},{5,4},{6,7},{7,6},{8,9},{9,8},{10,11... | collective-permute-start | bytes 786440 | tf_op jit(solution)/shard_map/ppermute | solution.py:17
  54.4 5.1 %collective-permute-start.26 = (f32[64,256]{1,0:T(8,128)S(1)}, f32[64,256]{1,0:T(8,128)S(1)}, u32[]{:S(2)}, u32[]{:S(2)}) collective-permute-start(f32[64,256]{1,0:T(8,128)S(1)} %add.51), channel_id=1, source_target_pairs={{0,17},{1,16},{2,19},{3,18},{4,21},{5,20},{6,23},{7,22},{8,25},{9,... | collective-permute-start | bytes 196616 | tf_op jit(solution)/shard_map/ppermute | solution.py:17
  59.8 2.5 %collective-permute-start.29 = (f32[64,256]{1,0:T(8,128)S(1)}, f32[64,256]{1,0:T(8,128)S(1)}, u32[]{:S(2)}, u32[]{:S(2)}) collective-permute-start(f32[64,256]{1,0:T(8,128)S(1)} %fusion.54), channel_id=1, source_target_pairs={{0,1},{1,0},{2,3},{3,2},{4,5},{5,4},{6,7},{7,6},{8,9},{9,8},{10,11... | collective-permute-start | bytes 196616 | tf_op jit(solution)/shard_map/ppermute | solution.py:17

commit v3 on v2

--- a/solution.py
+++ b/solution.py
@@ -245,7 +245,7 @@
         for bit in range(1, top):
             value = ahead_of.get(bit, lambda v: v)(value)
             value = value + across(value, bit)
-            if near and level < near[0][0] and bit == top - 2:
+            if near and level == 0 and bit == top - 2:
                 step(value)
                 step(value)
         if near and level == near[0][0]:

time: 63.8 us -> 63.2 us (level)
  waiting for transfers between devices: 20.3 us -> 18.8 us
  starting transfers between devices: 24.7 us -> 25.6 us
    ppermute x30, waiting for transfers between devices: 20.3 us -> 18.8 us  [exchange(): return lax.ppermute(value, 'leaf', pairs)]
    ppermute x30, starting transfers between devices: 24.7 us -> 25.6 us  [exchange(): return lax.ppermute(value, 'leaf', pairs)]
  transfers between devices with their start and end apart: 30 -> 30, of which waited for: 12 -> 13; matrix products, arithmetic and copies ran while one was open for 13% -> 13% of each run, Pallas kernels for 5% -> 5%
where the time goes in v3:
time: 63.2 us; the launch traced here: 63.1 us
  starting transfers between devices  25.6 us (41%)
  waiting for transfers between devices  18.8 us (30%)
  matrix products  9.97 us (16%)
  Pallas kernels  7.84 us (12%)
    ppermute x30, starting transfers between devices, exchange(): return lax.ppermute(value, 'leaf', pairs)  25.6 us
    ppermute x30, waiting for transfers between devices, exchange(): return lax.ppermute(value, 'leaf', pairs)  18.8 us
    pallas_call x2, Pallas kernels, fetch(): pl.pallas_call(body, in_specs=[IN_HBM, IN_HBM, pl.BlockSpec(memory_space=...  3.44 us
    pallas_call x1, Pallas kernels, begin(): pl.pallas_call(body, in_specs=[IN_HBM] * 4, out_specs=[IN_VMEM] * len(sha...  3.05 us
    dot_general x3, matrix products, on_device(): own = jnp.einsum('na,nb->ab', proj, corr, precision=HIGH)  2.98 us
    dot_general x8, matrix products, times_transposed(): return jnp.einsum('kb,ab->ka', left, right, precision=HIGH)  2.74 us
    dot_general x4, matrix products, update(): return state - jnp.einsum('ka,na->kn', held, corr, precision=HIGH)  2.63 us
    dot_general x4, matrix products, project(): return jnp.einsum('kn,nr->kr', state, basis, precision=HIGH)  1.62 us
  transfers between devices with their start and end apart: 30, of which 13 were waited for; matrix products, arithmetic and copies ran while one was open for 13% of the time, Pallas kernels for 5%

profile of v3, /device:TPU:0, one launch (start us, length us, event | category | flops | bytes accessed | tf_op | source)
XLA Modules:
  0.0 63.1 jit_solution(7724004447957440511)
XLA Ops:
  0.0 3.0 %begin.1 = (f32[128,256]{1,0:T(8,128)S(1)}, f32[128,1024]{1,0:T(8,128)S(1)}, f32[1024,256]{1,0:T(8,128)S(1)}, f32[1024,256]{1,0:T(8,128)S(1)}, f32[1024,256]{1,0...) custom-call(f32[1024,128]{1,0:T(8,128)} %x_hbm, ...), custom_call_target="tpu_custom_call" | custom-call | flops 201326592 | bytes 4194304 | tf_op jit(solution)/shard_map/begin/pallas_call | solution.py:90
  3.1 0.5 collective-permute-start
  3.6 1.0 %collective-permute-done = f32[128,256]{1,0:T(8,128)S(1)} collective-permute-done((f32[128,256]{1,0:T(8,128)S(1)}, f32[128,256]{1,0:T(8,128)S(1)}, u32[]{:S(2)}, u32[]{:S(2)}) %collective-permute-start) | collective-permute-done | bytes 131104 | tf_op jit(solution)/shard_map/ppermute | solution.py:17
  4.6 0.4 fusion.1
  5.0 0.7 %convolution_subtract_fusion.3 = f32[128,1024]{1,0:T(8,128)S(1)} fusion(f32[128,1024]{1,0:T(8,128)S(1)} %get-tuple-element.46, f32[128,256]{1,0:T(8,128)S(1)} %fusion.1, f32[1024,256]{1,0:T(8,128)S(1)} %get-tuple-element.50), kind=kOutput, calls=%fused_computation.3 | convolution fusion | flops 201457664 | bytes 2228224 | tf_op jit(solution)/shard_map/ka,na->kn/dot_general | solution.py:263
  5.6 0.4 fusion.87
  6.1 0.4 collective-permute-start.1
  6.5 2.6 %collective-permute-start.9 = (f32[1,64,512]{2,1,0:T(8,128)S(1)}, f32[1,64,512]{2,1,0:T(8,128)S(1)}, u32[]{:S(2)}, u32[]{:S(2)}) collective-permute-start(f32[1,64,512]{2,1,0:T(8,128)S(1)} %bitcast.44), channel_id=1, source_target_pairs={{0,2},{1,3},{2,0},{3,1},{4,6},{5,7},{6,4},{7,5},{8,10},{9,11},{10,... | collective-permute-start | bytes 393224 | tf_op jit(solution)/shard_map/ppermute | solution.py:17
  9.2 0.1 collective-permute-start.3
  9.3 1.0 %fusion.89 = f32[256,256]{1,0:T(8,128)S(1)} fusion(f32[1024,256]{1,0:T(8,128)S(1)} %get-tuple-element.60, f32[1024,256]{1,0:T(8,128)S(1)} %get-tuple-element.57), kind=kOutput, calls=%fused_computation.113 | convolution fusion | flops 402653184 | bytes 2359296 | tf_op jit(solution)/shard_map/na,nb->ab/dot_general | solution.py:295
  10.3 0.4 fusion.88
  10.7 1.2 %collective-permute-start.2 = (f32[64,256]{1,0:T(8,128)S(1)}, f32[64,256]{1,0:T(8,128)S(1)}, u32[]{:S(2)}, u32[]{:S(2)}) collective-permute-start(f32[64,256]{1,0:T(8,128)S(1)} %select_add_fusion._), channel_id=1, source_target_pairs={{0,3},{1,2},{2,1},{3,0},{4,7},{5,6},{6,5},{7,4},{8,11},{9,10},{10,... | collective-permute-start | bytes 196616 | tf_op jit(solution)/shard_map/ppermute | solution.py:17
  11.9 1.6 %fetch.2 = (f32[1024,256]{1,0:T(8,128)S(1)}, f32[1024,256]{1,0:T(8,128)S(1)}) custom-call(f32[5,1024,256]{2,1,0:T(8,128)} %p_hbm.5, f32[5,1024,256]{2,1,0:T(8,128)} %w_hbm.5, f32[64,256]{1,0:T(8,128)S(1)} %select_add_fusion._), custom_call_target="tpu_custom_call" | custom-call | bytes 65536 | tf_op jit(solution)/shard_map/fetch/pallas_call | solution.py:124
  13.5 0.2 collective-permute-start.6
  13.7 0.4 collective-permute-start.5
  14.2 0.4 collective-permute-done.2
  14.6 0.4 fusion.15
  15.0 0.5 collective-permute-start.4
  15.4 0.3 add_subtract_fusion.2
  15.7 1.1 %collective-permute-start.7 = (f32[64,256]{1,0:T(8,128)S(1)}, f32[64,256]{1,0:T(8,128)S(1)}, u32[]{:S(2)}, u32[]{:S(2)}) collective-permute-start(f32[64,256]{1,0:T(8,128)S(1)} %add_subtract_fusion.2), channel_id=1, source_target_pairs={{0,3},{1,2},{2,1},{3,0},{4,7},{5,6},{6,5},{7,4},{8,11},{9,10},{10,... | collective-permute-start | bytes 196616 | tf_op jit(solution)/shard_map/ppermute | solution.py:17
  16.8 1.0 %fusion.91 = f32[256,256]{1,0:T(8,128)S(1)} fusion(f32[1024,256]{1,0:T(8,128)S(1)} %get-tuple-element.68, f32[1024,256]{1,0:T(8,128)S(1)} %get-tuple-element.65), kind=kOutput, calls=%fused_computation.115 | convolution fusion | flops 402653184 | bytes 2359296 | tf_op jit(solution)/shard_map/na,nb->ab/dot_general | solution.py:295
  17.8 0.4 collective-permute-start.13
  18.2 0.3 collective-permute-start.10
  18.5 0.7 %convolution_subtract_fusion.2 = f32[128,1024]{1,0:T(8,128)S(1)} fusion(f32[128,1024]{1,0:T(8,128)S(1)} %convolution_subtract_fusion.3, f32[1024,256]{1,0:T(8,128)S(1)} %get-tuple-element.57, f32[64,256]{1,0:T(8,128)S(1)} %collective-permute-done.4, f32[64,256]{1,0:T(8,128)S(1)} %fusion.15, pred[]{:T(512)S(6)} %eq.18), kind=kOutput, calls=%fused_computation.2 | convolution fusion | flops 201555968 | bytes 2228225 | tf_op jit(solution)/shard_map/ka,na->kn/dot_general | solution.py:263
  19.1 0.4 fusion.90
  19.5 0.3 collective-permute-done.7
  19.9 1.3 %collective-permute-start.8 = (f32[64,256]{1,0:T(8,128)S(1)}, f32[64,256]{1,0:T(8,128)S(1)}, u32[]{:S(2)}, u32[]{:S(2)}) collective-permute-start(f32[64,256]{1,0:T(8,128)S(1)} %add.42._), channel_id=1, source_target_pairs={{0,5},{1,4},{2,7},{3,6},{4,1},{5,0},{6,3},{7,2},{8,13},{9,12},{10,... | collective-permute-start | bytes 196616 | tf_op jit(solution)/shard_map/ppermute | solution.py:17
  21.2 1.9 %fetch.3 = (f32[1024,256]{1,0:T(8,128)S(1)}, f32[1024,256]{1,0:T(8,128)S(1)}, f32[1024,256]{1,0:T(8,128)S(1)}) custom-call(f32[5,1024,256]{2,1,0:T(8,128)} %p_hbm.5, f32[5,1024,256]{2,1,0:T(8,128)} %w_hbm.5, f32[64,256]{1,0:T(8,128)S(1)} %add.42._), custom_call_target="tpu_custom_call" | custom-call | bytes 65536 | tf_op jit(solution)/shard_map/fetch/pallas_call | solution.py:124
  23.1 0.5 collective-permute-start.12
  23.6 1.2 %collective-permute-start.17 = (f32[1,48,512]{2,1,0:T(8,128)S(1)}, f32[1,48,512]{2,1,0:T(8,128)S(1)}, u32[]{:S(2)}, u32[]{:S(2)}) collective-permute-start(f32[1,48,512]{2,1,0:T(8,128)S(1)} %bitcast.46), channel_id=1, source_target_pairs={{0,2},{1,3},{2,0},{3,1},{4,6},{5,7},{6,4},{7,5},{8,10},{9,11},{10,... | collective-permute-start | bytes 294920 | tf_op jit(solution)/shard_map/ppermute | solution.py:17
  24.8 0.4 fusion.28
  25.3 0.3 add_subtract_fusion.1
  25.6 1.0 %collective-permute-start.14 = (f32[64,256]{1,0:T(8,128)S(1)}, f32[64,256]{1,0:T(8,128)S(1)}, u32[]{:S(2)}, u32[]{:S(2)}) collective-permute-start(f32[64,256]{1,0:T(8,128)S(1)} %add_subtract_fusion.1), channel_id=1, source_target_pairs={{0,3},{1,2},{2,1},{3,0},{4,7},{5,6},{6,5},{7,4},{8,11},{9,10},{10,... | collective-permute-start | bytes 196616 | tf_op jit(solution)/shard_map/ppermute | solution.py:17
  26.6 1.0 %fusion.93 = f32[256,256]{1,0:T(8,128)S(1)} fusion(f32[1024,256]{1,0:T(8,128)S(1)} %get-tuple-element.80, f32[1024,256]{1,0:T(8,128)S(1)} %get-tuple-element.76), kind=kOutput, calls=%fused_computation.117 | convolution fusion | flops 402653184 | bytes 2359296 | tf_op jit(solution)/shard_map/na,nb->ab/dot_general | solution.py:295
  27.6 0.1 collective-permute-start.22
  27.7 0.7 %collective-permute-done.17 = f32[1,48,512]{2,1,0:T(8,128)S(1)} collective-permute-done((f32[1,48,512]{2,1,0:T(8,128)S(1)}, f32[1,48,512]{2,1,0:T(8,128)S(1)}, u32[]{:S(2)}, u32[]{:S(2)}) %collective-permute-start.17) | collective-permute-done | bytes 98336 | tf_op jit(solution)/shard_map/ppermute | solution.py:17
  28.4 0.6 collective-permute-start.18
  29.0 0.5 collective-permute-done.14
  29.4 1.0 %collective-permute-start.15 = (f32[64,256]{1,0:T(8,128)S(1)}, f32[64,256]{1,0:T(8,128)S(1)}, u32[]{:S(2)}, u32[]{:S(2)}) collective-permute-start(f32[64,256]{1,0:T(8,128)S(1)} %add.45), channel_id=1, source_target_pairs={{0,5},{1,4},{2,7},{3,6},{4,1},{5,0},{6,3},{7,2},{8,13},{9,12},{10,... | collective-permute-start | bytes 196616 | tf_op jit(solution)/shard_map/ppermute | solution.py:17
  30.4 0.7 %convolution_subtract_fusion.1 = f32[128,1024]{1,0:T(8,128)S(1)} fusion(f32[128,1024]{1,0:T(8,128)S(1)} %convolution_subtract_fusion.2, f32[1024,256]{1,0:T(8,128)S(1)} %get-tuple-element.65, f32[64,256]{1,0:T(8,128)S(1)} %collective-permute-done.11, f32[64,256]{1,0:T(8,128)S(1)} %fusion.28, pred[]{:T(512)S(6)} %eq.18), kind=kOutput, calls=%fused_computation.1 | convolution fusion | flops 201555968 | bytes 2228225 | tf_op jit(solution)/shard_map/ka,na->kn/dot_general | solution.py:263
  31.1 4.2 %collective-permute-done.15 = f32[64,256]{1,0:T(8,128)S(1)} collective-permute-done((f32[64,256]{1,0:T(8,128)S(1)}, f32[64,256]{1,0:T(8,128)S(1)}, u32[]{:S(2)}, u32[]{:S(2)}) %collective-permute-start.15) | collective-permute-done | bytes 65568 | tf_op jit(solution)/shard_map/ppermute | solution.py:17
  35.3 0.5 collective-permute-done.18
  35.8 0.6 collective-permute-start.19
  36.5 0.4 fusion.92
  37.0 1.7 %collective-permute-start.16 = (f32[64,256]{1,0:T(8,128)S(1)}, f32[64,256]{1,0:T(8,128)S(1)}, u32[]{:S(2)}, u32[]{:S(2)}) collective-permute-start(f32[64,256]{1,0:T(8,128)S(1)} %add.46), channel_id=1, source_target_pairs={{0,9},{1,8},{2,11},{3,10},{4,13},{5,12},{6,15},{7,14},{8,1},{9,0},... | collective-permute-start | bytes 196616 | tf_op jit(solution)/shard_map/ppermute | solution.py:17
  38.8 2.1 %collective-permute-done.16 = f32[64,256]{1,0:T(8,128)S(1)} collective-permute-done((f32[64,256]{1,0:T(8,128)S(1)}, f32[64,256]{1,0:T(8,128)S(1)}, u32[]{:S(2)}, u32[]{:S(2)}) %collective-permute-start.16) | collective-permute-done | bytes 65568 | tf_op jit(solution)/shard_map/ppermute | solution.py:17
  40.9 0.4 fusion.41
  41.2 0.3 add_subtract_fusion
  41.5 1.2 %collective-permute-start.23 = (f32[64,256]{1,0:T(8,128)S(1)}, f32[64,256]{1,0:T(8,128)S(1)}, u32[]{:S(2)}, u32[]{:S(2)}) collective-permute-start(f32[64,256]{1,0:T(8,128)S(1)} %add_subtract_fusion), channel_id=1, source_target_pairs={{0,3},{1,2},{2,1},{3,0},{4,7},{5,6},{6,5},{7,4},{8,11},{9,10},{10,... | collective-permute-start | bytes 196616 | tf_op jit(solution)/shard_map/ppermute | solution.py:17
  42.8 1.6 %collective-permute-start.27 = (f32[4,16,512]{2,1,0:T(8,128)S(1)}, f32[4,16,512]{2,1,0:T(8,128)S(1)}, u32[]{:S(2)}, u32[]{:S(2)}) collective-permute-start(f32[4,16,512]{2,1,0:T(8,128)S(1)} %slice.57), channel_id=1, source_target_pairs={{0,8},{1,9},{2,10},{3,11},{4,12},{5,13},{6,14},{7,15},{8,0},{9,1},... | collective-permute-start | bytes 393224 | tf_op jit(solution)/shard_map/ppermute | solution.py:17
  44.4 1.1 %collective-permute-done.23 = f32[64,256]{1,0:T(8,128)S(1)} collective-permute-done((f32[64,256]{1,0:T(8,128)S(1)}, f32[64,256]{1,0:T(8,128)S(1)}, u32[]{:S(2)}, u32[]{:S(2)}) %collective-permute-start.23) | collective-permute-done | bytes 65568 | tf_op jit(solution)/shard_map/ppermute | solution.py:17
  45.6 1.0 %collective-permute-start.24 = (f32[64,256]{1,0:T(8,128)S(1)}, f32[64,256]{1,0:T(8,128)S(1)}, u32[]{:S(2)}, u32[]{:S(2)}) collective-permute-start(f32[64,256]{1,0:T(8,128)S(1)} %add.49), channel_id=1, source_target_pairs={{0,5},{1,4},{2,7},{3,6},{4,1},{5,0},{6,3},{7,2},{8,13},{9,12},{10,... | collective-permute-start | bytes 196616 | tf_op jit(solution)/shard_map/ppermute | solution.py:17
  46.5 0.2 collective-permute-start.20
  46.8 2.9 %collective-permute-done.24 = f32[64,256]{1,0:T(8,128)S(1)} collective-permute-done((f32[64,256]{1,0:T(8,128)S(1)}, f32[64,256]{1,0:T(8,128)S(1)}, u32[]{:S(2)}, u32[]{:S(2)}) %collective-permute-start.24) | collective-permute-done | bytes 65568 | tf_op jit(solution)/shard_map/ppermute | solution.py:17
  49.6 1.5 %collective-permute-start.25 = (f32[64,256]{1,0:T(8,128)S(1)}, f32[64,256]{1,0:T(8,128)S(1)}, u32[]{:S(2)}, u32[]{:S(2)}) collective-permute-start(f32[64,256]{1,0:T(8,128)S(1)} %add.50), channel_id=1, source_target_pairs={{0,9},{1,8},{2,11},{3,10},{4,13},{5,12},{6,15},{7,14},{8,1},{9,0},... | collective-permute-start | bytes 196616 | tf_op jit(solution)/shard_map/ppermute | solution.py:17
  51.1 0.3 collective-permute-start.28
  51.5 0.7 %convolution_subtract_fusion.x_ref = f32[128,1024]{1,0:T(8,128)S(1)} fusion(f32[128,1024]{1,0:T(8,128)S(1)} %convolution_subtract_fusion.1, f32[1024,256]{1,0:T(8,128)S(1)} %get-tuple-element.76, f32[64,256]{1,0:T(8,128)S(1)} %collective-permute-done.20, f32[64,256]{1,0:T(8,128)S(1)} %fusion.41, pred[]{:T(512)S(6)} %eq.18), kind=kOutput, calls=%fused_computation | convolution fusion | flops 201555968 | bytes 2228225 | tf_op jit(solution)/shard_map/ka,na->kn/dot_general | solution.py:263
  52.1 1.6 %collective-permute-done.25 = f32[64,256]{1,0:T(8,128)S(1)} collective-permute-done((f32[64,256]{1,0:T(8,128)S(1)}, f32[64,256]{1,0:T(8,128)S(1)}, u32[]{:S(2)}, u32[]{:S(2)}) %collective-permute-start.25) | collective-permute-done | bytes 65568 | tf_op jit(solution)/shard_map/ppermute | solution.py:17
  53.8 2.4 %collective-permute-start.26 = (f32[64,256]{1,0:T(8,128)S(1)}, f32[64,256]{1,0:T(8,128)S(1)}, u32[]{:S(2)}, u32[]{:S(2)}) collective-permute-start(f32[64,256]{1,0:T(8,128)S(1)} %add.51), channel_id=1, source_target_pairs={{0,17},{1,16},{2,19},{3,18},{4,21},{5,20},{6,23},{7,22},{8,25},{9,... | collective-permute-start | bytes 196616 | tf_op jit(solution)/shard_map/ppermute | solution.py:17
  56.3 2.5 %collective-permute-done.26 = f32[64,256]{1,0:T(8,128)S(1)} collective-permute-done((f32[64,256]{1,0:T(8,128)S(1)}, f32[64,256]{1,0:T(8,128)S(1)}, u32[]{:S(2)}, u32[]{:S(2)}) %collective-permute-start.26) | collective-permute-done | bytes 65568 | tf_op jit(solution)/shard_map/ppermute | solution.py:17
  58.8 0.4 fusion.54
  59.2 1.6 %collective-permute-start.29 = (f32[64,256]{1,0:T(8,128)S(1)}, f32[64,256]{1,0:T(8,128)S(1)}, u32[]{:S(2)}, u32[]{:S(2)}) collective-permute-start(f32[64,256]{1,0:T(8,128)S(1)} %fusion.54), channel_id=1, source_target_pairs={{0,1},{1,0},{2,3},{3,2},{4,5},{5,4},{6,7},{7,6},{8,9},{9,8},{10,11... | collective-permute-start | bytes 196616 | tf_op jit(solution)/shard_map/ppermute | solution.py:17
  60.8 0.9 %collective-permute-done.29 = f32[64,256]{1,0:T(8,128)S(1)} collective-permute-done((f32[64,256]{1,0:T(8,128)S(1)}, f32[64,256]{1,0:T(8,128)S(1)}, u32[]{:S(2)}, u32[]{:S(2)}) %collective-permute-start.29) | collective-permute-done | bytes 65568 | tf_op jit(solution)/shard_map/ppermute | solution.py:17
  61.7 1.4 %finish.1 = f32[1024,128]{1,0:T(8,128)} custom-call(f32[128,1024]{1,0:T(8,128)S(1)} %convolution_subtract_fusion.x_ref, f32[1024,256]{1,0:T(8,128)S(1)} %get-tuple-element.77.w_ref, f32[128,256]{1,0:T(8,128)S(1)} %maximum_select_fusion.19.t_ref), custom_call_target="tpu_custom_call" | custom-call | flops 201326592 | bytes 2097152 | tf_op jit(solution)/shard_map/finish/pallas_call | solution.py:144
  (44 shorter events, 0.7 us)
Async XLA Ops:
  3.1 1.5 %collective-permute-start = (f32[128,256]{1,0:T(8,128)S(1)}, f32[128,256]{1,0:T(8,128)S(1)}, u32[]{:S(2)}, u32[]{:S(2)}) collective-permute-start(f32[128,256]{1,0:T(8,128)S(1)} %get-tuple-element.48), channel_id=1, source_target_pairs={{0,1},{1,0},{2,3},{3,2},{4,5},{5,4},{6,7},{7,6},{8,9},{9,8},{10,11... | collective-permute-start | bytes 393224 | tf_op jit(solution)/shard_map/ppermute | solution.py:17
  6.1 3.1 %collective-permute-start.1 = (f32[64,256]{1,0:T(8,128)S(1)}, f32[64,256]{1,0:T(8,128)S(1)}, u32[]{:S(2)}, u32[]{:S(2)}) collective-permute-start(f32[64,256]{1,0:T(8,128)S(1)} %slice_select_fusion.3), channel_id=1, source_target_pairs={{0,1},{1,0},{2,3},{3,2},{4,5},{5,4},{6,7},{7,6},{8,9},{9,8},{10,11... | collective-permute-start | bytes 196616 | tf_op jit(solution)/shard_map/ppermute | solution.py:17
  6.5 11.7 %collective-permute-start.9 = (f32[1,64,512]{2,1,0:T(8,128)S(1)}, f32[1,64,512]{2,1,0:T(8,128)S(1)}, u32[]{:S(2)}, u32[]{:S(2)}) collective-permute-start(f32[1,64,512]{2,1,0:T(8,128)S(1)} %bitcast.44), channel_id=1, source_target_pairs={{0,2},{1,3},{2,0},{3,1},{4,6},{5,7},{6,4},{7,5},{8,10},{9,11},{10,... | collective-permute-start | bytes 393224 | tf_op jit(solution)/shard_map/ppermute | solution.py:17
  9.2 5.0 %collective-permute-start.3 = (f32[1,128,512]{2,1,0:T(8,128)S(1)}, f32[1,128,512]{2,1,0:T(8,128)S(1)}, u32[]{:S(2)}, u32[]{:S(2)}) collective-permute-start(f32[1,128,512]{2,1,0:T(8,128)S(1)} %bitcast.42), channel_id=1, source_target_pairs={{0,1},{1,0},{2,3},{3,2},{4,5},{5,4},{6,7},{7,6},{8,9},{9,8},{10,11... | collective-permute-start | bytes 786440 | tf_op jit(solution)/shard_map/ppermute | solution.py:17
  10.7 3.9 %collective-permute-start.2 = (f32[64,256]{1,0:T(8,128)S(1)}, f32[64,256]{1,0:T(8,128)S(1)}, u32[]{:S(2)}, u32[]{:S(2)}) collective-permute-start(f32[64,256]{1,0:T(8,128)S(1)} %select_add_fusion._), channel_id=1, source_target_pairs={{0,3},{1,2},{2,1},{3,0},{4,7},{5,6},{6,5},{7,4},{8,11},{9,10},{10,... | collective-permute-start | bytes 196616 | tf_op jit(solution)/shard_map/ppermute | solution.py:17
  13.5 2.0 %collective-permute-start.6 = (f32[256,256]{1,0:T(8,128)S(1)}, f32[256,256]{1,0:T(8,128)S(1)}, u32[]{:S(2)}, u32[]{:S(2)}) collective-permute-start(f32[256,256]{1,0:T(8,128)S(1)} %fusion.89), channel_id=1, source_target_pairs={{0,1},{1,0},{2,3},{3,2},{4,5},{5,4},{6,7},{7,6},{8,9},{9,8},{10,11... | collective-permute-start | bytes 786440 | tf_op jit(solution)/shard_map/ppermute | solution.py:17
  13.7 1.7 %collective-permute-start.5 = (f32[64,256]{1,0:T(8,128)S(1)}, f32[64,256]{1,0:T(8,128)S(1)}, u32[]{:S(2)}, u32[]{:S(2)}) collective-permute-start(f32[64,256]{1,0:T(8,128)S(1)} %slice_select_fusion.2), channel_id=1, source_target_pairs={{0,1},{1,0},{2,3},{3,2},{4,5},{5,4},{6,7},{7,6},{8,9},{9,8},{10,11... | collective-permute-start | bytes 196616 | tf_op jit(solution)/shard_map/ppermute | solution.py:17
  15.0 3.5 %collective-permute-start.4 = (f32[64,256]{1,0:T(8,128)S(1)}, f32[64,256]{1,0:T(8,128)S(1)}, u32[]{:S(2)}, u32[]{:S(2)}) collective-permute-start(f32[64,256]{1,0:T(8,128)S(1)} %fusion.15), channel_id=1, source_target_pairs={{0,1},{1,0},{2,3},{3,2},{4,5},{5,4},{6,7},{7,6},{8,9},{9,8},{10,11... | collective-permute-start | bytes 196616 | tf_op jit(solution)/shard_map/ppermute | solution.py:17
  15.7 4.2 %collective-permute-start.7 = (f32[64,256]{1,0:T(8,128)S(1)}, f32[64,256]{1,0:T(8,128)S(1)}, u32[]{:S(2)}, u32[]{:S(2)}) collective-permute-start(f32[64,256]{1,0:T(8,128)S(1)} %add_subtract_fusion.2), channel_id=1, source_target_pairs={{0,3},{1,2},{2,1},{3,0},{4,7},{5,6},{6,5},{7,4},{8,11},{9,10},{10,... | collective-permute-start | bytes 196616 | tf_op jit(solution)/shard_map/ppermute | solution.py:17
  17.8 7.5 %collective-permute-start.13 = (f32[256,256]{1,0:T(8,128)S(1)}, f32[256,256]{1,0:T(8,128)S(1)}, u32[]{:S(2)}, u32[]{:S(2)}) collective-permute-start(f32[256,256]{1,0:T(8,128)S(1)} %fusion.91), channel_id=1, source_target_pairs={{0,1},{1,0},{2,3},{3,2},{4,5},{5,4},{6,7},{7,6},{8,9},{9,8},{10,11... | collective-permute-start | bytes 786440 | tf_op jit(solution)/shard_map/ppermute | solution.py:17
  18.2 6.6 %collective-permute-start.10 = (f32[2,64,512]{2,1,0:T(8,128)S(1)}, f32[2,64,512]{2,1,0:T(8,128)S(1)}, u32[]{:S(2)}, u32[]{:S(2)}) collective-permute-start(f32[2,64,512]{2,1,0:T(8,128)S(1)} %maximum_select_fusion.6), channel_id=1, source_target_pairs={{0,1},{1,0},{2,3},{3,2},{4,5},{5,4},{6,7},{7,6},{8,9},{9,8},{10,11... | collective-permute-start | bytes 786440 | tf_op jit(solution)/shard_map/ppermute | solution.py:17
  19.9 4.9 %collective-permute-start.8 = (f32[64,256]{1,0:T(8,128)S(1)}, f32[64,256]{1,0:T(8,128)S(1)}, u32[]{:S(2)}, u32[]{:S(2)}) collective-permute-start(f32[64,256]{1,0:T(8,128)S(1)} %add.42._), channel_id=1, source_target_pairs={{0,5},{1,4},{2,7},{3,6},{4,1},{5,0},{6,3},{7,2},{8,13},{9,12},{10,... | collective-permute-start | bytes 196616 | tf_op jit(solution)/shard_map/ppermute | solution.py:17
  23.1 2.2 %collective-permute-start.12 = (f32[64,256]{1,0:T(8,128)S(1)}, f32[64,256]{1,0:T(8,128)S(1)}, u32[]{:S(2)}, u32[]{:S(2)}) collective-permute-start(f32[64,256]{1,0:T(8,128)S(1)} %slice_select_fusion.1), channel_id=1, source_target_pairs={{0,1},{1,0},{2,3},{3,2},{4,5},{5,4},{6,7},{7,6},{8,9},{9,8},{10,11... | collective-permute-start | bytes 196616 | tf_op jit(solution)/shard_map/ppermute | solution.py:17
  23.6 4.8 %collective-permute-start.17 = (f32[1,48,512]{2,1,0:T(8,128)S(1)}, f32[1,48,512]{2,1,0:T(8,128)S(1)}, u32[]{:S(2)}, u32[]{:S(2)}) collective-permute-start(f32[1,48,512]{2,1,0:T(8,128)S(1)} %bitcast.46), channel_id=1, source_target_pairs={{0,2},{1,3},{2,0},{3,1},{4,6},{5,7},{6,4},{7,5},{8,10},{9,11},{10,... | collective-permute-start | bytes 294920 | tf_op jit(solution)/shard_map/ppermute | solution.py:17
  25.2 5.2 %collective-permute-start.11 = (f32[64,256]{1,0:T(8,128)S(1)}, f32[64,256]{1,0:T(8,128)S(1)}, u32[]{:S(2)}, u32[]{:S(2)}) collective-permute-start(f32[64,256]{1,0:T(8,128)S(1)} %fusion.28), channel_id=1, source_target_pairs={{0,1},{1,0},{2,3},{3,2},{4,5},{5,4},{6,7},{7,6},{8,9},{9,8},{10,11... | collective-permute-start | bytes 196616 | tf_op jit(solution)/shard_map/ppermute | solution.py:17
  25.6 3.8 %collective-permute-start.14 = (f32[64,256]{1,0:T(8,128)S(1)}, f32[64,256]{1,0:T(8,128)S(1)}, u32[]{:S(2)}, u32[]{:S(2)}) collective-permute-start(f32[64,256]{1,0:T(8,128)S(1)} %add_subtract_fusion.1), channel_id=1, source_target_pairs={{0,3},{1,2},{2,1},{3,0},{4,7},{5,6},{6,5},{7,4},{8,11},{9,10},{10,... | collective-permute-start | bytes 196616 | tf_op jit(solution)/shard_map/ppermute | solution.py:17
  27.6 13.6 %collective-permute-start.22 = (f32[256,256]{1,0:T(8,128)S(1)}, f32[256,256]{1,0:T(8,128)S(1)}, u32[]{:S(2)}, u32[]{:S(2)}) collective-permute-start(f32[256,256]{1,0:T(8,128)S(1)} %fusion.93), channel_id=1, source_target_pairs={{0,1},{1,0},{2,3},{3,2},{4,5},{5,4},{6,7},{7,6},{8,9},{9,8},{10,11... | collective-permute-start | bytes 786440 | tf_op jit(solution)/shard_map/ppermute | solution.py:17
  28.4 7.4 %collective-permute-start.18 = (f32[2,48,512]{2,1,0:T(8,128)S(1)}, f32[2,48,512]{2,1,0:T(8,128)S(1)}, u32[]{:S(2)}, u32[]{:S(2)}) collective-permute-start(f32[2,48,512]{2,1,0:T(8,128)S(1)} %maximum_select_fusion.8), channel_id=1, source_target_pairs={{0,4},{1,5},{2,6},{3,7},{4,0},{5,1},{6,2},{7,3},{8,12},{9,13},{10,... | collective-permute-start | bytes 589832 | tf_op jit(solution)/shard_map/ppermute | solution.py:17
  29.4 5.8 %collective-permute-start.15 = (f32[64,256]{1,0:T(8,128)S(1)}, f32[64,256]{1,0:T(8,128)S(1)}, u32[]{:S(2)}, u32[]{:S(2)}) collective-permute-start(f32[64,256]{1,0:T(8,128)S(1)} %add.45), channel_id=1, source_target_pairs={{0,5},{1,4},{2,7},{3,6},{4,1},{5,0},{6,3},{7,2},{8,13},{9,12},{10,... | collective-permute-start | bytes 196616 | tf_op jit(solution)/shard_map/ppermute | solution.py:17
  35.8 2.8 %collective-permute-start.19 = (f32[4,32,512]{2,1,0:T(8,128)S(1)}, f32[4,32,512]{2,1,0:T(8,128)S(1)}, u32[]{:S(2)}, u32[]{:S(2)}) collective-permute-start(f32[4,32,512]{2,1,0:T(8,128)S(1)} %slice.54), channel_id=1, source_target_pairs={{0,1},{1,0},{2,3},{3,2},{4,5},{5,4},{6,7},{7,6},{8,9},{9,8},{10,11... | collective-permute-start | bytes 786440 | tf_op jit(solution)/shard_map/ppermute | solution.py:17
  36.9 4.3 %collective-permute-start.21 = (f32[64,256]{1,0:T(8,128)S(1)}, f32[64,256]{1,0:T(8,128)S(1)}, u32[]{:S(2)}, u32[]{:S(2)}) collective-permute-start(f32[64,256]{1,0:T(8,128)S(1)} %slice_select_fusion), channel_id=1, source_target_pairs={{0,1},{1,0},{2,3},{3,2},{4,5},{5,4},{6,7},{7,6},{8,9},{9,8},{10,11... | collective-permute-start | bytes 196616 | tf_op jit(solution)/shard_map/ppermute | solution.py:17
  37.0 3.9 %collective-permute-start.16 = (f32[64,256]{1,0:T(8,128)S(1)}, f32[64,256]{1,0:T(8,128)S(1)}, u32[]{:S(2)}, u32[]{:S(2)}) collective-permute-start(f32[64,256]{1,0:T(8,128)S(1)} %add.46), channel_id=1, source_target_pairs={{0,9},{1,8},{2,11},{3,10},{4,13},{5,12},{6,15},{7,14},{8,1},{9,0},... | collective-permute-start | bytes 196616 | tf_op jit(solution)/shard_map/ppermute | solution.py:17
  41.5 4.0 %collective-permute-start.23 = (f32[64,256]{1,0:T(8,128)S(1)}, f32[64,256]{1,0:T(8,128)S(1)}, u32[]{:S(2)}, u32[]{:S(2)}) collective-permute-start(f32[64,256]{1,0:T(8,128)S(1)} %add_subtract_fusion), channel_id=1, source_target_pairs={{0,3},{1,2},{2,1},{3,0},{4,7},{5,6},{6,5},{7,4},{8,11},{9,10},{10,... | collective-permute-start | bytes 196616 | tf_op jit(solution)/shard_map/ppermute | solution.py:17
  42.8 8.3 %collective-permute-start.27 = (f32[4,16,512]{2,1,0:T(8,128)S(1)}, f32[4,16,512]{2,1,0:T(8,128)S(1)}, u32[]{:S(2)}, u32[]{:S(2)}) collective-permute-start(f32[4,16,512]{2,1,0:T(8,128)S(1)} %slice.57), channel_id=1, source_target_pairs={{0,8},{1,9},{2,10},{3,11},{4,12},{5,13},{6,14},{7,15},{8,0},{9,1},... | collective-permute-start | bytes 393224 | tf_op jit(solution)/shard_map/ppermute | solution.py:17
  45.6 4.1 %collective-permute-start.24 = (f32[64,256]{1,0:T(8,128)S(1)}, f32[64,256]{1,0:T(8,128)S(1)}, u32[]{:S(2)}, u32[]{:S(2)}) collective-permute-start(f32[64,256]{1,0:T(8,128)S(1)} %add.49), channel_id=1, source_target_pairs={{0,5},{1,4},{2,7},{3,6},{4,1},{5,0},{6,3},{7,2},{8,13},{9,12},{10,... | collective-permute-start | bytes 196616 | tf_op jit(solution)/shard_map/ppermute | solution.py:17
  46.5 4.9 %collective-permute-start.20 = (f32[64,256]{1,0:T(8,128)S(1)}, f32[64,256]{1,0:T(8,128)S(1)}, u32[]{:S(2)}, u32[]{:S(2)}) collective-permute-start(f32[64,256]{1,0:T(8,128)S(1)} %fusion.41), channel_id=1, source_target_pairs={{0,1},{1,0},{2,3},{3,2},{4,5},{5,4},{6,7},{7,6},{8,9},{9,8},{10,11... | collective-permute-start | bytes 196616 | tf_op jit(solution)/shard_map/ppermute | solution.py:17
  49.6 4.1 %collective-permute-start.25 = (f32[64,256]{1,0:T(8,128)S(1)}, f32[64,256]{1,0:T(8,128)S(1)}, u32[]{:S(2)}, u32[]{:S(2)}) collective-permute-start(f32[64,256]{1,0:T(8,128)S(1)} %add.50), channel_id=1, source_target_pairs={{0,9},{1,8},{2,11},{3,10},{4,13},{5,12},{6,15},{7,14},{8,1},{9,0},... | collective-permute-start | bytes 196616 | tf_op jit(solution)/shard_map/ppermute | solution.py:17
  51.1 5.1 %collective-permute-start.28 = (f32[8,16,512]{2,1,0:T(8,128)S(1)}, f32[8,16,512]{2,1,0:T(8,128)S(1)}, u32[]{:S(2)}, u32[]{:S(2)}) collective-permute-start(f32[8,16,512]{2,1,0:T(8,128)S(1)} %maximum_select_fusion.7), channel_id=1, source_target_pairs={{0,1},{1,0},{2,3},{3,2},{4,5},{5,4},{6,7},{7,6},{8,9},{9,8},{10,11... | collective-permute-start | bytes 786440 | tf_op jit(solution)/shard_map/ppermute | solution.py:17
  53.8 5.0 %collective-permute-start.26 = (f32[64,256]{1,0:T(8,128)S(1)}, f32[64,256]{1,0:T(8,128)S(1)}, u32[]{:S(2)}, u32[]{:S(2)}) collective-permute-start(f32[64,256]{1,0:T(8,128)S(1)} %add.51), channel_id=1, source_target_pairs={{0,17},{1,16},{2,19},{3,18},{4,21},{5,20},{6,23},{7,22},{8,25},{9,... | collective-permute-start | bytes 196616 | tf_op jit(solution)/shard_map/ppermute | solution.py:17
  59.2 2.5 %collective-permute-start.29 = (f32[64,256]{1,0:T(8,128)S(1)}, f32[64,256]{1,0:T(8,128)S(1)}, u32[]{:S(2)}, u32[]{:S(2)}) collective-permute-start(f32[64,256]{1,0:T(8,128)S(1)} %fusion.54), channel_id=1, source_target_pairs={{0,1},{1,0},{2,3},{3,2},{4,5},{5,4},{6,7},{7,6},{8,9},{9,8},{10,11... | collective-permute-start | bytes 196616 | tf_op jit(solution)/shard_map/ppermute | solution.py:17

commit v4 on v3

--- a/solution.py
+++ b/solution.py
@@ -240,11 +240,15 @@
     else:
         open_gather(far, fetched[-1], None)
 
+    marks = {}
+
     def solve(level, value, ahead_of, later=None, fetch_rest=None):
         top = bits[level]
         for bit in range(1, top):
             value = ahead_of.get(bit, lambda v: v)(value)
             value = value + across(value, bit)
+            if bit == 1:
+                marks[level] = value
             if near and level == 0 and bit == top - 2:
                 step(value)
                 step(value)
@@ -290,7 +294,8 @@
         held = solve(level, value, {}, later, fetch_rest if level == first - 2 else None)
         if level < first - 1:
             proj, corr = (later[0][0], later[0][1]) if level == first - 2 else (later[1][0], later[1][1])
-        proj, corr = tie(proj, start), tie(corr, start)
+        after = marks[level] if level == 1 else start
+        proj, corr = tie(proj, after), tie(corr, after)
         ahead = chip_sum(project(proj, state))
         own = jnp.einsum("na,nb->ab", proj, corr, precision=HIGH)
         value = ahead - times_transposed(held, own + exchange(own, 1))

time: 63.2 us -> 62.7 us (level)
  no operation moved by 1% of the time
where the time goes in v4:
time: 62.7 us; the launch traced here: 62.6 us
  starting transfers between devices  25.4 us (41%)
  waiting for transfers between devices  18.5 us (30%)
  matrix products  9.98 us (16%)
  Pallas kernels  7.84 us (13%)
    ppermute x30, starting transfers between devices, exchange(): return lax.ppermute(value, 'leaf', pairs)  25.4 us
    ppermute x30, waiting for transfers between devices, exchange(): return lax.ppermute(value, 'leaf', pairs)  18.5 us
    pallas_call x2, Pallas kernels, fetch(): pl.pallas_call(body, in_specs=[IN_HBM, IN_HBM, pl.BlockSpec(memory_space=...  3.44 us
    pallas_call x1, Pallas kernels, begin(): pl.pallas_call(body, in_specs=[IN_HBM] * 4, out_specs=[IN_VMEM] * len(sha...  3.05 us
    dot_general x3, matrix products, on_device(): own = jnp.einsum('na,nb->ab', proj, corr, precision=HIGH)  2.98 us
    dot_general x8, matrix products, times_transposed(): return jnp.einsum('kb,ab->ka', left, right, precision=HIGH)  2.74 us
    dot_general x4, matrix products, update(): return state - jnp.einsum('ka,na->kn', held, corr, precision=HIGH)  2.64 us
    dot_general x4, matrix products, project(): return jnp.einsum('kn,nr->kr', state, basis, precision=HIGH)  1.62 us
  transfers between devices with their start and end apart: 30, of which 13 were waited for; matrix products, arithmetic and copies ran while one was open for 13% of the time, Pallas kernels for 5%

profile of v4, /device:TPU:0, one launch (start us, length us, event | category | flops | bytes accessed | tf_op | source)
XLA Modules:
  0.0 62.6 jit_solution(526427494072415085)
XLA Ops:
  0.0 3.0 %begin.1 = (f32[128,256]{1,0:T(8,128)S(1)}, f32[128,1024]{1,0:T(8,128)S(1)}, f32[1024,256]{1,0:T(8,128)S(1)}, f32[1024,256]{1,0:T(8,128)S(1)}, f32[1024,256]{1,0...) custom-call(f32[1024,128]{1,0:T(8,128)} %x_hbm, ...), custom_call_target="tpu_custom_call" | custom-call | flops 201326592 | bytes 4194304 | tf_op jit(solution)/shard_map/begin/pallas_call | solution.py:90
  3.1 0.5 collective-permute-start
  3.6 1.0 %collective-permute-done = f32[128,256]{1,0:T(8,128)S(1)} collective-permute-done((f32[128,256]{1,0:T(8,128)S(1)}, f32[128,256]{1,0:T(8,128)S(1)}, u32[]{:S(2)}, u32[]{:S(2)}) %collective-permute-start) | collective-permute-done | bytes 131104 | tf_op jit(solution)/shard_map/ppermute | solution.py:17
  4.6 0.4 fusion.1
  5.0 0.7 %convolution_subtract_fusion.3 = f32[128,1024]{1,0:T(8,128)S(1)} fusion(f32[128,1024]{1,0:T(8,128)S(1)} %get-tuple-element.46, f32[128,256]{1,0:T(8,128)S(1)} %fusion.1, f32[1024,256]{1,0:T(8,128)S(1)} %get-tuple-element.50), kind=kOutput, calls=%fused_computation.3 | convolution fusion | flops 201457664 | bytes 2228224 | tf_op jit(solution)/shard_map/ka,na->kn/dot_general | solution.py:267
  5.6 0.4 fusion.87
  6.1 0.4 collective-permute-start.1
  6.5 2.6 %collective-permute-start.9 = (f32[1,64,512]{2,1,0:T(8,128)S(1)}, f32[1,64,512]{2,1,0:T(8,128)S(1)}, u32[]{:S(2)}, u32[]{:S(2)}) collective-permute-start(f32[1,64,512]{2,1,0:T(8,128)S(1)} %bitcast.44), channel_id=1, source_target_pairs={{0,2},{1,3},{2,0},{3,1},{4,6},{5,7},{6,4},{7,5},{8,10},{9,11},{10,... | collective-permute-start | bytes 393224 | tf_op jit(solution)/shard_map/ppermute | solution.py:17
  9.2 0.1 collective-permute-start.3
  9.3 1.0 %fusion.89 = f32[256,256]{1,0:T(8,128)S(1)} fusion(f32[1024,256]{1,0:T(8,128)S(1)} %get-tuple-element.60, f32[1024,256]{1,0:T(8,128)S(1)} %get-tuple-element.57), kind=kOutput, calls=%fused_computation.113 | convolution fusion | flops 402653184 | bytes 2359296 | tf_op jit(solution)/shard_map/na,nb->ab/dot_general | solution.py:300
  10.3 0.4 fusion.88
  10.7 1.2 %collective-permute-start.2 = (f32[64,256]{1,0:T(8,128)S(1)}, f32[64,256]{1,0:T(8,128)S(1)}, u32[]{:S(2)}, u32[]{:S(2)}) collective-permute-start(f32[64,256]{1,0:T(8,128)S(1)} %select_add_fusion._), channel_id=1, source_target_pairs={{0,3},{1,2},{2,1},{3,0},{4,7},{5,6},{6,5},{7,4},{8,11},{9,10},{10,... | collective-permute-start | bytes 196616 | tf_op jit(solution)/shard_map/ppermute | solution.py:17
  11.9 1.6 %fetch.2 = (f32[1024,256]{1,0:T(8,128)S(1)}, f32[1024,256]{1,0:T(8,128)S(1)}) custom-call(f32[5,1024,256]{2,1,0:T(8,128)} %p_hbm.5, f32[5,1024,256]{2,1,0:T(8,128)} %w_hbm.5, f32[64,256]{1,0:T(8,128)S(1)} %select_add_fusion._), custom_call_target="tpu_custom_call" | custom-call | bytes 65536 | tf_op jit(solution)/shard_map/fetch/pallas_call | solution.py:124
  13.5 0.2 collective-permute-start.6
  13.7 0.4 collective-permute-start.5
  14.2 0.4 collective-permute-done.2
  14.6 0.4 fusion.15
  15.0 0.5 collective-permute-start.4
  15.4 0.3 add_subtract_fusion.2
  15.7 1.1 %collective-permute-start.7 = (f32[64,256]{1,0:T(8,128)S(1)}, f32[64,256]{1,0:T(8,128)S(1)}, u32[]{:S(2)}, u32[]{:S(2)}) collective-permute-start(f32[64,256]{1,0:T(8,128)S(1)} %add_subtract_fusion.2), channel_id=1, source_target_pairs={{0,3},{1,2},{2,1},{3,0},{4,7},{5,6},{6,5},{7,4},{8,11},{9,10},{10,... | collective-permute-start | bytes 196616 | tf_op jit(solution)/shard_map/ppermute | solution.py:17
  16.8 1.0 %fusion.91 = f32[256,256]{1,0:T(8,128)S(1)} fusion(f32[1024,256]{1,0:T(8,128)S(1)} %get-tuple-element.68, f32[1024,256]{1,0:T(8,128)S(1)} %get-tuple-element.65), kind=kOutput, calls=%fused_computation.115 | convolution fusion | flops 402653184 | bytes 2359296 | tf_op jit(solution)/shard_map/na,nb->ab/dot_general | solution.py:300
  17.8 0.4 collective-permute-start.13
  18.2 0.3 collective-permute-start.10
  18.5 0.7 %convolution_subtract_fusion.2 = f32[128,1024]{1,0:T(8,128)S(1)} fusion(f32[128,1024]{1,0:T(8,128)S(1)} %convolution_subtract_fusion.3, f32[1024,256]{1,0:T(8,128)S(1)} %get-tuple-element.57, f32[64,256]{1,0:T(8,128)S(1)} %collective-permute-done.4, f32[64,256]{1,0:T(8,128)S(1)} %fusion.15, pred[]{:T(512)S(6)} %eq.18), kind=kOutput, calls=%fused_computation.2 | convolution fusion | flops 201555968 | bytes 2228225 | tf_op jit(solution)/shard_map/ka,na->kn/dot_general | solution.py:267
  19.1 0.4 fusion.90
  19.5 0.3 collective-permute-done.7
  19.9 1.3 %collective-permute-start.8 = (f32[64,256]{1,0:T(8,128)S(1)}, f32[64,256]{1,0:T(8,128)S(1)}, u32[]{:S(2)}, u32[]{:S(2)}) collective-permute-start(f32[64,256]{1,0:T(8,128)S(1)} %add.42._), channel_id=1, source_target_pairs={{0,5},{1,4},{2,7},{3,6},{4,1},{5,0},{6,3},{7,2},{8,13},{9,12},{10,... | collective-permute-start | bytes 196616 | tf_op jit(solution)/shard_map/ppermute | solution.py:17
  21.2 1.9 %fetch.3 = (f32[1024,256]{1,0:T(8,128)S(1)}, f32[1024,256]{1,0:T(8,128)S(1)}, f32[1024,256]{1,0:T(8,128)S(1)}) custom-call(f32[5,1024,256]{2,1,0:T(8,128)} %p_hbm.5, f32[5,1024,256]{2,1,0:T(8,128)} %w_hbm.5, f32[64,256]{1,0:T(8,128)S(1)} %add.42._), custom_call_target="tpu_custom_call" | custom-call | bytes 65536 | tf_op jit(solution)/shard_map/fetch/pallas_call | solution.py:124
  23.1 0.5 collective-permute-start.12
  23.6 1.2 %collective-permute-start.17 = (f32[1,48,512]{2,1,0:T(8,128)S(1)}, f32[1,48,512]{2,1,0:T(8,128)S(1)}, u32[]{:S(2)}, u32[]{:S(2)}) collective-permute-start(f32[1,48,512]{2,1,0:T(8,128)S(1)} %bitcast.46), channel_id=1, source_target_pairs={{0,2},{1,3},{2,0},{3,1},{4,6},{5,7},{6,4},{7,5},{8,10},{9,11},{10,... | collective-permute-start | bytes 294920 | tf_op jit(solution)/shard_map/ppermute | solution.py:17
  24.8 0.4 fusion.28
  25.3 0.3 add_subtract_fusion.1
  25.6 1.0 %collective-permute-start.14 = (f32[64,256]{1,0:T(8,128)S(1)}, f32[64,256]{1,0:T(8,128)S(1)}, u32[]{:S(2)}, u32[]{:S(2)}) collective-permute-start(f32[64,256]{1,0:T(8,128)S(1)} %add_subtract_fusion.1), channel_id=1, source_target_pairs={{0,3},{1,2},{2,1},{3,0},{4,7},{5,6},{6,5},{7,4},{8,11},{9,10},{10,... | collective-permute-start | bytes 196616 | tf_op jit(solution)/shard_map/ppermute | solution.py:17
  26.6 1.8 %collective-permute-done.17 = f32[1,48,512]{2,1,0:T(8,128)S(1)} collective-permute-done((f32[1,48,512]{2,1,0:T(8,128)S(1)}, f32[1,48,512]{2,1,0:T(8,128)S(1)}, u32[]{:S(2)}, u32[]{:S(2)}) %collective-permute-start.17) | collective-permute-done | bytes 98336 | tf_op jit(solution)/shard_map/ppermute | solution.py:17
  28.4 0.6 collective-permute-start.18
  29.0 0.5 collective-permute-done.14
  29.4 1.0 %collective-permute-start.15 = (f32[64,256]{1,0:T(8,128)S(1)}, f32[64,256]{1,0:T(8,128)S(1)}, u32[]{:S(2)}, u32[]{:S(2)}) collective-permute-start(f32[64,256]{1,0:T(8,128)S(1)} %add.45), channel_id=1, source_target_pairs={{0,5},{1,4},{2,7},{3,6},{4,1},{5,0},{6,3},{7,2},{8,13},{9,12},{10,... | collective-permute-start | bytes 196616 | tf_op jit(solution)/shard_map/ppermute | solution.py:17
  30.4 1.0 %fusion.93 = f32[256,256]{1,0:T(8,128)S(1)} fusion(f32[1024,256]{1,0:T(8,128)S(1)} %get-tuple-element.80, f32[1024,256]{1,0:T(8,128)S(1)} %get-tuple-element.76), kind=kOutput, calls=%fused_computation.117 | convolution fusion | flops 402653184 | bytes 2359296 | tf_op jit(solution)/shard_map/na,nb->ab/dot_general | solution.py:300
  31.4 0.4 collective-permute-start.22
  31.8 0.7 %convolution_subtract_fusion.1 = f32[128,1024]{1,0:T(8,128)S(1)} fusion(f32[128,1024]{1,0:T(8,128)S(1)} %convolution_subtract_fusion.2, f32[1024,256]{1,0:T(8,128)S(1)} %get-tuple-element.65, f32[64,256]{1,0:T(8,128)S(1)} %collective-permute-done.11, f32[64,256]{1,0:T(8,128)S(1)} %fusion.28, pred[]{:T(512)S(6)} %eq.18), kind=kOutput, calls=%fused_computation.1 | convolution fusion | flops 201555968 | bytes 2228225 | tf_op jit(solution)/shard_map/ka,na->kn/dot_general | solution.py:267
  32.4 1.8 %collective-permute-done.15 = f32[64,256]{1,0:T(8,128)S(1)} collective-permute-done((f32[64,256]{1,0:T(8,128)S(1)}, f32[64,256]{1,0:T(8,128)S(1)}, u32[]{:S(2)}, u32[]{:S(2)}) %collective-permute-start.15) | collective-permute-done | bytes 65568 | tf_op jit(solution)/shard_map/ppermute | solution.py:17
  34.2 1.0 %collective-permute-done.18 = f32[2,48,512]{2,1,0:T(8,128)S(1)} collective-permute-done((f32[2,48,512]{2,1,0:T(8,128)S(1)}, f32[2,48,512]{2,1,0:T(8,128)S(1)}, u32[]{:S(2)}, u32[]{:S(2)}) %collective-permute-start.18) | collective-permute-done | bytes 196640 | tf_op jit(solution)/shard_map/ppermute | solution.py:17
  35.3 0.6 collective-permute-start.19
  35.9 0.4 fusion.92
  36.4 1.7 %collective-permute-start.16 = (f32[64,256]{1,0:T(8,128)S(1)}, f32[64,256]{1,0:T(8,128)S(1)}, u32[]{:S(2)}, u32[]{:S(2)}) collective-permute-start(f32[64,256]{1,0:T(8,128)S(1)} %add.46), channel_id=1, source_target_pairs={{0,9},{1,8},{2,11},{3,10},{4,13},{5,12},{6,15},{7,14},{8,1},{9,0},... | collective-permute-start | bytes 196616 | tf_op jit(solution)/shard_map/ppermute | solution.py:17
  38.2 2.1 %collective-permute-done.16 = f32[64,256]{1,0:T(8,128)S(1)} collective-permute-done((f32[64,256]{1,0:T(8,128)S(1)}, f32[64,256]{1,0:T(8,128)S(1)}, u32[]{:S(2)}, u32[]{:S(2)}) %collective-permute-start.16) | collective-permute-done | bytes 65568 | tf_op jit(solution)/shard_map/ppermute | solution.py:17
  40.3 0.4 fusion.41
  40.7 0.3 add_subtract_fusion
  41.0 1.3 %collective-permute-start.23 = (f32[64,256]{1,0:T(8,128)S(1)}, f32[64,256]{1,0:T(8,128)S(1)}, u32[]{:S(2)}, u32[]{:S(2)}) collective-permute-start(f32[64,256]{1,0:T(8,128)S(1)} %add_subtract_fusion), channel_id=1, source_target_pairs={{0,3},{1,2},{2,1},{3,0},{4,7},{5,6},{6,5},{7,4},{8,11},{9,10},{10,... | collective-permute-start | bytes 196616 | tf_op jit(solution)/shard_map/ppermute | solution.py:17
  42.3 1.6 %collective-permute-start.27 = (f32[4,16,512]{2,1,0:T(8,128)S(1)}, f32[4,16,512]{2,1,0:T(8,128)S(1)}, u32[]{:S(2)}, u32[]{:S(2)}) collective-permute-start(f32[4,16,512]{2,1,0:T(8,128)S(1)} %slice.57), channel_id=1, source_target_pairs={{0,8},{1,9},{2,10},{3,11},{4,12},{5,13},{6,14},{7,15},{8,0},{9,1},... | collective-permute-start | bytes 393224 | tf_op jit(solution)/shard_map/ppermute | solution.py:17
  43.9 1.1 %collective-permute-done.23 = f32[64,256]{1,0:T(8,128)S(1)} collective-permute-done((f32[64,256]{1,0:T(8,128)S(1)}, f32[64,256]{1,0:T(8,128)S(1)}, u32[]{:S(2)}, u32[]{:S(2)}) %collective-permute-start.23) | collective-permute-done | bytes 65568 | tf_op jit(solution)/shard_map/ppermute | solution.py:17
  45.0 0.5 collective-permute-start.24
  45.5 0.2 collective-permute-start.20
  45.7 3.4 %collective-permute-done.24 = f32[64,256]{1,0:T(8,128)S(1)} collective-permute-done((f32[64,256]{1,0:T(8,128)S(1)}, f32[64,256]{1,0:T(8,128)S(1)}, u32[]{:S(2)}, u32[]{:S(2)}) %collective-permute-start.24) | collective-permute-done | bytes 65568 | tf_op jit(solution)/shard_map/ppermute | solution.py:17
  49.1 1.5 %collective-permute-start.25 = (f32[64,256]{1,0:T(8,128)S(1)}, f32[64,256]{1,0:T(8,128)S(1)}, u32[]{:S(2)}, u32[]{:S(2)}) collective-permute-start(f32[64,256]{1,0:T(8,128)S(1)} %add.50), channel_id=1, source_target_pairs={{0,9},{1,8},{2,11},{3,10},{4,13},{5,12},{6,15},{7,14},{8,1},{9,0},... | collective-permute-start | bytes 196616 | tf_op jit(solution)/shard_map/ppermute | solution.py:17
  50.6 0.3 collective-permute-start.28
  51.0 0.7 %convolution_subtract_fusion.x_ref = f32[128,1024]{1,0:T(8,128)S(1)} fusion(f32[128,1024]{1,0:T(8,128)S(1)} %convolution_subtract_fusion.1, f32[1024,256]{1,0:T(8,128)S(1)} %get-tuple-element.76, f32[64,256]{1,0:T(8,128)S(1)} %collective-permute-done.20, f32[64,256]{1,0:T(8,128)S(1)} %fusion.41, pred[]{:T(512)S(6)} %eq.18), kind=kOutput, calls=%fused_computation | convolution fusion | flops 201555968 | bytes 2228225 | tf_op jit(solution)/shard_map/ka,na->kn/dot_general | solution.py:267
  51.6 1.6 %collective-permute-done.25 = f32[64,256]{1,0:T(8,128)S(1)} collective-permute-done((f32[64,256]{1,0:T(8,128)S(1)}, f32[64,256]{1,0:T(8,128)S(1)}, u32[]{:S(2)}, u32[]{:S(2)}) %collective-permute-start.25) | collective-permute-done | bytes 65568 | tf_op jit(solution)/shard_map/ppermute | solution.py:17
  53.3 2.4 %collective-permute-start.26 = (f32[64,256]{1,0:T(8,128)S(1)}, f32[64,256]{1,0:T(8,128)S(1)}, u32[]{:S(2)}, u32[]{:S(2)}) collective-permute-start(f32[64,256]{1,0:T(8,128)S(1)} %add.51), channel_id=1, source_target_pairs={{0,17},{1,16},{2,19},{3,18},{4,21},{5,20},{6,23},{7,22},{8,25},{9,... | collective-permute-start | bytes 196616 | tf_op jit(solution)/shard_map/ppermute | solution.py:17
  55.8 2.5 %collective-permute-done.26 = f32[64,256]{1,0:T(8,128)S(1)} collective-permute-done((f32[64,256]{1,0:T(8,128)S(1)}, f32[64,256]{1,0:T(8,128)S(1)}, u32[]{:S(2)}, u32[]{:S(2)}) %collective-permute-start.26) | collective-permute-done | bytes 65568 | tf_op jit(solution)/shard_map/ppermute | solution.py:17
  58.3 0.4 fusion.54
  58.7 1.6 %collective-permute-start.29 = (f32[64,256]{1,0:T(8,128)S(1)}, f32[64,256]{1,0:T(8,128)S(1)}, u32[]{:S(2)}, u32[]{:S(2)}) collective-permute-start(f32[64,256]{1,0:T(8,128)S(1)} %fusion.54), channel_id=1, source_target_pairs={{0,1},{1,0},{2,3},{3,2},{4,5},{5,4},{6,7},{7,6},{8,9},{9,8},{10,11... | collective-permute-start | bytes 196616 | tf_op jit(solution)/shard_map/ppermute | solution.py:17
  60.3 0.9 %collective-permute-done.29 = f32[64,256]{1,0:T(8,128)S(1)} collective-permute-done((f32[64,256]{1,0:T(8,128)S(1)}, f32[64,256]{1,0:T(8,128)S(1)}, u32[]{:S(2)}, u32[]{:S(2)}) %collective-permute-start.29) | collective-permute-done | bytes 65568 | tf_op jit(solution)/shard_map/ppermute | solution.py:17
  61.2 1.4 %finish.1 = f32[1024,128]{1,0:T(8,128)} custom-call(f32[128,1024]{1,0:T(8,128)S(1)} %convolution_subtract_fusion.x_ref, f32[1024,256]{1,0:T(8,128)S(1)} %get-tuple-element.77.w_ref, f32[128,256]{1,0:T(8,128)S(1)} %maximum_select_fusion.19.t_ref), custom_call_target="tpu_custom_call" | custom-call | flops 201326592 | bytes 2097152 | tf_op jit(solution)/shard_map/finish/pallas_call | solution.py:144
  (44 shorter events, 0.7 us)
Async XLA Ops:
  3.1 1.5 %collective-permute-start = (f32[128,256]{1,0:T(8,128)S(1)}, f32[128,256]{1,0:T(8,128)S(1)}, u32[]{:S(2)}, u32[]{:S(2)}) collective-permute-start(f32[128,256]{1,0:T(8,128)S(1)} %get-tuple-element.48), channel_id=1, source_target_pairs={{0,1},{1,0},{2,3},{3,2},{4,5},{5,4},{6,7},{7,6},{8,9},{9,8},{10,11... | collective-permute-start | bytes 393224 | tf_op jit(solution)/shard_map/ppermute | solution.py:17
  6.1 3.1 %collective-permute-start.1 = (f32[64,256]{1,0:T(8,128)S(1)}, f32[64,256]{1,0:T(8,128)S(1)}, u32[]{:S(2)}, u32[]{:S(2)}) collective-permute-start(f32[64,256]{1,0:T(8,128)S(1)} %slice_select_fusion.3), channel_id=1, source_target_pairs={{0,1},{1,0},{2,3},{3,2},{4,5},{5,4},{6,7},{7,6},{8,9},{9,8},{10,11... | collective-permute-start | bytes 196616 | tf_op jit(solution)/shard_map/ppermute | solution.py:17
  6.5 11.7 %collective-permute-start.9 = (f32[1,64,512]{2,1,0:T(8,128)S(1)}, f32[1,64,512]{2,1,0:T(8,128)S(1)}, u32[]{:S(2)}, u32[]{:S(2)}) collective-permute-start(f32[1,64,512]{2,1,0:T(8,128)S(1)} %bitcast.44), channel_id=1, source_target_pairs={{0,2},{1,3},{2,0},{3,1},{4,6},{5,7},{6,4},{7,5},{8,10},{9,11},{10,... | collective-permute-start | bytes 393224 | tf_op jit(solution)/shard_map/ppermute | solution.py:17
  9.2 5.0 %collective-permute-start.3 = (f32[1,128,512]{2,1,0:T(8,128)S(1)}, f32[1,128,512]{2,1,0:T(8,128)S(1)}, u32[]{:S(2)}, u32[]{:S(2)}) collective-permute-start(f32[1,128,512]{2,1,0:T(8,128)S(1)} %bitcast.42), channel_id=1, source_target_pairs={{0,1},{1,0},{2,3},{3,2},{4,5},{5,4},{6,7},{7,6},{8,9},{9,8},{10,11... | collective-permute-start | bytes 786440 | tf_op jit(solution)/shard_map/ppermute | solution.py:17
  10.7 3.9 %collective-permute-start.2 = (f32[64,256]{1,0:T(8,128)S(1)}, f32[64,256]{1,0:T(8,128)S(1)}, u32[]{:S(2)}, u32[]{:S(2)}) collective-permute-start(f32[64,256]{1,0:T(8,128)S(1)} %select_add_fusion._), channel_id=1, source_target_pairs={{0,3},{1,2},{2,1},{3,0},{4,7},{5,6},{6,5},{7,4},{8,11},{9,10},{10,... | collective-permute-start | bytes 196616 | tf_op jit(solution)/shard_map/ppermute | solution.py:17
  13.5 2.0 %collective-permute-start.6 = (f32[256,256]{1,0:T(8,128)S(1)}, f32[256,256]{1,0:T(8,128)S(1)}, u32[]{:S(2)}, u32[]{:S(2)}) collective-permute-start(f32[256,256]{1,0:T(8,128)S(1)} %fusion.89), channel_id=1, source_target_pairs={{0,1},{1,0},{2,3},{3,2},{4,5},{5,4},{6,7},{7,6},{8,9},{9,8},{10,11... | collective-permute-start | bytes 786440 | tf_op jit(solution)/shard_map/ppermute | solution.py:17
  13.7 1.7 %collective-permute-start.5 = (f32[64,256]{1,0:T(8,128)S(1)}, f32[64,256]{1,0:T(8,128)S(1)}, u32[]{:S(2)}, u32[]{:S(2)}) collective-permute-start(f32[64,256]{1,0:T(8,128)S(1)} %slice_select_fusion.2), channel_id=1, source_target_pairs={{0,1},{1,0},{2,3},{3,2},{4,5},{5,4},{6,7},{7,6},{8,9},{9,8},{10,11... | collective-permute-start | bytes 196616 | tf_op jit(solution)/shard_map/ppermute | solution.py:17
  15.0 3.5 %collective-permute-start.4 = (f32[64,256]{1,0:T(8,128)S(1)}, f32[64,256]{1,0:T(8,128)S(1)}, u32[]{:S(2)}, u32[]{:S(2)}) collective-permute-start(f32[64,256]{1,0:T(8,128)S(1)} %fusion.15), channel_id=1, source_target_pairs={{0,1},{1,0},{2,3},{3,2},{4,5},{5,4},{6,7},{7,6},{8,9},{9,8},{10,11... | collective-permute-start | bytes 196616 | tf_op jit(solution)/shard_map/ppermute | solution.py:17
  15.7 4.2 %collective-permute-start.7 = (f32[64,256]{1,0:T(8,128)S(1)}, f32[64,256]{1,0:T(8,128)S(1)}, u32[]{:S(2)}, u32[]{:S(2)}) collective-permute-start(f32[64,256]{1,0:T(8,128)S(1)} %add_subtract_fusion.2), channel_id=1, source_target_pairs={{0,3},{1,2},{2,1},{3,0},{4,7},{5,6},{6,5},{7,4},{8,11},{9,10},{10,... | collective-permute-start | bytes 196616 | tf_op jit(solution)/shard_map/ppermute | solution.py:17
  17.8 7.5 %collective-permute-start.13 = (f32[256,256]{1,0:T(8,128)S(1)}, f32[256,256]{1,0:T(8,128)S(1)}, u32[]{:S(2)}, u32[]{:S(2)}) collective-permute-start(f32[256,256]{1,0:T(8,128)S(1)} %fusion.91), channel_id=1, source_target_pairs={{0,1},{1,0},{2,3},{3,2},{4,5},{5,4},{6,7},{7,6},{8,9},{9,8},{10,11... | collective-permute-start | bytes 786440 | tf_op jit(solution)/shard_map/ppermute | solution.py:17
  18.2 6.6 %collective-permute-start.10 = (f32[2,64,512]{2,1,0:T(8,128)S(1)}, f32[2,64,512]{2,1,0:T(8,128)S(1)}, u32[]{:S(2)}, u32[]{:S(2)}) collective-permute-start(f32[2,64,512]{2,1,0:T(8,128)S(1)} %maximum_select_fusion.6), channel_id=1, source_target_pairs={{0,1},{1,0},{2,3},{3,2},{4,5},{5,4},{6,7},{7,6},{8,9},{9,8},{10,11... | collective-permute-start | bytes 786440 | tf_op jit(solution)/shard_map/ppermute | solution.py:17
  19.9 4.9 %collective-permute-start.8 = (f32[64,256]{1,0:T(8,128)S(1)}, f32[64,256]{1,0:T(8,128)S(1)}, u32[]{:S(2)}, u32[]{:S(2)}) collective-permute-start(f32[64,256]{1,0:T(8,128)S(1)} %add.42._), channel_id=1, source_target_pairs={{0,5},{1,4},{2,7},{3,6},{4,1},{5,0},{6,3},{7,2},{8,13},{9,12},{10,... | collective-permute-start | bytes 196616 | tf_op jit(solution)/shard_map/ppermute | solution.py:17
  23.1 2.2 %collective-permute-start.12 = (f32[64,256]{1,0:T(8,128)S(1)}, f32[64,256]{1,0:T(8,128)S(1)}, u32[]{:S(2)}, u32[]{:S(2)}) collective-permute-start(f32[64,256]{1,0:T(8,128)S(1)} %slice_select_fusion.1), channel_id=1, source_target_pairs={{0,1},{1,0},{2,3},{3,2},{4,5},{5,4},{6,7},{7,6},{8,9},{9,8},{10,11... | collective-permute-start | bytes 196616 | tf_op jit(solution)/shard_map/ppermute | solution.py:17
  23.6 4.8 %collective-permute-start.17 = (f32[1,48,512]{2,1,0:T(8,128)S(1)}, f32[1,48,512]{2,1,0:T(8,128)S(1)}, u32[]{:S(2)}, u32[]{:S(2)}) collective-permute-start(f32[1,48,512]{2,1,0:T(8,128)S(1)} %bitcast.46), channel_id=1, source_target_pairs={{0,2},{1,3},{2,0},{3,1},{4,6},{5,7},{6,4},{7,5},{8,10},{9,11},{10,... | collective-permute-start | bytes 294920 | tf_op jit(solution)/shard_map/ppermute | solution.py:17
  25.2 6.6 %collective-permute-start.11 = (f32[64,256]{1,0:T(8,128)S(1)}, f32[64,256]{1,0:T(8,128)S(1)}, u32[]{:S(2)}, u32[]{:S(2)}) collective-permute-start(f32[64,256]{1,0:T(8,128)S(1)} %fusion.28), channel_id=1, source_target_pairs={{0,1},{1,0},{2,3},{3,2},{4,5},{5,4},{6,7},{7,6},{8,9},{9,8},{10,11... | collective-permute-start | bytes 196616 | tf_op jit(solution)/shard_map/ppermute | solution.py:17
  25.6 3.8 %collective-permute-start.14 = (f32[64,256]{1,0:T(8,128)S(1)}, f32[64,256]{1,0:T(8,128)S(1)}, u32[]{:S(2)}, u32[]{:S(2)}) collective-permute-start(f32[64,256]{1,0:T(8,128)S(1)} %add_subtract_fusion.1), channel_id=1, source_target_pairs={{0,3},{1,2},{2,1},{3,0},{4,7},{5,6},{6,5},{7,4},{8,11},{9,10},{10,... | collective-permute-start | bytes 196616 | tf_op jit(solution)/shard_map/ppermute | solution.py:17
  28.4 6.9 %collective-permute-start.18 = (f32[2,48,512]{2,1,0:T(8,128)S(1)}, f32[2,48,512]{2,1,0:T(8,128)S(1)}, u32[]{:S(2)}, u32[]{:S(2)}) collective-permute-start(f32[2,48,512]{2,1,0:T(8,128)S(1)} %maximum_select_fusion.8), channel_id=1, source_target_pairs={{0,4},{1,5},{2,6},{3,7},{4,0},{5,1},{6,2},{7,3},{8,12},{9,13},{10,... | collective-permute-start | bytes 589832 | tf_op jit(solution)/shard_map/ppermute | solution.py:17
  29.4 4.8 %collective-permute-start.15 = (f32[64,256]{1,0:T(8,128)S(1)}, f32[64,256]{1,0:T(8,128)S(1)}, u32[]{:S(2)}, u32[]{:S(2)}) collective-permute-start(f32[64,256]{1,0:T(8,128)S(1)} %add.45), channel_id=1, source_target_pairs={{0,5},{1,4},{2,7},{3,6},{4,1},{5,0},{6,3},{7,2},{8,13},{9,12},{10,... | collective-permute-start | bytes 196616 | tf_op jit(solution)/shard_map/ppermute | solution.py:17
  31.4 9.3 %collective-permute-start.22 = (f32[256,256]{1,0:T(8,128)S(1)}, f32[256,256]{1,0:T(8,128)S(1)}, u32[]{:S(2)}, u32[]{:S(2)}) collective-permute-start(f32[256,256]{1,0:T(8,128)S(1)} %fusion.93), channel_id=1, source_target_pairs={{0,1},{1,0},{2,3},{3,2},{4,5},{5,4},{6,7},{7,6},{8,9},{9,8},{10,11... | collective-permute-start | bytes 786440 | tf_op jit(solution)/shard_map/ppermute | solution.py:17
  35.3 2.8 %collective-permute-start.19 = (f32[4,32,512]{2,1,0:T(8,128)S(1)}, f32[4,32,512]{2,1,0:T(8,128)S(1)}, u32[]{:S(2)}, u32[]{:S(2)}) collective-permute-start(f32[4,32,512]{2,1,0:T(8,128)S(1)} %slice.54), channel_id=1, source_target_pairs={{0,1},{1,0},{2,3},{3,2},{4,5},{5,4},{6,7},{7,6},{8,9},{9,8},{10,11... | collective-permute-start | bytes 786440 | tf_op jit(solution)/shard_map/ppermute | solution.py:17
  36.4 4.3 %collective-permute-start.21 = (f32[64,256]{1,0:T(8,128)S(1)}, f32[64,256]{1,0:T(8,128)S(1)}, u32[]{:S(2)}, u32[]{:S(2)}) collective-permute-start(f32[64,256]{1,0:T(8,128)S(1)} %slice_select_fusion), channel_id=1, source_target_pairs={{0,1},{1,0},{2,3},{3,2},{4,5},{5,4},{6,7},{7,6},{8,9},{9,8},{10,11... | collective-permute-start | bytes 196616 | tf_op jit(solution)/shard_map/ppermute | solution.py:17
  36.4 3.9 %collective-permute-start.16 = (f32[64,256]{1,0:T(8,128)S(1)}, f32[64,256]{1,0:T(8,128)S(1)}, u32[]{:S(2)}, u32[]{:S(2)}) collective-permute-start(f32[64,256]{1,0:T(8,128)S(1)} %add.46), channel_id=1, source_target_pairs={{0,9},{1,8},{2,11},{3,10},{4,13},{5,12},{6,15},{7,14},{8,1},{9,0},... | collective-permute-start | bytes 196616 | tf_op jit(solution)/shard_map/ppermute | solution.py:17
  41.0 4.0 %collective-permute-start.23 = (f32[64,256]{1,0:T(8,128)S(1)}, f32[64,256]{1,0:T(8,128)S(1)}, u32[]{:S(2)}, u32[]{:S(2)}) collective-permute-start(f32[64,256]{1,0:T(8,128)S(1)} %add_subtract_fusion), channel_id=1, source_target_pairs={{0,3},{1,2},{2,1},{3,0},{4,7},{5,6},{6,5},{7,4},{8,11},{9,10},{10,... | collective-permute-start | bytes 196616 | tf_op jit(solution)/shard_map/ppermute | solution.py:17
  42.3 8.3 %collective-permute-start.27 = (f32[4,16,512]{2,1,0:T(8,128)S(1)}, f32[4,16,512]{2,1,0:T(8,128)S(1)}, u32[]{:S(2)}, u32[]{:S(2)}) collective-permute-start(f32[4,16,512]{2,1,0:T(8,128)S(1)} %slice.57), channel_id=1, source_target_pairs={{0,8},{1,9},{2,10},{3,11},{4,12},{5,13},{6,14},{7,15},{8,0},{9,1},... | collective-permute-start | bytes 393224 | tf_op jit(solution)/shard_map/ppermute | solution.py:17
  45.0 4.1 %collective-permute-start.24 = (f32[64,256]{1,0:T(8,128)S(1)}, f32[64,256]{1,0:T(8,128)S(1)}, u32[]{:S(2)}, u32[]{:S(2)}) collective-permute-start(f32[64,256]{1,0:T(8,128)S(1)} %add.49), channel_id=1, source_target_pairs={{0,5},{1,4},{2,7},{3,6},{4,1},{5,0},{6,3},{7,2},{8,13},{9,12},{10,... | collective-permute-start | bytes 196616 | tf_op jit(solution)/shard_map/ppermute | solution.py:17
  45.5 5.4 %collective-permute-start.20 = (f32[64,256]{1,0:T(8,128)S(1)}, f32[64,256]{1,0:T(8,128)S(1)}, u32[]{:S(2)}, u32[]{:S(2)}) collective-permute-start(f32[64,256]{1,0:T(8,128)S(1)} %fusion.41), channel_id=1, source_target_pairs={{0,1},{1,0},{2,3},{3,2},{4,5},{5,4},{6,7},{7,6},{8,9},{9,8},{10,11... | collective-permute-start | bytes 196616 | tf_op jit(solution)/shard_map/ppermute | solution.py:17
  49.1 4.1 %collective-permute-start.25 = (f32[64,256]{1,0:T(8,128)S(1)}, f32[64,256]{1,0:T(8,128)S(1)}, u32[]{:S(2)}, u32[]{:S(2)}) collective-permute-start(f32[64,256]{1,0:T(8,128)S(1)} %add.50), channel_id=1, source_target_pairs={{0,9},{1,8},{2,11},{3,10},{4,13},{5,12},{6,15},{7,14},{8,1},{9,0},... | collective-permute-start | bytes 196616 | tf_op jit(solution)/shard_map/ppermute | solution.py:17
  50.6 5.1 %collective-permute-start.28 = (f32[8,16,512]{2,1,0:T(8,128)S(1)}, f32[8,16,512]{2,1,0:T(8,128)S(1)}, u32[]{:S(2)}, u32[]{:S(2)}) collective-permute-start(f32[8,16,512]{2,1,0:T(8,128)S(1)} %maximum_select_fusion.7), channel_id=1, source_target_pairs={{0,1},{1,0},{2,3},{3,2},{4,5},{5,4},{6,7},{7,6},{8,9},{9,8},{10,11... | collective-permute-start | bytes 786440 | tf_op jit(solution)/shard_map/ppermute | solution.py:17
  53.3 5.0 %collective-permute-start.26 = (f32[64,256]{1,0:T(8,128)S(1)}, f32[64,256]{1,0:T(8,128)S(1)}, u32[]{:S(2)}, u32[]{:S(2)}) collective-permute-start(f32[64,256]{1,0:T(8,128)S(1)} %add.51), channel_id=1, source_target_pairs={{0,17},{1,16},{2,19},{3,18},{4,21},{5,20},{6,23},{7,22},{8,25},{9,... | collective-permute-start | bytes 196616 | tf_op jit(solution)/shard_map/ppermute | solution.py:17
  58.7 2.5 %collective-permute-start.29 = (f32[64,256]{1,0:T(8,128)S(1)}, f32[64,256]{1,0:T(8,128)S(1)}, u32[]{:S(2)}, u32[]{:S(2)}) collective-permute-start(f32[64,256]{1,0:T(8,128)S(1)} %fusion.54), channel_id=1, source_target_pairs={{0,1},{1,0},{2,3},{3,2},{4,5},{5,4},{6,7},{7,6},{8,9},{9,8},{10,11... | collective-permute-start | bytes 196616 | tf_op jit(solution)/shard_map/ppermute | solution.py:17

commit v5 on v4

--- a/solution.py
+++ b/solution.py
@@ -57,14 +57,14 @@
 def begin(rhs, proj_bases, corr_bases, cores, first, leaf_core, groups):
     rows, width = rhs.shape
     rank = proj_bases.shape[2]
-    shapes = [(width, rank), (width, rows)] + [(rows, rank)] * 4
+    shapes = [(width, rank), (width, rows)] + [(rows, rank)] * 6
     shapes += [(rank, 2 * rank)] if leaf_core else []
     shapes += [(sum(n for _, n in group), 2 * rank) for group in groups]
 
     def body(x_hbm, p_hbm, w_hbm, c_hbm, *refs):
         outs, (x_ref, p_ref, sems) = list(refs[: len(shapes)]), refs[len(shapes) :]
-        q_out, state_out, w_out, p_out, w_next, p_next = outs[:6]
-        rest = outs[6:]
+        q_out, state_out, w_out, p_out, w_next, p_next, w_third, p_third = outs[:8]
+        rest = outs[8:]
         moves = [(x_hbm, x_ref), (p_hbm.at[first], p_ref)]
         if leaf_core:
             moves.append((c_hbm.at[first], rest.pop(0)))
@@ -75,6 +75,7 @@
                 moves.append((c_hbm.at[level, 0:n], out.at[start : start + n]))
                 start += n
         moves += [(w_hbm.at[first - 1], w_next), (p_hbm.at[first - 2], p_next)]
+        moves += [(w_hbm.at[first - 2], w_third), (p_hbm.at[first - 3], p_third)]
         copies = [pltpu.make_async_copy(a, b, sems.at[at]) for at, (a, b) in enumerate(moves)]
         for copy in copies:
             copy.start()
@@ -86,7 +87,7 @@
         for copy in copies[2:]:
             copy.wait()
 
-    count = 6 + (1 if leaf_core else 0) + sum(len(group) for group in groups)
+    count = 8 + (1 if leaf_core else 0) + sum(len(group) for group in groups)
     return pl.pallas_call(
         body,
         in_specs=[IN_HBM] * 4,
@@ -190,7 +191,7 @@
     far = [item for item in tails if item not in near]
     groups = [group for group in (heads, near, far) if group]
     leaf_core = bits[first] == 0
-    value, state, top_corr, next_proj, corr, proj, *fetched = begin(
+    value, state, top_corr, next_proj, corr, proj, third_corr, third_proj, *fetched = begin(
         rhs, proj_bases, corr_bases, cores, first, leaf_core, groups
     )
 
@@ -286,7 +287,7 @@
             for _ in range(3):
                 step(start)
         if level == first - 1:
-            later.append(fetch(proj_bases, corr_bases, [level - 2], [level - 1], start))
+            later.append((third_proj, third_corr))
         if level == first - 2:
             fetch_rest = lambda v: fetch(
                 proj_bases, corr_bases, list(reversed(range(level - 1))), list(reversed(range(level))), v

time: 62.7 us -> 63.3 us (level)
  waiting for transfers between devices: 18.5 us -> 19.9 us
  Pallas kernels: 7.84 us -> 6.9 us
    pallas_call x2 -> x1, Pallas kernels: 3.44 us -> 1.88 us  [fetch(): pl.pallas_call(body, in_specs=[IN_HBM, IN_HBM, pl.BlockSpec(memory_space=...]
    ppermute x30, waiting for transfers between devices: 18.5 us -> 19.9 us  [exchange(): return lax.ppermute(value, 'leaf', pairs)]
  transfers between devices with their start and end apart: 30 -> 30, of which waited for: 13 -> 12; matrix products, arithmetic and copies ran while one was open for 13% -> 13% of each run, Pallas kernels for 5% -> 3%
where the time goes in v5:
time: 63.3 us; the launch traced here: 63.2 us
  starting transfers between devices  25.5 us (40%)
  waiting for transfers between devices  19.9 us (31%)
  matrix products  9.97 us (16%)
  Pallas kernels  6.9 us (11%)
    ppermute x30, starting transfers between devices, exchange(): return lax.ppermute(value, 'leaf', pairs)  25.5 us
    ppermute x30, waiting for transfers between devices, exchange(): return lax.ppermute(value, 'leaf', pairs)  19.9 us
    pallas_call x1, Pallas kernels, begin(): pl.pallas_call(body, in_specs=[IN_HBM] * 4, out_specs=[IN_VMEM] * len(sha...  3.66 us
    dot_general x3, matrix products, on_device(): own = jnp.einsum('na,nb->ab', proj, corr, precision=HIGH)  2.98 us
    dot_general x8, matrix products, times_transposed(): return jnp.einsum('kb,ab->ka', left, right, precision=HIGH)  2.74 us
    dot_general x4, matrix products, update(): return state - jnp.einsum('ka,na->kn', held, corr, precision=HIGH)  2.63 us
    pallas_call x1, Pallas kernels, fetch(): pl.pallas_call(body, in_specs=[IN_HBM, IN_HBM, pl.BlockSpec(memory_space=...  1.88 us
    dot_general x4, matrix products, project(): return jnp.einsum('kn,nr->kr', state, basis, precision=HIGH)  1.62 us
  transfers between devices with their start and end apart: 30, of which 12 were waited for; matrix products, arithmetic and copies ran while one was open for 13% of the time, Pallas kernels for 3%

profile of v5, /device:TPU:0, one launch (start us, length us, event | category | flops | bytes accessed | tf_op | source)
XLA Modules:
  0.0 63.2 jit_solution(17794520702615969277)
XLA Ops:
  0.0 3.7 %begin.1 = (f32[128,256]{1,0:T(8,128)S(1)}, f32[128,1024]{1,0:T(8,128)S(1)}, f32[1024,256]{1,0:T(8,128)S(1)}, f32[1024,256]{1,0:T(8,128)S(1)}, f32[1024,256]{1,0...) custom-call(f32[1024,128]{1,0:T(8,128)} %x_hbm, ...), custom_call_target="tpu_custom_call" | custom-call | flops 201326592 | bytes 4194304 | tf_op jit(solution)/shard_map/begin/pallas_call | solution.py:91
  3.7 0.5 collective-permute-start
  4.2 1.0 %collective-permute-done = f32[128,256]{1,0:T(8,128)S(1)} collective-permute-done((f32[128,256]{1,0:T(8,128)S(1)}, f32[128,256]{1,0:T(8,128)S(1)}, u32[]{:S(2)}, u32[]{:S(2)}) %collective-permute-start) | collective-permute-done | bytes 131104 | tf_op jit(solution)/shard_map/ppermute | solution.py:17
  5.2 0.4 fusion.1
  5.6 0.7 %convolution_subtract_fusion.3 = f32[128,1024]{1,0:T(8,128)S(1)} fusion(f32[128,1024]{1,0:T(8,128)S(1)} %get-tuple-element.46, f32[128,256]{1,0:T(8,128)S(1)} %fusion.1, f32[1024,256]{1,0:T(8,128)S(1)} %get-tuple-element.50), kind=kOutput, calls=%fused_computation.3 | convolution fusion | flops 201457664 | bytes 2228224 | tf_op jit(solution)/shard_map/ka,na->kn/dot_general | solution.py:268
  6.2 0.4 fusion.87
  6.7 0.4 collective-permute-start.1
  7.1 2.6 %collective-permute-start.9 = (f32[1,64,512]{2,1,0:T(8,128)S(1)}, f32[1,64,512]{2,1,0:T(8,128)S(1)}, u32[]{:S(2)}, u32[]{:S(2)}) collective-permute-start(f32[1,64,512]{2,1,0:T(8,128)S(1)} %bitcast.44), channel_id=1, source_target_pairs={{0,2},{1,3},{2,0},{3,1},{4,6},{5,7},{6,4},{7,5},{8,10},{9,11},{10,... | collective-permute-start | bytes 393224 | tf_op jit(solution)/shard_map/ppermute | solution.py:17
  9.8 0.9 %collective-permute-start.2 = (f32[64,256]{1,0:T(8,128)S(1)}, f32[64,256]{1,0:T(8,128)S(1)}, u32[]{:S(2)}, u32[]{:S(2)}) collective-permute-start(f32[64,256]{1,0:T(8,128)S(1)} %select_add_fusion), channel_id=1, source_target_pairs={{0,3},{1,2},{2,1},{3,0},{4,7},{5,6},{6,5},{7,4},{8,11},{9,10},{10,... | collective-permute-start | bytes 196616 | tf_op jit(solution)/shard_map/ppermute | solution.py:17
  10.7 0.4 fusion.88
  11.1 0.4 collective-permute-start.3
  11.5 1.0 %fusion.89 = f32[256,256]{1,0:T(8,128)S(1)} fusion(f32[1024,256]{1,0:T(8,128)S(1)} %get-tuple-element.60, f32[1024,256]{1,0:T(8,128)S(1)} %get-tuple-element.57), kind=kOutput, calls=%fused_computation.113 | convolution fusion | flops 402653184 | bytes 2359296 | tf_op jit(solution)/shard_map/na,nb->ab/dot_general | solution.py:301
  12.5 0.2 collective-permute-start.6
  12.7 0.4 collective-permute-start.5
  13.2 1.6 %collective-permute-done.2 = f32[64,256]{1,0:T(8,128)S(1)} collective-permute-done((f32[64,256]{1,0:T(8,128)S(1)}, f32[64,256]{1,0:T(8,128)S(1)}, u32[]{:S(2)}, u32[]{:S(2)}) %collective-permute-start.2) | collective-permute-done | bytes 65568 | tf_op jit(solution)/shard_map/ppermute | solution.py:17
  14.8 0.4 fusion.15
  15.2 0.2 collective-permute-start.4
  15.4 0.3 add_subtract_fusion.2
  15.7 1.5 %collective-permute-start.7 = (f32[64,256]{1,0:T(8,128)S(1)}, f32[64,256]{1,0:T(8,128)S(1)}, u32[]{:S(2)}, u32[]{:S(2)}) collective-permute-start(f32[64,256]{1,0:T(8,128)S(1)} %add_subtract_fusion.2), channel_id=1, source_target_pairs={{0,3},{1,2},{2,1},{3,0},{4,7},{5,6},{6,5},{7,4},{8,11},{9,10},{10,... | collective-permute-start | bytes 196616 | tf_op jit(solution)/shard_map/ppermute | solution.py:17
  17.2 1.0 %fusion.91 = f32[256,256]{1,0:T(8,128)S(1)} fusion(f32[1024,256]{1,0:T(8,128)S(1)} %get-tuple-element.68, f32[1024,256]{1,0:T(8,128)S(1)} %get-tuple-element.65), kind=kOutput, calls=%fused_computation.115 | convolution fusion | flops 402653184 | bytes 2359296 | tf_op jit(solution)/shard_map/na,nb->ab/dot_general | solution.py:301
  18.2 0.5 collective-permute-start.13
  18.7 0.2 collective-permute-start.10
  18.9 0.7 %convolution_subtract_fusion.2 = f32[128,1024]{1,0:T(8,128)S(1)} fusion(f32[128,1024]{1,0:T(8,128)S(1)} %convolution_subtract_fusion.3, f32[1024,256]{1,0:T(8,128)S(1)} %get-tuple-element.57, f32[64,256]{1,0:T(8,128)S(1)} %collective-permute-done.4, f32[64,256]{1,0:T(8,128)S(1)} %fusion.15, pred[]{:T(512)S(6)} %eq.18), kind=kOutput, calls=%fused_computation.2 | convolution fusion | flops 201555968 | bytes 2228225 | tf_op jit(solution)/shard_map/ka,na->kn/dot_general | solution.py:268
  19.6 0.4 fusion.90
  20.0 1.6 %collective-permute-start.8 = (f32[64,256]{1,0:T(8,128)S(1)}, f32[64,256]{1,0:T(8,128)S(1)}, u32[]{:S(2)}, u32[]{:S(2)}) collective-permute-start(f32[64,256]{1,0:T(8,128)S(1)} %add.42._), channel_id=1, source_target_pairs={{0,5},{1,4},{2,7},{3,6},{4,1},{5,0},{6,3},{7,2},{8,13},{9,12},{10,... | collective-permute-start | bytes 196616 | tf_op jit(solution)/shard_map/ppermute | solution.py:17
  21.6 1.9 %fetch.1 = (f32[1024,256]{1,0:T(8,128)S(1)}, f32[1024,256]{1,0:T(8,128)S(1)}, f32[1024,256]{1,0:T(8,128)S(1)}) custom-call(f32[5,1024,256]{2,1,0:T(8,128)} %p_hbm.3, f32[5,1024,256]{2,1,0:T(8,128)} %w_hbm.3, f32[64,256]{1,0:T(8,128)S(1)} %add.42._), custom_call_target="tpu_custom_call" | custom-call | bytes 65536 | tf_op jit(solution)/shard_map/fetch/pallas_call | solution.py:125
  23.5 0.3 collective-permute-start.12
  23.8 1.5 %collective-permute-start.17 = (f32[1,48,512]{2,1,0:T(8,128)S(1)}, f32[1,48,512]{2,1,0:T(8,128)S(1)}, u32[]{:S(2)}, u32[]{:S(2)}) collective-permute-start(f32[1,48,512]{2,1,0:T(8,128)S(1)} %bitcast.46), channel_id=1, source_target_pairs={{0,2},{1,3},{2,0},{3,1},{4,6},{5,7},{6,4},{7,5},{8,10},{9,11},{10,... | collective-permute-start | bytes 294920 | tf_op jit(solution)/shard_map/ppermute | solution.py:17
  25.4 0.4 fusion.28
  25.8 0.1 collective-permute-start.11
  25.9 0.3 add_subtract_fusion.1
  26.2 0.7 %collective-permute-start.14 = (f32[64,256]{1,0:T(8,128)S(1)}, f32[64,256]{1,0:T(8,128)S(1)}, u32[]{:S(2)}, u32[]{:S(2)}) collective-permute-start(f32[64,256]{1,0:T(8,128)S(1)} %add_subtract_fusion.1), channel_id=1, source_target_pairs={{0,3},{1,2},{2,1},{3,0},{4,7},{5,6},{6,5},{7,4},{8,11},{9,10},{10,... | collective-permute-start | bytes 196616 | tf_op jit(solution)/shard_map/ppermute | solution.py:17
  26.8 1.9 %collective-permute-done.17 = f32[1,48,512]{2,1,0:T(8,128)S(1)} collective-permute-done((f32[1,48,512]{2,1,0:T(8,128)S(1)}, f32[1,48,512]{2,1,0:T(8,128)S(1)}, u32[]{:S(2)}, u32[]{:S(2)}) %collective-permute-start.17) | collective-permute-done | bytes 98336 | tf_op jit(solution)/shard_map/ppermute | solution.py:17
  28.8 0.6 collective-permute-start.18
  29.4 0.6 %collective-permute-done.14 = f32[64,256]{1,0:T(8,128)S(1)} collective-permute-done((f32[64,256]{1,0:T(8,128)S(1)}, f32[64,256]{1,0:T(8,128)S(1)}, u32[]{:S(2)}, u32[]{:S(2)}) %collective-permute-start.14) | collective-permute-done | bytes 65568 | tf_op jit(solution)/shard_map/ppermute | solution.py:17
  30.0 0.6 collective-permute-start.15
  30.6 1.0 %fusion.93 = f32[256,256]{1,0:T(8,128)S(1)} fusion(f32[1024,256]{1,0:T(8,128)S(1)} %get-tuple-element.80, f32[1024,256]{1,0:T(8,128)S(1)} %get-tuple-element.76), kind=kOutput, calls=%fused_computation.117 | convolution fusion | flops 402653184 | bytes 2359296 | tf_op jit(solution)/shard_map/na,nb->ab/dot_general | solution.py:301
  31.6 0.5 collective-permute-start.22
  32.2 0.7 %convolution_subtract_fusion.1 = f32[128,1024]{1,0:T(8,128)S(1)} fusion(f32[128,1024]{1,0:T(8,128)S(1)} %convolution_subtract_fusion.2, f32[1024,256]{1,0:T(8,128)S(1)} %get-tuple-element.65, f32[64,256]{1,0:T(8,128)S(1)} %collective-permute-done.11, f32[64,256]{1,0:T(8,128)S(1)} %fusion.28, pred[]{:T(512)S(6)} %eq.18), kind=kOutput, calls=%fused_computation.1 | convolution fusion | flops 201555968 | bytes 2228225 | tf_op jit(solution)/shard_map/ka,na->kn/dot_general | solution.py:268
  32.8 2.2 %collective-permute-done.15 = f32[64,256]{1,0:T(8,128)S(1)} collective-permute-done((f32[64,256]{1,0:T(8,128)S(1)}, f32[64,256]{1,0:T(8,128)S(1)}, u32[]{:S(2)}, u32[]{:S(2)}) %collective-permute-start.15) | collective-permute-done | bytes 65568 | tf_op jit(solution)/shard_map/ppermute | solution.py:17
  35.0 0.8 %collective-permute-done.18 = f32[2,48,512]{2,1,0:T(8,128)S(1)} collective-permute-done((f32[2,48,512]{2,1,0:T(8,128)S(1)}, f32[2,48,512]{2,1,0:T(8,128)S(1)}, u32[]{:S(2)}, u32[]{:S(2)}) %collective-permute-start.18) | collective-permute-done | bytes 196640 | tf_op jit(solution)/shard_map/ppermute | solution.py:17
  35.9 0.6 collective-permute-start.19
  36.6 0.4 fusion.92
  37.0 0.1 collective-permute-start.21
  37.1 1.7 %collective-permute-start.16 = (f32[64,256]{1,0:T(8,128)S(1)}, f32[64,256]{1,0:T(8,128)S(1)}, u32[]{:S(2)}, u32[]{:S(2)}) collective-permute-start(f32[64,256]{1,0:T(8,128)S(1)} %add.46), channel_id=1, source_target_pairs={{0,9},{1,8},{2,11},{3,10},{4,13},{5,12},{6,15},{7,14},{8,1},{9,0},... | collective-permute-start | bytes 196616 | tf_op jit(solution)/shard_map/ppermute | solution.py:17
  38.8 2.1 %collective-permute-done.16 = f32[64,256]{1,0:T(8,128)S(1)} collective-permute-done((f32[64,256]{1,0:T(8,128)S(1)}, f32[64,256]{1,0:T(8,128)S(1)}, u32[]{:S(2)}, u32[]{:S(2)}) %collective-permute-start.16) | collective-permute-done | bytes 65568 | tf_op jit(solution)/shard_map/ppermute | solution.py:17
  40.9 0.4 fusion.41
  41.3 0.3 add_subtract_fusion
  41.6 1.2 %collective-permute-start.23 = (f32[64,256]{1,0:T(8,128)S(1)}, f32[64,256]{1,0:T(8,128)S(1)}, u32[]{:S(2)}, u32[]{:S(2)}) collective-permute-start(f32[64,256]{1,0:T(8,128)S(1)} %add_subtract_fusion), channel_id=1, source_target_pairs={{0,3},{1,2},{2,1},{3,0},{4,7},{5,6},{6,5},{7,4},{8,11},{9,10},{10,... | collective-permute-start | bytes 196616 | tf_op jit(solution)/shard_map/ppermute | solution.py:17
  42.8 1.6 %collective-permute-start.27 = (f32[4,16,512]{2,1,0:T(8,128)S(1)}, f32[4,16,512]{2,1,0:T(8,128)S(1)}, u32[]{:S(2)}, u32[]{:S(2)}) collective-permute-start(f32[4,16,512]{2,1,0:T(8,128)S(1)} %slice.57), channel_id=1, source_target_pairs={{0,8},{1,9},{2,10},{3,11},{4,12},{5,13},{6,14},{7,15},{8,0},{9,1},... | collective-permute-start | bytes 393224 | tf_op jit(solution)/shard_map/ppermute | solution.py:17
  44.5 1.2 %collective-permute-done.23 = f32[64,256]{1,0:T(8,128)S(1)} collective-permute-done((f32[64,256]{1,0:T(8,128)S(1)}, f32[64,256]{1,0:T(8,128)S(1)}, u32[]{:S(2)}, u32[]{:S(2)}) %collective-permute-start.23) | collective-permute-done | bytes 65568 | tf_op jit(solution)/shard_map/ppermute | solution.py:17
  45.7 0.5 collective-permute-start.24
  46.2 0.2 collective-permute-start.20
  46.4 3.3 %collective-permute-done.24 = f32[64,256]{1,0:T(8,128)S(1)} collective-permute-done((f32[64,256]{1,0:T(8,128)S(1)}, f32[64,256]{1,0:T(8,128)S(1)}, u32[]{:S(2)}, u32[]{:S(2)}) %collective-permute-start.24) | collective-permute-done | bytes 65568 | tf_op jit(solution)/shard_map/ppermute | solution.py:17
  49.7 1.4 %collective-permute-start.25 = (f32[64,256]{1,0:T(8,128)S(1)}, f32[64,256]{1,0:T(8,128)S(1)}, u32[]{:S(2)}, u32[]{:S(2)}) collective-permute-start(f32[64,256]{1,0:T(8,128)S(1)} %add.50), channel_id=1, source_target_pairs={{0,9},{1,8},{2,11},{3,10},{4,13},{5,12},{6,15},{7,14},{8,1},{9,0},... | collective-permute-start | bytes 196616 | tf_op jit(solution)/shard_map/ppermute | solution.py:17
  51.2 0.3 collective-permute-start.28
  51.6 0.7 %convolution_subtract_fusion.x_ref = f32[128,1024]{1,0:T(8,128)S(1)} fusion(f32[128,1024]{1,0:T(8,128)S(1)} %convolution_subtract_fusion.1, f32[1024,256]{1,0:T(8,128)S(1)} %get-tuple-element.76, f32[64,256]{1,0:T(8,128)S(1)} %collective-permute-done.20, f32[64,256]{1,0:T(8,128)S(1)} %fusion.41, pred[]{:T(512)S(6)} %eq.18), kind=kOutput, calls=%fused_computation | convolution fusion | flops 201555968 | bytes 2228225 | tf_op jit(solution)/shard_map/ka,na->kn/dot_general | solution.py:268
  52.2 1.6 %collective-permute-done.25 = f32[64,256]{1,0:T(8,128)S(1)} collective-permute-done((f32[64,256]{1,0:T(8,128)S(1)}, f32[64,256]{1,0:T(8,128)S(1)}, u32[]{:S(2)}, u32[]{:S(2)}) %collective-permute-start.25) | collective-permute-done | bytes 65568 | tf_op jit(solution)/shard_map/ppermute | solution.py:17
  53.9 2.4 %collective-permute-start.26 = (f32[64,256]{1,0:T(8,128)S(1)}, f32[64,256]{1,0:T(8,128)S(1)}, u32[]{:S(2)}, u32[]{:S(2)}) collective-permute-start(f32[64,256]{1,0:T(8,128)S(1)} %add.51), channel_id=1, source_target_pairs={{0,17},{1,16},{2,19},{3,18},{4,21},{5,20},{6,23},{7,22},{8,25},{9,... | collective-permute-start | bytes 196616 | tf_op jit(solution)/shard_map/ppermute | solution.py:17
  56.4 2.6 %collective-permute-done.26 = f32[64,256]{1,0:T(8,128)S(1)} collective-permute-done((f32[64,256]{1,0:T(8,128)S(1)}, f32[64,256]{1,0:T(8,128)S(1)}, u32[]{:S(2)}, u32[]{:S(2)}) %collective-permute-start.26) | collective-permute-done | bytes 65568 | tf_op jit(solution)/shard_map/ppermute | solution.py:17
  58.9 0.4 fusion.54
  59.3 1.6 %collective-permute-start.29 = (f32[64,256]{1,0:T(8,128)S(1)}, f32[64,256]{1,0:T(8,128)S(1)}, u32[]{:S(2)}, u32[]{:S(2)}) collective-permute-start(f32[64,256]{1,0:T(8,128)S(1)} %fusion.54), channel_id=1, source_target_pairs={{0,1},{1,0},{2,3},{3,2},{4,5},{5,4},{6,7},{7,6},{8,9},{9,8},{10,11... | collective-permute-start | bytes 196616 | tf_op jit(solution)/shard_map/ppermute | solution.py:17
  60.9 0.9 %collective-permute-done.29 = f32[64,256]{1,0:T(8,128)S(1)} collective-permute-done((f32[64,256]{1,0:T(8,128)S(1)}, f32[64,256]{1,0:T(8,128)S(1)}, u32[]{:S(2)}, u32[]{:S(2)}) %collective-permute-start.29) | collective-permute-done | bytes 65568 | tf_op jit(solution)/shard_map/ppermute | solution.py:17
  61.8 1.4 %finish.1 = f32[1024,128]{1,0:T(8,128)} custom-call(f32[128,1024]{1,0:T(8,128)S(1)} %convolution_subtract_fusion.x_ref, f32[1024,256]{1,0:T(8,128)S(1)} %get-tuple-element.77.w_ref, f32[128,256]{1,0:T(8,128)S(1)} %maximum_select_fusion.19.t_ref), custom_call_target="tpu_custom_call" | custom-call | flops 201326592 | bytes 2097152 | tf_op jit(solution)/shard_map/finish/pallas_call | solution.py:145
  (43 shorter events, 0.6 us)
Async XLA Ops:
  3.7 1.5 %collective-permute-start = (f32[128,256]{1,0:T(8,128)S(1)}, f32[128,256]{1,0:T(8,128)S(1)}, u32[]{:S(2)}, u32[]{:S(2)}) collective-permute-start(f32[128,256]{1,0:T(8,128)S(1)} %get-tuple-element.48), channel_id=1, source_target_pairs={{0,1},{1,0},{2,3},{3,2},{4,5},{5,4},{6,7},{7,6},{8,9},{9,8},{10,11... | collective-permute-start | bytes 393224 | tf_op jit(solution)/shard_map/ppermute | solution.py:17
  6.7 3.1 %collective-permute-start.1 = (f32[64,256]{1,0:T(8,128)S(1)}, f32[64,256]{1,0:T(8,128)S(1)}, u32[]{:S(2)}, u32[]{:S(2)}) collective-permute-start(f32[64,256]{1,0:T(8,128)S(1)} %slice_select_fusion.3), channel_id=1, source_target_pairs={{0,1},{1,0},{2,3},{3,2},{4,5},{5,4},{6,7},{7,6},{8,9},{9,8},{10,11... | collective-permute-start | bytes 196616 | tf_op jit(solution)/shard_map/ppermute | solution.py:17
  7.1 11.6 %collective-permute-start.9 = (f32[1,64,512]{2,1,0:T(8,128)S(1)}, f32[1,64,512]{2,1,0:T(8,128)S(1)}, u32[]{:S(2)}, u32[]{:S(2)}) collective-permute-start(f32[1,64,512]{2,1,0:T(8,128)S(1)} %bitcast.44), channel_id=1, source_target_pairs={{0,2},{1,3},{2,0},{3,1},{4,6},{5,7},{6,4},{7,5},{8,10},{9,11},{10,... | collective-permute-start | bytes 393224 | tf_op jit(solution)/shard_map/ppermute | solution.py:17
  9.8 5.1 %collective-permute-start.2 = (f32[64,256]{1,0:T(8,128)S(1)}, f32[64,256]{1,0:T(8,128)S(1)}, u32[]{:S(2)}, u32[]{:S(2)}) collective-permute-start(f32[64,256]{1,0:T(8,128)S(1)} %select_add_fusion), channel_id=1, source_target_pairs={{0,3},{1,2},{2,1},{3,0},{4,7},{5,6},{6,5},{7,4},{8,11},{9,10},{10,... | collective-permute-start | bytes 196616 | tf_op jit(solution)/shard_map/ppermute | solution.py:17
  11.1 2.1 %collective-permute-start.3 = (f32[1,128,512]{2,1,0:T(8,128)S(1)}, f32[1,128,512]{2,1,0:T(8,128)S(1)}, u32[]{:S(2)}, u32[]{:S(2)}) collective-permute-start(f32[1,128,512]{2,1,0:T(8,128)S(1)} %bitcast.42), channel_id=1, source_target_pairs={{0,1},{1,0},{2,3},{3,2},{4,5},{5,4},{6,7},{7,6},{8,9},{9,8},{10,11... | collective-permute-start | bytes 786440 | tf_op jit(solution)/shard_map/ppermute | solution.py:17
  12.5 2.9 %collective-permute-start.6 = (f32[256,256]{1,0:T(8,128)S(1)}, f32[256,256]{1,0:T(8,128)S(1)}, u32[]{:S(2)}, u32[]{:S(2)}) collective-permute-start(f32[256,256]{1,0:T(8,128)S(1)} %fusion.89), channel_id=1, source_target_pairs={{0,1},{1,0},{2,3},{3,2},{4,5},{5,4},{6,7},{7,6},{8,9},{9,8},{10,11... | collective-permute-start | bytes 786440 | tf_op jit(solution)/shard_map/ppermute | solution.py:17
  12.7 2.7 %collective-permute-start.5 = (f32[64,256]{1,0:T(8,128)S(1)}, f32[64,256]{1,0:T(8,128)S(1)}, u32[]{:S(2)}, u32[]{:S(2)}) collective-permute-start(f32[64,256]{1,0:T(8,128)S(1)} %slice_select_fusion.2), channel_id=1, source_target_pairs={{0,1},{1,0},{2,3},{3,2},{4,5},{5,4},{6,7},{7,6},{8,9},{9,8},{10,11... | collective-permute-start | bytes 196616 | tf_op jit(solution)/shard_map/ppermute | solution.py:17
  15.2 3.7 %collective-permute-start.4 = (f32[64,256]{1,0:T(8,128)S(1)}, f32[64,256]{1,0:T(8,128)S(1)}, u32[]{:S(2)}, u32[]{:S(2)}) collective-permute-start(f32[64,256]{1,0:T(8,128)S(1)} %fusion.15), channel_id=1, source_target_pairs={{0,1},{1,0},{2,3},{3,2},{4,5},{5,4},{6,7},{7,6},{8,9},{9,8},{10,11... | collective-permute-start | bytes 196616 | tf_op jit(solution)/shard_map/ppermute | solution.py:17
  15.7 4.3 %collective-permute-start.7 = (f32[64,256]{1,0:T(8,128)S(1)}, f32[64,256]{1,0:T(8,128)S(1)}, u32[]{:S(2)}, u32[]{:S(2)}) collective-permute-start(f32[64,256]{1,0:T(8,128)S(1)} %add_subtract_fusion.2), channel_id=1, source_target_pairs={{0,3},{1,2},{2,1},{3,0},{4,7},{5,6},{6,5},{7,4},{8,11},{9,10},{10,... | collective-permute-start | bytes 196616 | tf_op jit(solution)/shard_map/ppermute | solution.py:17
  18.2 7.6 %collective-permute-start.13 = (f32[256,256]{1,0:T(8,128)S(1)}, f32[256,256]{1,0:T(8,128)S(1)}, u32[]{:S(2)}, u32[]{:S(2)}) collective-permute-start(f32[256,256]{1,0:T(8,128)S(1)} %fusion.91), channel_id=1, source_target_pairs={{0,1},{1,0},{2,3},{3,2},{4,5},{5,4},{6,7},{7,6},{8,9},{9,8},{10,11... | collective-permute-start | bytes 786440 | tf_op jit(solution)/shard_map/ppermute | solution.py:17
  18.7 6.6 %collective-permute-start.10 = (f32[2,64,512]{2,1,0:T(8,128)S(1)}, f32[2,64,512]{2,1,0:T(8,128)S(1)}, u32[]{:S(2)}, u32[]{:S(2)}) collective-permute-start(f32[2,64,512]{2,1,0:T(8,128)S(1)} %maximum_select_fusion.6), channel_id=1, source_target_pairs={{0,1},{1,0},{2,3},{3,2},{4,5},{5,4},{6,7},{7,6},{8,9},{9,8},{10,11... | collective-permute-start | bytes 786440 | tf_op jit(solution)/shard_map/ppermute | solution.py:17
  20.0 5.4 %collective-permute-start.8 = (f32[64,256]{1,0:T(8,128)S(1)}, f32[64,256]{1,0:T(8,128)S(1)}, u32[]{:S(2)}, u32[]{:S(2)}) collective-permute-start(f32[64,256]{1,0:T(8,128)S(1)} %add.42._), channel_id=1, source_target_pairs={{0,5},{1,4},{2,7},{3,6},{4,1},{5,0},{6,3},{7,2},{8,13},{9,12},{10,... | collective-permute-start | bytes 196616 | tf_op jit(solution)/shard_map/ppermute | solution.py:17
  23.5 2.3 %collective-permute-start.12 = (f32[64,256]{1,0:T(8,128)S(1)}, f32[64,256]{1,0:T(8,128)S(1)}, u32[]{:S(2)}, u32[]{:S(2)}) collective-permute-start(f32[64,256]{1,0:T(8,128)S(1)} %slice_select_fusion.1), channel_id=1, source_target_pairs={{0,1},{1,0},{2,3},{3,2},{4,5},{5,4},{6,7},{7,6},{8,9},{9,8},{10,11... | collective-permute-start | bytes 196616 | tf_op jit(solution)/shard_map/ppermute | solution.py:17
  23.8 5.0 %collective-permute-start.17 = (f32[1,48,512]{2,1,0:T(8,128)S(1)}, f32[1,48,512]{2,1,0:T(8,128)S(1)}, u32[]{:S(2)}, u32[]{:S(2)}) collective-permute-start(f32[1,48,512]{2,1,0:T(8,128)S(1)} %bitcast.46), channel_id=1, source_target_pairs={{0,2},{1,3},{2,0},{3,1},{4,6},{5,7},{6,4},{7,5},{8,10},{9,11},{10,... | collective-permute-start | bytes 294920 | tf_op jit(solution)/shard_map/ppermute | solution.py:17
  25.8 6.4 %collective-permute-start.11 = (f32[64,256]{1,0:T(8,128)S(1)}, f32[64,256]{1,0:T(8,128)S(1)}, u32[]{:S(2)}, u32[]{:S(2)}) collective-permute-start(f32[64,256]{1,0:T(8,128)S(1)} %fusion.28), channel_id=1, source_target_pairs={{0,1},{1,0},{2,3},{3,2},{4,5},{5,4},{6,7},{7,6},{8,9},{9,8},{10,11... | collective-permute-start | bytes 196616 | tf_op jit(solution)/shard_map/ppermute | solution.py:17
  26.2 3.8 %collective-permute-start.14 = (f32[64,256]{1,0:T(8,128)S(1)}, f32[64,256]{1,0:T(8,128)S(1)}, u32[]{:S(2)}, u32[]{:S(2)}) collective-permute-start(f32[64,256]{1,0:T(8,128)S(1)} %add_subtract_fusion.1), channel_id=1, source_target_pairs={{0,3},{1,2},{2,1},{3,0},{4,7},{5,6},{6,5},{7,4},{8,11},{9,10},{10,... | collective-permute-start | bytes 196616 | tf_op jit(solution)/shard_map/ppermute | solution.py:17
  28.8 7.1 %collective-permute-start.18 = (f32[2,48,512]{2,1,0:T(8,128)S(1)}, f32[2,48,512]{2,1,0:T(8,128)S(1)}, u32[]{:S(2)}, u32[]{:S(2)}) collective-permute-start(f32[2,48,512]{2,1,0:T(8,128)S(1)} %maximum_select_fusion.8), channel_id=1, source_target_pairs={{0,4},{1,5},{2,6},{3,7},{4,0},{5,1},{6,2},{7,3},{8,12},{9,13},{10,... | collective-permute-start | bytes 589832 | tf_op jit(solution)/shard_map/ppermute | solution.py:17
  30.0 5.0 %collective-permute-start.15 = (f32[64,256]{1,0:T(8,128)S(1)}, f32[64,256]{1,0:T(8,128)S(1)}, u32[]{:S(2)}, u32[]{:S(2)}) collective-permute-start(f32[64,256]{1,0:T(8,128)S(1)} %add.45), channel_id=1, source_target_pairs={{0,5},{1,4},{2,7},{3,6},{4,1},{5,0},{6,3},{7,2},{8,13},{9,12},{10,... | collective-permute-start | bytes 196616 | tf_op jit(solution)/shard_map/ppermute | solution.py:17
  31.6 9.7 %collective-permute-start.22 = (f32[256,256]{1,0:T(8,128)S(1)}, f32[256,256]{1,0:T(8,128)S(1)}, u32[]{:S(2)}, u32[]{:S(2)}) collective-permute-start(f32[256,256]{1,0:T(8,128)S(1)} %fusion.93), channel_id=1, source_target_pairs={{0,1},{1,0},{2,3},{3,2},{4,5},{5,4},{6,7},{7,6},{8,9},{9,8},{10,11... | collective-permute-start | bytes 786440 | tf_op jit(solution)/shard_map/ppermute | solution.py:17
  35.9 2.8 %collective-permute-start.19 = (f32[4,32,512]{2,1,0:T(8,128)S(1)}, f32[4,32,512]{2,1,0:T(8,128)S(1)}, u32[]{:S(2)}, u32[]{:S(2)}) collective-permute-start(f32[4,32,512]{2,1,0:T(8,128)S(1)} %slice.54), channel_id=1, source_target_pairs={{0,1},{1,0},{2,3},{3,2},{4,5},{5,4},{6,7},{7,6},{8,9},{9,8},{10,11... | collective-permute-start | bytes 786440 | tf_op jit(solution)/shard_map/ppermute | solution.py:17
  37.0 4.3 %collective-permute-start.21 = (f32[64,256]{1,0:T(8,128)S(1)}, f32[64,256]{1,0:T(8,128)S(1)}, u32[]{:S(2)}, u32[]{:S(2)}) collective-permute-start(f32[64,256]{1,0:T(8,128)S(1)} %slice_select_fusion), channel_id=1, source_target_pairs={{0,1},{1,0},{2,3},{3,2},{4,5},{5,4},{6,7},{7,6},{8,9},{9,8},{10,11... | collective-permute-start | bytes 196616 | tf_op jit(solution)/shard_map/ppermute | solution.py:17
  37.1 3.9 %collective-permute-start.16 = (f32[64,256]{1,0:T(8,128)S(1)}, f32[64,256]{1,0:T(8,128)S(1)}, u32[]{:S(2)}, u32[]{:S(2)}) collective-permute-start(f32[64,256]{1,0:T(8,128)S(1)} %add.46), channel_id=1, source_target_pairs={{0,9},{1,8},{2,11},{3,10},{4,13},{5,12},{6,15},{7,14},{8,1},{9,0},... | collective-permute-start | bytes 196616 | tf_op jit(solution)/shard_map/ppermute | solution.py:17
  41.6 4.0 %collective-permute-start.23 = (f32[64,256]{1,0:T(8,128)S(1)}, f32[64,256]{1,0:T(8,128)S(1)}, u32[]{:S(2)}, u32[]{:S(2)}) collective-permute-start(f32[64,256]{1,0:T(8,128)S(1)} %add_subtract_fusion), channel_id=1, source_target_pairs={{0,3},{1,2},{2,1},{3,0},{4,7},{5,6},{6,5},{7,4},{8,11},{9,10},{10,... | collective-permute-start | bytes 196616 | tf_op jit(solution)/shard_map/ppermute | solution.py:17
  42.8 8.3 %collective-permute-start.27 = (f32[4,16,512]{2,1,0:T(8,128)S(1)}, f32[4,16,512]{2,1,0:T(8,128)S(1)}, u32[]{:S(2)}, u32[]{:S(2)}) collective-permute-start(f32[4,16,512]{2,1,0:T(8,128)S(1)} %slice.57), channel_id=1, source_target_pairs={{0,8},{1,9},{2,10},{3,11},{4,12},{5,13},{6,14},{7,15},{8,0},{9,1},... | collective-permute-start | bytes 393224 | tf_op jit(solution)/shard_map/ppermute | solution.py:17
  45.7 4.1 %collective-permute-start.24 = (f32[64,256]{1,0:T(8,128)S(1)}, f32[64,256]{1,0:T(8,128)S(1)}, u32[]{:S(2)}, u32[]{:S(2)}) collective-permute-start(f32[64,256]{1,0:T(8,128)S(1)} %add.49), channel_id=1, source_target_pairs={{0,5},{1,4},{2,7},{3,6},{4,1},{5,0},{6,3},{7,2},{8,13},{9,12},{10,... | collective-permute-start | bytes 196616 | tf_op jit(solution)/shard_map/ppermute | solution.py:17
  46.2 5.4 %collective-permute-start.20 = (f32[64,256]{1,0:T(8,128)S(1)}, f32[64,256]{1,0:T(8,128)S(1)}, u32[]{:S(2)}, u32[]{:S(2)}) collective-permute-start(f32[64,256]{1,0:T(8,128)S(1)} %fusion.41), channel_id=1, source_target_pairs={{0,1},{1,0},{2,3},{3,2},{4,5},{5,4},{6,7},{7,6},{8,9},{9,8},{10,11... | collective-permute-start | bytes 196616 | tf_op jit(solution)/shard_map/ppermute | solution.py:17
  49.7 4.1 %collective-permute-start.25 = (f32[64,256]{1,0:T(8,128)S(1)}, f32[64,256]{1,0:T(8,128)S(1)}, u32[]{:S(2)}, u32[]{:S(2)}) collective-permute-start(f32[64,256]{1,0:T(8,128)S(1)} %add.50), channel_id=1, source_target_pairs={{0,9},{1,8},{2,11},{3,10},{4,13},{5,12},{6,15},{7,14},{8,1},{9,0},... | collective-permute-start | bytes 196616 | tf_op jit(solution)/shard_map/ppermute | solution.py:17
  51.2 5.1 %collective-permute-start.28 = (f32[8,16,512]{2,1,0:T(8,128)S(1)}, f32[8,16,512]{2,1,0:T(8,128)S(1)}, u32[]{:S(2)}, u32[]{:S(2)}) collective-permute-start(f32[8,16,512]{2,1,0:T(8,128)S(1)} %maximum_select_fusion.7), channel_id=1, source_target_pairs={{0,1},{1,0},{2,3},{3,2},{4,5},{5,4},{6,7},{7,6},{8,9},{9,8},{10,11... | collective-permute-start | bytes 786440 | tf_op jit(solution)/shard_map/ppermute | solution.py:17
  53.9 5.0 %collective-permute-start.26 = (f32[64,256]{1,0:T(8,128)S(1)}, f32[64,256]{1,0:T(8,128)S(1)}, u32[]{:S(2)}, u32[]{:S(2)}) collective-permute-start(f32[64,256]{1,0:T(8,128)S(1)} %add.51), channel_id=1, source_target_pairs={{0,17},{1,16},{2,19},{3,18},{4,21},{5,20},{6,23},{7,22},{8,25},{9,... | collective-permute-start | bytes 196616 | tf_op jit(solution)/shard_map/ppermute | solution.py:17
  59.3 2.5 %collective-permute-start.29 = (f32[64,256]{1,0:T(8,128)S(1)}, f32[64,256]{1,0:T(8,128)S(1)}, u32[]{:S(2)}, u32[]{:S(2)}) collective-permute-start(f32[64,256]{1,0:T(8,128)S(1)} %fusion.54), channel_id=1, source_target_pairs={{0,1},{1,0},{2,3},{3,2},{4,5},{5,4},{6,7},{7,6},{8,9},{9,8},{10,11... | collective-permute-start | bytes 196616 | tf_op jit(solution)/shard_map/ppermute | solution.py:17
